TPU v7x, 32 devices: a whole 2x2x4 slice. The times are simulated.
32 devices in a mesh: lon: 8 (over z, core), lat: 4 (over y, x).
Axes of the slice: x: 2, y: 2, z: 4, core: 2. Of those that a mesh axis runs over, the one named last changes fastest.
Arguments:
- state: float32 [150, 128, 1024], P(None, 'lat', 'lon'), may hold values from -6 to 6
- diffusivity: float32 [150, 128, 1024], P(None, 'lat', 'lon'), may hold values from 0.02 to 0.24
- sea_mask: int32 [75, 128, 1024], P(None, 'lat', 'lon'), may hold values 0 or 1
- send_cols: int32 [32, 768], P(('lon', 'lat')), may hold values from 0 to 4096, as said below
- obs_slots: int32 [4, 65536], P(None, ('lon', 'lat')), may hold values from 0 to 767, as said below
- obs_weights: float32 [4, 65536], P(None, ('lon', 'lat')), may hold values from 0.05 to 0.5
- obs_precision: float32 [150, 65536], P(None, ('lon', 'lat')), may hold values from 0.25 to 4
Outputs:
- product: float32 [150, 128, 1024], P(None, 'lat', 'lon')
- equivalents: float32 [150, 65536], P(None, ('lon', 'lat'))
Inputs may be any that keep to these rules, and one draw needn't show every extreme that they name: `send_cols`: for each device s and owner o the first n entries of the owner's 24 entries are local column indices below 4096, the rest are 4096; n is at least 1 and at most 24; every device has some owner with n = 24, and some owner receives 24 columns from every device. `obs_slots`: every slot named refers to a live entry: for owner o, slot s * 24 + p with p below the number of live entries of device s for owner o.
All inputs are finite; a program needn't handle non-finite values. No bound on the sum of `sea_mask` on one device may be relied on, other than what follows from the above.
Results may differ from a plain program's by a relative error of at most 0.00002.
Values sent between devices are 32-bit elements; how exact they have to be, the bound alone decides.
No kernel may reach another device: no remote copies, remote signals or barrier semaphores. Data moves between devices by JAX's collectives and lax.ppermute only.
A program may use at most 128 MiB of HBM per device.

v0:
```python
import functools

import jax
import jax.numpy as jnp
from jax import lax
from jax.experimental import pallas as pl
from jax.experimental.pallas import tpu as pltpu
from jax.sharding import PartitionSpec as P

CAP = 24
LANES = 128
GROUPS = 5
ROWS = 32
OBS_BLOCK = 256
F32, BF16 = jnp.float32, jnp.bfloat16
MIB = 1 << 20


def up(n, k):
    return -(-n // k) * k


def roll(x, k):
    k %= LANES
    return x if k == 0 else pltpu.roll(x, k, axis=1)


def lane_of(x):
    return lax.broadcasted_iota(jnp.int32, x.shape, 1)


def tall(x, rows):
    return jnp.concatenate([x, jnp.zeros((rows - x.shape[0], x.shape[1]), x.dtype)], axis=0)


def halves(x):
    hi = x.astype(BF16)
    return hi, (x - hi.astype(F32)).astype(BF16)


def dot(a, b):
    return lax.dot_general(a, b, (((1,), (0,)), ((), ())), preferred_element_type=F32)


def dot_nt(a, b):
    return lax.dot_general(a, b, (((1,), (1,)), ((), ())), preferred_element_type=F32)


def stacked(x):
    return jnp.concatenate(halves(x), axis=0)


def folded(x):
    n = x.shape[0] // 2
    return x[:n] + x[n:]


def row_edges(c):
    east = jnp.where(lane_of(c) == LANES - 1, 0.0, jnp.minimum(c, roll(c, -1)))
    return east, roll(east, 1)


def pack_edges(cp):
    lane = lane_of(cp)
    kind = lane & 3
    inner = jnp.where(kind == 1, roll(cp, 1), roll(cp, -1))
    inner = jnp.where((kind == 1) | (kind == 2), jnp.minimum(cp, inner), 0.0)
    south = jnp.where(lane >= LANES - 4, 0.0, jnp.minimum(cp, roll(cp, -4)))
    return kind, inner, south, roll(south, 4)


def rim_rows(v0, v1, v30, v31, c0, c1, c30, c31):
    out = []
    for v, w, c, d in ((v0, v1, c0, c1), (v31, v30, c31, c30)):
        east, west = row_edges(c)
        out.append(v + east * (roll(v, -1) - v) + west * (roll(v, 1) - v) + jnp.minimum(c, d) * (w - v))
    return out


def rim_pack(vp, cp):
    kind, inner, south, north = pack_edges(cp)
    beside = jnp.where(kind == 1, roll(vp, 1), roll(vp, -1))
    return vp + inner * (beside - vp) + south * (roll(vp, -4) - vp) + north * (roll(vp, 4) - vp)


def pack_messages(vp, cp, pp):
    kind = lane_of(vp) & 3
    east = jnp.where(kind == 0, roll(vp, -1), jnp.where(kind == 1, cp, roll(pp, 1)))
    west = jnp.where(kind == 0, roll(vp, -2), jnp.where(kind == 1, roll(cp, -1), pp))
    return east, west


def ghost_pack(from_w, from_e):
    one = (lane_of(from_w) & 3) == 1
    v = jnp.where(one, roll(from_e, 1), roll(from_w, 2))
    c = jnp.where(one, from_e, roll(from_w, 1))
    p = jnp.where(one, roll(from_e, -1), from_w)
    return v, c, p


CORNER_LANES = (1, 2, LANES - 3, LANES - 2)


def corner_messages(vp, cp):
    vt, ct = tall(vp, 256).T, tall(cp, 256).T
    row = lax.broadcasted_iota(jnp.int32, (8, 256), 0)
    return [jnp.where(row == 0, vt[k : k + 1], jnp.where(row == 1, ct[k : k + 1], 0.0)) for k in CORNER_LANES]


def corner_pack(messages, which, rows):
    row = lax.broadcasted_iota(jnp.int32, (LANES, 256), 0)
    t = jnp.zeros((LANES, 256), F32)
    for k, m in zip(CORNER_LANES, messages):
        t = jnp.where(row == k, m[which : which + 1], t)
    return t.T[:rows]


def rim_correction(own, coef, ghosts):
    v0, v31, p0, p31, vp, pp = own
    c0, c1, c30, c31, cp = coef
    (gvn, gcn, gpn), (gvs, gcs, gps), (gv, gc, gp), (kv, kc) = ghosts
    lane = lane_of(v0)
    ends = (lane == 0) | (lane == LANES - 1)
    kind, inner, south, north = pack_edges(cp)
    mid = (kind == 1) | (kind == 2)
    mg = jnp.where(mid, jnp.minimum(cp, gc), 0.0)
    f = mg * (gv - vp)
    mn, ms = jnp.minimum(c0, gcn), jnp.minimum(c31, gcs)
    fn, fs = mn * (gvn - v0), ms * (gvs - v31)
    ghost = gp - f + jnp.where(mid, jnp.minimum(gc, kc), 0.0) * (kv - gv)
    ghost_n = gpn - fn + jnp.where(ends, jnp.minimum(gcn, roll(kc, -2)), 0.0) * (roll(kv, -2) - gvn)
    ghost_s = gps - fs + jnp.where(ends, jnp.minimum(gcs, roll(kc, 2)), 0.0) * (roll(kv, 2) - gvs)
    whole = pp + f + jnp.where((lane == 1) | (lane == 2), roll(fn, 2), 0.0)
    whole = whole + jnp.where((lane == LANES - 3) | (lane == LANES - 2), roll(fs, -2), 0.0)
    whole_n = p0 + fn + jnp.where(ends, roll(f, -2), 0.0)
    whole_s = p31 + fs + jnp.where(ends, roll(f, 2), 0.0)
    qf = inner * f
    rp = f - qf + south * (roll(f, -4) - f) + north * (roll(f, 4) - f) + mg * (ghost - whole)
    rp = jnp.where(mid, rp, jnp.where(kind == 0, roll(qf, -1), roll(qf, 1)))
    rows = []
    for c, d, m, g, w, x in ((c0, c1, mn, ghost_n, whole_n, fn), (c31, c30, ms, ghost_s, whole_s, fs)):
        east, west = row_edges(c)
        across = jnp.minimum(c, d)
        rows.append(x + east * (roll(x, -1) - x) + west * (roll(x, 1) - x) - across * x + m * (g - w))
        rows.append(across * x)
    return rows[0], rows[1], rows[3], rows[2], rp


def two_sweeps(load_v, load_c, store):
    x, c = load_v(0), load_c(0)
    last = lane_of(x) == LANES - 1
    zero = jnp.zeros_like(x)
    f_up, g_up = zero, zero
    before = None
    for i in range(ROWS):
        if i < ROWS - 1:
            xn, cn = load_v(i + 1), load_c(i + 1)
            across = jnp.minimum(c, cn)
            f = across * (xn - x)
        else:
            f = zero
        east = jnp.where(last, 0.0, jnp.minimum(c, roll(c, -1)))
        e = east * (roll(x, -1) - x)
        y = x + (e - roll(e, 1)) + (f - f_up)
        if before is not None:
            yb, hb, across_b = before
            g = across_b * (y - yb)
            store(i - 1, yb + hb + (g - g_up))
            g_up = g
        h = east * (roll(y, -1) - y)
        before = (y, h - roll(h, 1), across)
        f_up = f
        if i < ROWS - 1:
            x, c = xn, cn
    yb, hb, _ = before
    store(ROWS - 1, yb + hb - g_up)


def chosen(cells, ids):
    return jnp.where(ids == cells, 1.0, 0.0).astype(BF16)


def rim_ids(n):
    line = lax.broadcasted_iota(jnp.int32, (LANES, n), 0)
    rows = [line + i * LANES for i in (0, 1, ROWS - 2, ROWS - 1)]
    k = line & 3
    pack = (line >> 2) * LANES + jnp.where(k < 2, LANES - 2 + k, k - 2)
    return jnp.concatenate(rows + [pack], axis=0)


def pack_payload(x, out_ref, owners):
    lane = lax.broadcasted_iota(jnp.int32, (ROWS, LANES), 1)
    for o in range(owners):
        a, b = divmod(o, GROUPS)
        block = jnp.zeros((ROWS, LANES), F32)
        for g in range(GROUPS):
            piece = roll(x[ROWS * g : ROWS * (g + 1), LANES * a : LANES * (a + 1)], CAP * (g - b))
            block = jnp.where((lane >= CAP * g) & (lane < CAP * (g + 1)), piece, block)
        out_ref[ROWS * o : ROWS * (o + 1), :] = block


def unpack_payload(in_ref, owners, slots):
    lane = lax.broadcasted_iota(jnp.int32, (ROWS, LANES), 1)
    columns = []
    for a in range(slots // LANES):
        pieces = []
        for g in range(GROUPS):
            piece = jnp.zeros((ROWS, LANES), F32)
            for b in range(GROUPS):
                o = GROUPS * a + b
                if o < owners:
                    block = roll(in_ref[ROWS * o : ROWS * (o + 1), :], CAP * (b - g))
                    piece = jnp.where((lane >= CAP * b) & (lane < CAP * (b + 1)), block, piece)
            pieces.append(piece)
        columns.append(jnp.concatenate(pieces, axis=0))
    return jnp.concatenate(columns, axis=1)


def call(kernel, outs, *args, in_specs=None, scratch=(), vmem=48, flops=0, nbytes=0, **kw):
    any_spec = pl.BlockSpec(memory_space=pltpu.VMEM)
    return pl.pallas_call(
        kernel,
        out_shape=[jax.ShapeDtypeStruct(s, d) for s, d in outs],
        in_specs=in_specs or [any_spec] * len(args),
        scratch_shapes=list(scratch),
        compiler_params=pltpu.CompilerParams(vmem_limit_bytes=vmem * MIB),
        cost_estimate=pl.CostEstimate(flops=flops, bytes_accessed=nbytes, transcendentals=0),
        **kw,
    )(*args)


HBM = pl.BlockSpec(memory_space=pl.ANY)
VMEM = pl.BlockSpec(memory_space=pltpu.VMEM)


def load_fields(vals, refs, scratch, sems):
    state, diff, mask = refs
    sv, sd, sm = scratch
    n = vals * ROWS
    copies = [
        pltpu.make_async_copy(state, sv.at[pl.ds(0, n)], sems.at[0]),
        pltpu.make_async_copy(diff, sd.at[pl.ds(0, n)], sems.at[1]),
        pltpu.make_async_copy(mask, sm.at[pl.ds(0, n // 2)], sems.at[2]),
        pltpu.make_async_copy(mask, sm.at[pl.ds(n // 2, n // 2)], sems.at[3]),
    ]
    for c in copies:
        c.start()
    rest = sv.shape[0] - n
    sv[pl.ds(n, rest), :] = jnp.zeros((rest, LANES), F32)
    sd[pl.ds(n, rest), :] = jnp.zeros((rest, LANES), F32)
    sm[pl.ds(n, rest), :] = jnp.zeros((rest, LANES), jnp.int32)
    for c in copies:
        c.wait()


def grid_row(ref, i, vp):
    return ref[pl.ds(i, vp, stride=ROWS), :]


def prepare_kernel(vals, vp, mp, state, diff, mask, m_n, m_s, m_e, m_w, k_ne, k_nw, k_se, k_sw, rv, rc, pk, sv, sd, sm, sems):
    load_fields(vals, (state, diff, mask), (sv, sd, sm), sems)

    def coef(i):
        return grid_row(sd, i, vp) * grid_row(sm, i, vp).astype(F32)

    lane = lax.broadcasted_iota(jnp.int32, (vp, LANES), 1)
    pv = jnp.zeros((vp, LANES), F32)
    pc = jnp.zeros((vp, LANES), F32)
    for i in range(ROWS):
        here = (lane >> 2) == i
        pv = jnp.where(here, roll(grid_row(sv, i, vp), 4 * i + 2), pv)
        pc = jnp.where(here, roll(coef(i), 4 * i + 2), pc)
    v0, v1, v30, v31 = (grid_row(sv, i, vp) for i in (0, 1, ROWS - 2, ROWS - 1))
    c0, c1, c30, c31 = (coef(i) for i in (0, 1, ROWS - 2, ROWS - 1))
    p0, p31 = rim_rows(v0, v1, v30, v31, c0, c1, c30, c31)
    pp = rim_pack(pv, pc)
    east, west = pack_messages(pv, pc, pp)
    for ref, parts in ((m_n, (v0, c0, p0)), (m_s, (v31, c31, p31)), (m_e, (east,)), (m_w, (west,))):
        for k, x in enumerate(parts):
            ref[mp * k : mp * (k + 1), :] = x[:mp]
    for ref, m in zip((k_ne, k_nw, k_se, k_sw), corner_messages(pv, pc)):
        ref[...] = m
    for ref, parts in ((rv, (v0, v31, p0, p31)), (rc, (c0, c1, c30, c31)), (pk, (pv, pc, pp))):
        for k, x in enumerate(parts):
            ref[vp * k : vp * (k + 1), :] = x


def inner_kernel(vals, vp, state, diff, mask, cells, out, sv, sd, sm, smooth, hot, sems):
    load_fields(vals, (state, diff, mask), (sv, sd, sm), sems)

    def step(t, carry):
        def load(ref, i):
            return ref[pl.ds(t * (16 * ROWS) + i, 16, stride=ROWS), :]

        def store(i, x):
            smooth[pl.ds(t * 16, 16), LANES * i : LANES * (i + 1)] = x

        two_sweeps(lambda i: load(sv, i), lambda i: load(sd, i) * load(sm, i).astype(F32), store)
        return carry

    lax.fori_loop(0, vp // 16, step, 0)
    chunk = hot.shape[1]
    wide = 4 * LANES
    for base in range(0, cells.shape[1], chunk):
        total = jnp.zeros((2 * vp, chunk), F32)
        for k in range(0, ROWS * LANES, wide):
            ids = lax.broadcasted_iota(jnp.int32, (wide, chunk), 0) + k
            hot[k : k + wide, :] = chosen(cells[:, base : base + chunk], ids)
        for k in range(0, ROWS * LANES, wide):
            total = total + dot(stacked(smooth[:, k : k + wide]), hot[k : k + wide, :])
        out[:, base : base + chunk] = folded(total)


def weights_kernel(slots, weights, hi, lo):
    s = slots[...]
    place = s + 8 * jnp.floor((s.astype(F32) + 0.5) * (1.0 / (CAP * GROUPS))).astype(jnp.int32)
    row = lax.broadcasted_iota(jnp.int32, hi.shape, 0)
    total = jnp.zeros(hi.shape, F32)
    for k in range(slots.shape[0]):
        total = total + jnp.where(row == place[k : k + 1], weights[k : k + 1, :], 0.0)
    hi[...], lo[...] = halves(total)


def read_ghosts(vp, mp, f_n, f_s, f_e, f_w, corners):
    def part(ref, k):
        return tall(ref[mp * k : mp * (k + 1), :], vp)

    gn = [part(f_n, k) for k in range(3)]
    gs = [part(f_s, k) for k in range(3)]
    gp = ghost_pack(part(f_w, 0), part(f_e, 0))
    k = [corner_pack([m[...] for m in corners], i, vp) for i in (0, 1)]
    return gn, gs, gp, k


def parts_of(ref, vp):
    return [ref[vp * k : vp * (k + 1), :] for k in range(ref.shape[0] // vp)]


def send_kernel(owners, vp, mp, f_n, f_s, f_e, f_w, k_ne, k_nw, k_se, k_sw, rv, rc, pk, inner, cells, out):
    ghosts = read_ghosts(vp, mp, f_n, f_s, f_e, f_w, (k_ne, k_nw, k_se, k_sw))
    v0, v31, p0, p31 = parts_of(rv, vp)
    pv, pc, pp = parts_of(pk, vp)
    fix = rim_correction((v0, v31, p0, p31, pv, pp), parts_of(rc, vp) + [pc], ghosts)
    slots = cells.shape[1]
    total = folded(dot(stacked(jnp.concatenate(fix, axis=1)), chosen(cells[...], rim_ids(slots))))
    pack_payload(inner[...] + total, out, owners)


def owner_kernel(vals, vp, owners, got, w_hi, w_lo, prec, equiv, back, r2, w2, acc):
    step = pl.program_id(0)

    @pl.when(step == 0)
    def _():
        r2[...] = stacked(unpack_payload(got, owners, acc.shape[1]))
        w2[...] = jnp.zeros(w2.shape, F32)
        acc[...] = jnp.zeros(acc.shape, F32)

    hi, lo = w_hi[...], w_lo[...]
    e = folded(dot(r2[...], hi)) + dot(r2[:vp, :], lo)
    equiv[...] = e[:vals]
    w2[:vals, :] = prec[...] * e[:vals]
    w = stacked(w2[...])
    acc[...] += folded(dot_nt(w, hi)) + dot_nt(w[:vp], lo)

    @pl.when(step == pl.num_programs(0) - 1)
    def _():
        pack_payload(acc[...], back, owners)


def back_kernel(owners, vp, mp, got, cells, rc, pk, m_n, m_s, m_e, m_w, k_ne, k_nw, k_se, k_sw, inc, ra, pa):
    slots = cells.shape[1]
    x = stacked(unpack_payload(got, owners, slots))
    inc[...] = x
    rims = folded(dot_nt(x, chosen(cells[...], rim_ids(slots))))
    v0, v1, v30, v31, pv = (rims[:, LANES * k : LANES * (k + 1)] for k in range(5))
    pc = pk[vp : 2 * vp, :]
    p0, p31 = rim_rows(v0, v1, v30, v31, *parts_of(rc, vp))
    pp = rim_pack(pv, pc)
    east, west = pack_messages(pv, pc, pp)
    for ref, parts in ((m_n, (v0, p0)), (m_s, (v31, p31)), (m_e, (east,)), (m_w, (west,))):
        for k, y in enumerate(parts):
            ref[mp * k : mp * (k + 1), :] = y[:mp]
    for ref, m in zip((k_ne, k_nw, k_se, k_sw), corner_messages(pv, pc)):
        ref[...] = m
    for ref, parts in ((ra, (v0, v31, p0, p31)), (pa, (pv, pp))):
        for k, y in enumerate(parts):
            ref[vp * k : vp * (k + 1), :] = y


def adjoint_kernel(vals, vp, state, diff, mask, inc, cells, out, sv, sd, sm, adj, sems, sem):
    load_fields(vals, (state, diff, mask), (sv, sd, sm), sems)
    wide = 2 * LANES
    slots = cells.shape[1]

    def scatter(k, carry):
        ids = lax.broadcasted_iota(jnp.int32, (wide, slots), 0) + k * wide
        x = folded(dot_nt(inc[...], chosen(cells[...], ids)))
        for j in range(2):
            adj[pl.ds((2 * k + j) * vp, vp), :] = x[:, LANES * j : LANES * (j + 1)]
        return carry

    lax.fori_loop(0, ROWS // 2, scatter, 0)

    def step(t, carry):
        def rows(i):
            return pl.ds(t * (16 * ROWS) + i, 16, stride=ROWS)

        def store(i, x):
            sv[rows(i), :] = sv[rows(i), :] + x

        two_sweeps(
            lambda i: adj[pl.ds(i * vp + t * 16, 16), :],
            lambda i: sd[rows(i), :] * sm[rows(i), :].astype(F32),
            store,
        )
        return carry

    lax.fori_loop(0, vp // 16, step, 0)
    copy = pltpu.make_async_copy(sv.at[pl.ds(0, vals * ROWS)], out, sem)
    copy.start()
    copy.wait()


def final_kernel(vals, vp, mp, f_n, f_s, f_e, f_w, k_ne, k_nw, k_se, k_sw, a_n, a_s, a_e, a_w, j_ne, j_nw, j_se, j_sw, ra, rc, pk, pa, part, out, buf, rp, sem):
    n = vals * ROWS
    copy = pltpu.make_async_copy(part, buf.at[pl.ds(0, n)], sem)
    copy.start()
    (_, gcn, _), (_, gcs, _), (_, gc, _), (_, kc) = read_ghosts(vp, mp, f_n, f_s, f_e, f_w, (k_ne, k_nw, k_se, k_sw))

    def piece(ref, k):
        return tall(ref[mp * k : mp * (k + 1), :], vp)

    gv, _, gp = ghost_pack(piece(a_w, 0), piece(a_e, 0))
    kv = corner_pack([m[...] for m in (j_ne, j_nw, j_se, j_sw)], 0, vp)
    ghosts = (piece(a_n, 0), gcn, piece(a_n, 1)), (piece(a_s, 0), gcs, piece(a_s, 1)), (gv, gc, gp), (kv, kc)
    v0, v31, p0, p31 = parts_of(ra, vp)
    pv, pp = parts_of(pa, vp)
    r0, r1, r30, r31, fix = rim_correction((v0, v31, p0, p31, pv, pp), parts_of(rc, vp) + [pk[vp : 2 * vp, :]], ghosts)
    rp[...] = fix
    copy.wait()
    lane = lax.broadcasted_iota(jnp.int32, (vp, LANES), 1)
    outer = (lane < 2) | (lane >= LANES - 2)
    for i in range(ROWS):
        x = grid_row(buf, i, vp) + jnp.where(outer, roll(rp[...], -(4 * i + 2)), 0.0)
        row = {0: r0, 1: r1, ROWS - 2: r30, ROWS - 1: r31}.get(i)
        buf[pl.ds(i, vp, stride=ROWS), :] = x if row is None else x + row
    copy = pltpu.make_async_copy(buf.at[pl.ds(0, n)], out, sem)
    copy.start()
    copy.wait()


def neighbour(x, dlon, dlat):
    nlon, nlat = lax.axis_size("lon"), lax.axis_size("lat")
    pairs = [
        (a * nlat + b, (a + dlon) % nlon * nlat + b + dlat)
        for a in range(nlon)
        for b in range(nlat)
        if 0 <= b + dlat < nlat
    ]
    return lax.ppermute(x, ("lon", "lat"), pairs)


def exchange(m_n, m_s, m_e, m_w, k_ne, k_nw, k_se, k_sw):
    f_s = neighbour(m_n, 0, -1)
    f_n = neighbour(m_s, 0, 1)
    f_w = neighbour(m_e, 1, 0)
    f_e = neighbour(m_w, -1, 0)
    g_sw = neighbour(k_ne, 1, -1)
    g_se = neighbour(k_nw, -1, -1)
    g_nw = neighbour(k_se, 1, 1)
    g_ne = neighbour(k_sw, -1, 1)
    return f_n, f_s, f_e, f_w, g_ne, g_nw, g_se, g_sw


def across(x):
    return lax.all_to_all(x, ("lon", "lat"), split_axis=0, concat_axis=0, tiled=True)


def on_device(state, diffusivity, sea_mask, send_cols, obs_slots, obs_weights, obs_precision):
    vals, taps, obs = state.shape[0], obs_slots.shape[0], obs_slots.shape[1]
    owners = send_cols.shape[1] // CAP
    vp, mp = up(vals, ROWS), up(vals, 8)
    tiles = up(owners, 7 * GROUPS) // GROUPS
    slots = tiles * LANES
    cell_count = ROWS * LANES
    flat = [x.reshape(-1, LANES) for x in (state, diffusivity, sea_mask)]
    cells = jnp.pad(send_cols, ((0, 0), (0, tiles * GROUPS * CAP - owners * CAP)), constant_values=cell_count)
    cells = jnp.pad(cells.reshape(tiles, GROUPS * CAP), ((0, 0), (0, LANES - GROUPS * CAP)), constant_values=cell_count)
    cells = cells.reshape(1, slots)

    fields = [pltpu.VMEM((vp * ROWS, LANES), d) for d in (F32, F32, jnp.int32)]
    dma4 = pltpu.SemaphoreType.DMA((4,))
    line = (vp, LANES)
    corner = [((8, 256), F32)] * 4

    def messages(n):
        return [((n * mp, LANES), F32)] * 2 + [((mp, LANES), F32)] * 2 + corner

    *sent, rv, rc, pk = call(
        functools.partial(prepare_kernel, vals, vp, mp),
        messages(3) + [((4 * vp, LANES), F32)] * 2 + [((3 * vp, LANES), F32)],
        *flat,
        in_specs=[HBM] * 3,
        scratch=fields + [dma4],
    )
    ghosts = exchange(*sent)
    w_hi, w_lo = pl.pallas_call(
        weights_kernel,
        grid=(obs // OBS_BLOCK,),
        out_shape=[jax.ShapeDtypeStruct((slots, obs), BF16)] * 2,
        in_specs=[pl.BlockSpec((taps, OBS_BLOCK), lambda j: (0, j))] * 2,
        out_specs=[pl.BlockSpec((slots, OBS_BLOCK), lambda j: (0, j))] * 2,
        compiler_params=pltpu.CompilerParams(vmem_limit_bytes=48 * MIB),
        cost_estimate=pl.CostEstimate(flops=10 * slots * obs, bytes_accessed=4 * slots * obs, transcendentals=0),
    )(obs_slots, obs_weights)
    (inner,) = call(
        functools.partial(inner_kernel, vals, vp),
        [((vp, slots), F32)],
        *flat,
        cells,
        in_specs=[HBM] * 3 + [VMEM],
        scratch=fields + [pltpu.VMEM((vp, cell_count), F32), pltpu.VMEM((cell_count, 7 * LANES), BF16), dma4],
        flops=4 * vp * cell_count * slots,
        nbytes=8 * MIB,
    )
    (payload,) = call(
        functools.partial(send_kernel, owners, vp, mp),
        [((owners * ROWS, LANES), F32)],
        *ghosts, rv, rc, pk, inner, cells,
    )
    received = across(payload)
    equivalents, payload = pl.pallas_call(
        functools.partial(owner_kernel, vals, vp, owners),
        grid=(obs // OBS_BLOCK,),
        out_shape=[jax.ShapeDtypeStruct((vals, obs), F32), jax.ShapeDtypeStruct((owners * ROWS, LANES), F32)],
        in_specs=[
            pl.BlockSpec((owners * ROWS, LANES), lambda j: (0, 0)),
            pl.BlockSpec((slots, OBS_BLOCK), lambda j: (0, j)),
            pl.BlockSpec((slots, OBS_BLOCK), lambda j: (0, j)),
            pl.BlockSpec((vals, OBS_BLOCK), lambda j: (0, j)),
        ],
        out_specs=[
            pl.BlockSpec((vals, OBS_BLOCK), lambda j: (0, j)),
            pl.BlockSpec((owners * ROWS, LANES), lambda j: (0, 0)),
        ],
        scratch_shapes=[pltpu.VMEM((2 * vp, slots), BF16), pltpu.VMEM((vp, OBS_BLOCK), F32), pltpu.VMEM((vp, slots), F32)],
        compiler_params=pltpu.CompilerParams(vmem_limit_bytes=48 * MIB),
    )(received, w_hi, w_lo, obs_precision)
    incoming = across(payload)
    *sent, inc, ra, pa = call(
        functools.partial(back_kernel, owners, vp, mp),
        messages(2) + [((2 * vp, slots), BF16), ((4 * vp, LANES), F32), ((2 * vp, LANES), F32)],
        incoming, cells, rc, pk,
    )
    adjoint_ghosts = exchange(*sent)
    (part,) = call(
        functools.partial(adjoint_kernel, vals, vp),
        [((vals * ROWS, LANES), F32)],
        *flat, inc, cells,
        in_specs=[HBM] * 3 + [VMEM] * 2,
        scratch=fields + [pltpu.VMEM((ROWS * vp, LANES), F32), dma4, pltpu.SemaphoreType.DMA(())],
        out_specs=[HBM],
        flops=4 * vp * cell_count * slots,
        nbytes=10 * MIB,
    )
    (product,) = call(
        functools.partial(final_kernel, vals, vp, mp),
        [((vals * ROWS, LANES), F32)],
        *ghosts, *adjoint_ghosts, ra, rc, pk, pa, part,
        in_specs=[VMEM] * 20 + [HBM],
        scratch=[pltpu.VMEM((vp * ROWS, LANES), F32), pltpu.VMEM(line, F32), pltpu.SemaphoreType.DMA(())],
        out_specs=[HBM],
    )
    return product.reshape(state.shape), equivalents


def solution(mesh):
    placed = (
        P(None, "lat", "lon"),
        P(None, "lat", "lon"),
        P(None, "lat", "lon"),
        P(("lon", "lat"), None),
        P(None, ("lon", "lat")),
        P(None, ("lon", "lat")),
        P(None, ("lon", "lat")),
    )
    return jax.shard_map(
        on_device,
        mesh=mesh,
        in_specs=placed,
        out_specs=(P(None, "lat", "lon"), P(None, ("lon", "lat"))),
        check_vma=False,
    )
```

profile of v0, /device:TPU:2, one launch (start us, length us, event | category | flops | bytes accessed | tf_op | source)
XLA Modules:
  0.0 173.9 jit_solution(1484491955906375297)
XLA Ops:
  3.6 11.4 %shard_map.86 = (f32[456,128]{1,0:T(8,128)}, f32[456,128]{1,0:T(8,128)}, f32[152,128]{1,0:T(8,128)S(1)}, f32[152,128]{1,0:T(8,128)S(1)}, f32[8,256]{1,0:T(8,128)...) custom-call(f32[4800,128]{1,0:T(8,128)S(1)} %bitcast.15, ...), custom_call_target="tpu_custom_call" | custom-call | tf_op jit(solution)/shard_map/pallas_call | solution.py:221
  17.0 5.9 %collective-permute-start.4 = (f32[8,256]{1,0:T(8,128)S(1)}, f32[8,256]{1,0:T(8,128)S(1)}, u32[]{:S(2)}, u32[]{:S(2)}) collective-permute-start(f32[8,256]{1,0:T(8,128)S(1)} %get-tuple-element.32), channel_id=1, source_target_pairs={{0,29},{1,30},{2,31},{4,1},{5,2},{6,3},{8,5},{9,6},{10,7},{12,9},{... | collective-permute-start | bytes 24584 | tf_op jit(solution)/shard_map/ppermute | solution.py:460
  22.9 1.9 %collective-permute-start.5 = (f32[8,256]{1,0:T(8,128)}, f32[8,256]{1,0:T(8,128)S(1)}, u32[]{:S(2)}, u32[]{:S(2)}) collective-permute-start(f32[8,256]{1,0:T(8,128)} %get-tuple-element.33), channel_id=1, source_target_pairs={{0,5},{1,6},{2,7},{4,9},{5,10},{6,11},{8,13},{9,14},{10,15},{12,17... | collective-permute-start | bytes 24584 | tf_op jit(solution)/shard_map/ppermute | solution.py:460
  24.8 6.3 %collective-permute-start.6 = (f32[8,256]{1,0:T(8,128)S(1)}, f32[8,256]{1,0:T(8,128)S(1)}, u32[]{:S(2)}, u32[]{:S(2)}) collective-permute-start(f32[8,256]{1,0:T(8,128)S(1)} %get-tuple-element.34), channel_id=1, source_target_pairs={{1,28},{2,29},{3,30},{5,0},{6,1},{7,2},{9,4},{10,5},{11,6},{13,8},... | collective-permute-start | bytes 24584 | tf_op jit(solution)/shard_map/ppermute | solution.py:460
  31.2 4.3 %collective-permute-start = (f32[456,128]{1,0:T(8,128)}, f32[456,128]{1,0:T(8,128)S(1)}, u32[]{:S(2)}, u32[]{:S(2)}) collective-permute-start(f32[456,128]{1,0:T(8,128)} %get-tuple-element.28), channel_id=1, source_target_pairs={{0,1},{1,2},{2,3},{4,5},{5,6},{6,7},{8,9},{9,10},{10,11},{12,13},{... | collective-permute-start | bytes 700424 | tf_op jit(solution)/shard_map/ppermute | solution.py:460
  35.5 1.9 %collective-permute-start.1 = (f32[456,128]{1,0:T(8,128)}, f32[456,128]{1,0:T(8,128)S(1)}, u32[]{:S(2)}, u32[]{:S(2)}) collective-permute-start(f32[456,128]{1,0:T(8,128)} %get-tuple-element.29), channel_id=1, source_target_pairs={{1,0},{2,1},{3,2},{5,4},{6,5},{7,6},{9,8},{10,9},{11,10},{13,12},{... | collective-permute-start | bytes 700424 | tf_op jit(solution)/shard_map/ppermute | solution.py:460
  37.6 1.9 %collective-permute-start.7 = (f32[8,256]{1,0:T(8,128)S(1)}, f32[8,256]{1,0:T(8,128)S(1)}, u32[]{:S(2)}, u32[]{:S(2)}) collective-permute-start(f32[8,256]{1,0:T(8,128)S(1)} %get-tuple-element.35), channel_id=1, source_target_pairs={{1,4},{2,5},{3,6},{5,8},{6,9},{7,10},{9,12},{10,13},{11,14},{13,16... | collective-permute-start | bytes 24584 | tf_op jit(solution)/shard_map/ppermute | solution.py:460
  39.5 2.0 %collective-permute-start.2 = (f32[152,128]{1,0:T(8,128)}, f32[152,128]{1,0:T(8,128)S(1)}, u32[]{:S(2)}, u32[]{:S(2)}) collective-permute-start(f32[152,128]{1,0:T(8,128)} %copy-done.15), channel_id=1, source_target_pairs={{0,28},{1,29},{2,30},{3,31},{4,0},{5,1},{6,2},{7,3},{8,4},{9,5},{1... | collective-permute-start | bytes 233480 | tf_op jit(solution)/shard_map/ppermute | solution.py:460
  42.8 16.5 %shard_map.87.inner = f32[160,896]{1,0:T(8,128)S(1)} custom-call(f32[4800,128]{1,0:T(8,128)S(1)} %bitcast.16, f32[4800,128]{1,0:T(8,128)} %bitcast.28, s32[2400,128]{1,0:T(8,128)S(1)} %bitcast.18, s32[1,896]{1,0:T(1,128)S(1)} %bitcast.23), custom_call_target="tpu_custom_call" | custom-call | flops 2348810240 | bytes 8388608 | tf_op jit(solution)/shard_map/pallas_call | solution.py:221
  59.5 2.6 %shard_map.88 = f32[1024,128]{1,0:T(8,128)} custom-call(f32[456,128]{1,0:T(8,128)S(1)} %collective-permute-done.f_n, f32[456,128]{1,0:T(8,128)S(1)} %collective-permute-done.1.f_s, f32[152,128]{1,0:T(8,128)S(1)} %collective-permute-done.2.f_e, f32[152,128]{1,0:T(8,128)S(1)} %collective-permute-done.3.f_w, f32[8,256]{1,0:T(8,128)S(1)} %collective-permute-done.4.k_ne, ...), custom_call_target="tpu_custom_call" | custom-call | tf_op jit(solution)/shard_map/pallas_call | solution.py:221
  62.1 9.0 %all-to-all-start = ((f32[32,32,128]{2,1,0:T(8,128)}), f32[32,32,128]{2,1,0:T(8,128)S(1)}, u32[]{:S(2)}, u32[]{:S(2)}) async-start(f32[32,32,128]{2,1,0:T(8,128)} %bitcast.3), calls=%async_computation | async-start | bytes 1048576 | tf_op jit(solution)/shard_map/all_to_all | solution.py:476
  71.2 5.9 %shard_map.89 = (bf16[896,2048]{1,0:T(8,128)(2,1)S(1)}, bf16[896,2048]{1,0:T(8,128)(2,1)}) custom-call(s32[4,2048]{1,0:T(4,128)S(1)} %copy-done.16, f32[4,2048]{1,0:T(4,128)S(1)} %copy-done.17), custom_call_target="tpu_custom_call" | custom-call | flops 18350080 | bytes 7340032 | tf_op jit(solution)/shard_map/pallas_call | solution.py:507
  78.8 7.0 %all-to-all-done = f32[32,32,128]{2,1,0:T(8,128)S(1)} async-done(((f32[32,32,128]{2,1,0:T(8,128)}), f32[32,32,128]{2,1,0:T(8,128)S(1)}, u32[]{:S(2)}, u32[]{:S(2)}) %all-to-all-start) | async-done | bytes 524320 | tf_op jit(solution)/shard_map/all_to_all | solution.py:476
  85.8 2.0 %copy-done.6 = bf16[896,2048]{1,0:T(8,128)(2,1)S(1)} copy-done((bf16[896,2048]{1,0:T(8,128)(2,1)S(1)}, bf16[896,2048]{1,0:T(8,128)(2,1)}, u32[]{:S(2)}) %copy-start.6) | copy-done | bytes 3670040
  87.9 13.8 %shard_map.90 = (f32[150,2048]{1,0:T(8,128)}, f32[1024,128]{1,0:T(8,128)S(1)}) custom-call(f32[1024,128]{1,0:T(8,128)S(1)} %bitcast.20, bf16[896,2048]{1,0:T(8,128)(2,1)S(1)} %copy-done.6, bf16[896,2048]{1,0:T(8,128)(2,1)} %get-tuple-element.40.w_lo, f32[150,2048]{1,0:T(8,128)S(1)} %copy-done.7), custom_call_target="tpu_custom_call" | custom-call | tf_op jit(solution)/shard_map/pallas_call | solution.py:532
  101.7 18.4 %all_to_all.22 = f32[32,32,128]{2,1,0:T(8,128)S(1)} all-to-all(f32[32,32,128]{2,1,0:T(8,128)S(1)} %bitcast.22), channel_id=1, replica_groups=mesh['lon'=8,'lat'=4] {'lon','lat'}, dimensions={0} | all-to-all | bytes 1048576 | tf_op jit(solution)/shard_map/all_to_all | solution.py:476
  121.6 4.4 %collective-permute-start.12 = (f32[8,256]{1,0:T(8,128)S(1)}, f32[8,256]{1,0:T(8,128)S(1)}, u32[]{:S(2)}, u32[]{:S(2)}) collective-permute-start(f32[8,256]{1,0:T(8,128)S(1)} %get-tuple-element.46), channel_id=1, source_target_pairs={{0,29},{1,30},{2,31},{4,1},{5,2},{6,3},{8,5},{9,6},{10,7},{12,9},{... | collective-permute-start | bytes 24584 | tf_op jit(solution)/shard_map/ppermute | solution.py:460
  126.0 2.1 %collective-permute-start.13 = (f32[8,256]{1,0:T(8,128)S(1)}, f32[8,256]{1,0:T(8,128)S(1)}, u32[]{:S(2)}, u32[]{:S(2)}) collective-permute-start(f32[8,256]{1,0:T(8,128)S(1)} %get-tuple-element.47), channel_id=1, source_target_pairs={{0,5},{1,6},{2,7},{4,9},{5,10},{6,11},{8,13},{9,14},{10,15},{12,17... | collective-permute-start | bytes 24584 | tf_op jit(solution)/shard_map/ppermute | solution.py:460
  128.1 6.2 %collective-permute-start.14 = (f32[8,256]{1,0:T(8,128)S(1)}, f32[8,256]{1,0:T(8,128)S(1)}, u32[]{:S(2)}, u32[]{:S(2)}) collective-permute-start(f32[8,256]{1,0:T(8,128)S(1)} %get-tuple-element.48), channel_id=1, source_target_pairs={{1,28},{2,29},{3,30},{5,0},{6,1},{7,2},{9,4},{10,5},{11,6},{13,8},... | collective-permute-start | bytes 24584 | tf_op jit(solution)/shard_map/ppermute | solution.py:460
  134.3 1.9 %collective-permute-start.15 = (f32[8,256]{1,0:T(8,128)S(1)}, f32[8,256]{1,0:T(8,128)S(1)}, u32[]{:S(2)}, u32[]{:S(2)}) collective-permute-start(f32[8,256]{1,0:T(8,128)S(1)} %get-tuple-element.49), channel_id=1, source_target_pairs={{1,4},{2,5},{3,6},{5,8},{6,9},{7,10},{9,12},{10,13},{11,14},{13,16... | collective-permute-start | bytes 24584 | tf_op jit(solution)/shard_map/ppermute | solution.py:460
  136.8 7.3 %collective-permute-start.8 = (f32[304,128]{1,0:T(8,128)S(1)}, f32[304,128]{1,0:T(8,128)S(1)}, u32[]{:S(2)}, u32[]{:S(2)}) collective-permute-start(f32[304,128]{1,0:T(8,128)S(1)} %get-tuple-element.42), channel_id=1, source_target_pairs={{0,1},{1,2},{2,3},{4,5},{5,6},{6,7},{8,9},{9,10},{10,11},{12,13},{... | collective-permute-start | bytes 466952 | tf_op jit(solution)/shard_map/ppermute | solution.py:460
  144.1 2.1 %collective-permute-start.9 = (f32[304,128]{1,0:T(8,128)S(1)}, f32[304,128]{1,0:T(8,128)S(1)}, u32[]{:S(2)}, u32[]{:S(2)}) collective-permute-start(f32[304,128]{1,0:T(8,128)S(1)} %get-tuple-element.43), channel_id=1, source_target_pairs={{1,0},{2,1},{3,2},{5,4},{6,5},{7,6},{9,8},{10,9},{11,10},{13,12},{... | collective-permute-start | bytes 466952 | tf_op jit(solution)/shard_map/ppermute | solution.py:460
  146.3 21.3 %shard_map.92.part = f32[4800,128]{1,0:T(8,128)S(1)} custom-call(f32[4800,128]{1,0:T(8,128)} %bitcast.14, f32[4800,128]{1,0:T(8,128)} %bitcast.29, s32[2400,128]{1,0:T(8,128)S(1)} %bitcast.19, bf16[320,896]{1,0:T(8,128)(2,1)S(1)} %get-tuple-element.52.inc, s32[1,896]{1,0:T(1,128)S(1)} %bitcast.26), custom_call_target="tpu_custom_call" | custom-call | flops 2348810240 | bytes 10485760 | tf_op jit(solution)/shard_map/pallas_call | solution.py:221
  167.7 6.1 %shard_map.93 = f32[4800,128]{1,0:T(8,128)} custom-call(f32[456,128]{1,0:T(8,128)S(1)} %collective-permute-done.f_n, f32[456,128]{1,0:T(8,128)S(1)} %collective-permute-done.1.f_s, f32[152,128]{1,0:T(8,128)S(1)} %copy-done.11, f32[152,128]{1,0:T(8,128)S(1)} %copy-done.13, f32[8,256]{1,0:T(8,128)S(1)} %collective-permute-done.4.k_ne, ...), custom_call_target="tpu_custom_call" | custom-call | tf_op jit(solution)/shard_map/pallas_call | solution.py:221
  (61 shorter events, 10.3 us)
Async XLA Ops:
  3.6 33.8 %copy-start.18 = (s32[1,768]{1,0:T(1,128)S(1)}, s32[1,768]{1,0:T(1,128)}, u32[]{:S(2)}) copy-start(s32[1,768]{1,0:T(1,128)} %param.10) | copy-start | bytes 9220
  3.6 37.9 %copy-start.1 = (f32[150,32,128]{2,1,0:T(8,128)S(1)}, f32[150,32,128]{2,1,0:T(8,128)}, u32[]{:S(2)}) copy-start(f32[150,32,128]{2,1,0:T(8,128)} %param.7) | copy-start | bytes 7372804
  17.0 20.5 %collective-permute-start.4 = (f32[8,256]{1,0:T(8,128)S(1)}, f32[8,256]{1,0:T(8,128)S(1)}, u32[]{:S(2)}, u32[]{:S(2)}) collective-permute-start(f32[8,256]{1,0:T(8,128)S(1)} %get-tuple-element.32), channel_id=1, source_target_pairs={{0,29},{1,30},{2,31},{4,1},{5,2},{6,3},{8,5},{9,6},{10,7},{12,9},{... | collective-permute-start | bytes 24584 | tf_op jit(solution)/shard_map/ppermute | solution.py:460
  22.9 16.6 %collective-permute-start.5 = (f32[8,256]{1,0:T(8,128)}, f32[8,256]{1,0:T(8,128)S(1)}, u32[]{:S(2)}, u32[]{:S(2)}) collective-permute-start(f32[8,256]{1,0:T(8,128)} %get-tuple-element.33), channel_id=1, source_target_pairs={{0,5},{1,6},{2,7},{4,9},{5,10},{6,11},{8,13},{9,14},{10,15},{12,17... | collective-permute-start | bytes 24584 | tf_op jit(solution)/shard_map/ppermute | solution.py:460
  24.8 16.7 %collective-permute-start.6 = (f32[8,256]{1,0:T(8,128)S(1)}, f32[8,256]{1,0:T(8,128)S(1)}, u32[]{:S(2)}, u32[]{:S(2)}) collective-permute-start(f32[8,256]{1,0:T(8,128)S(1)} %get-tuple-element.34), channel_id=1, source_target_pairs={{1,28},{2,29},{3,30},{5,0},{6,1},{7,2},{9,4},{10,5},{11,6},{13,8},... | collective-permute-start | bytes 24584 | tf_op jit(solution)/shard_map/ppermute | solution.py:460
  31.2 28.3 %collective-permute-start = (f32[456,128]{1,0:T(8,128)}, f32[456,128]{1,0:T(8,128)S(1)}, u32[]{:S(2)}, u32[]{:S(2)}) collective-permute-start(f32[456,128]{1,0:T(8,128)} %get-tuple-element.28), channel_id=1, source_target_pairs={{0,1},{1,2},{2,3},{4,5},{5,6},{6,7},{8,9},{9,10},{10,11},{12,13},{... | collective-permute-start | bytes 700424 | tf_op jit(solution)/shard_map/ppermute | solution.py:460
  35.5 24.0 %collective-permute-start.1 = (f32[456,128]{1,0:T(8,128)}, f32[456,128]{1,0:T(8,128)S(1)}, u32[]{:S(2)}, u32[]{:S(2)}) collective-permute-start(f32[456,128]{1,0:T(8,128)} %get-tuple-element.29), channel_id=1, source_target_pairs={{1,0},{2,1},{3,2},{5,4},{6,5},{7,6},{9,8},{10,9},{11,10},{13,12},{... | collective-permute-start | bytes 700424 | tf_op jit(solution)/shard_map/ppermute | solution.py:460
  37.6 21.9 %collective-permute-start.7 = (f32[8,256]{1,0:T(8,128)S(1)}, f32[8,256]{1,0:T(8,128)S(1)}, u32[]{:S(2)}, u32[]{:S(2)}) collective-permute-start(f32[8,256]{1,0:T(8,128)S(1)} %get-tuple-element.35), channel_id=1, source_target_pairs={{1,4},{2,5},{3,6},{5,8},{6,9},{7,10},{9,12},{10,13},{11,14},{13,16... | collective-permute-start | bytes 24584 | tf_op jit(solution)/shard_map/ppermute | solution.py:460
  39.5 19.9 %collective-permute-start.2 = (f32[152,128]{1,0:T(8,128)}, f32[152,128]{1,0:T(8,128)S(1)}, u32[]{:S(2)}, u32[]{:S(2)}) collective-permute-start(f32[152,128]{1,0:T(8,128)} %copy-done.15), channel_id=1, source_target_pairs={{0,28},{1,29},{2,30},{3,31},{4,0},{5,1},{6,2},{7,3},{8,4},{9,5},{1... | collective-permute-start | bytes 233480 | tf_op jit(solution)/shard_map/ppermute | solution.py:460
  41.5 17.9 %collective-permute-start.3 = (f32[152,128]{1,0:T(8,128)}, f32[152,128]{1,0:T(8,128)S(1)}, u32[]{:S(2)}, u32[]{:S(2)}) collective-permute-start(f32[152,128]{1,0:T(8,128)} %copy-done.14), channel_id=1, source_target_pairs={{0,4},{1,5},{2,6},{3,7},{4,8},{5,9},{6,10},{7,11},{8,12},{9,13},{1... | collective-permute-start | bytes 233480 | tf_op jit(solution)/shard_map/ppermute | solution.py:460
  42.8 16.7 %copy-start.9 = (f32[640,128]{1,0:T(8,128)S(1)}, f32[640,128]{1,0:T(8,128)}, u32[]{:S(2)}) copy-start(f32[640,128]{1,0:T(8,128)} %copy-done.8) | copy-start | bytes 983044
  59.4 26.4 %copy-start.7 = (f32[150,2048]{1,0:T(8,128)S(1)}, f32[150,2048]{1,0:T(8,128)}, u32[]{:S(2)}) copy-start(f32[150,2048]{1,0:T(8,128)} %prec.1) | copy-start | bytes 3686404
  62.1 23.7 %all-to-all-start = ((f32[32,32,128]{2,1,0:T(8,128)}), f32[32,32,128]{2,1,0:T(8,128)S(1)}, u32[]{:S(2)}, u32[]{:S(2)}) async-start(f32[32,32,128]{2,1,0:T(8,128)} %bitcast.3), calls=%async_computation | async-start | bytes 1048576 | tf_op jit(solution)/shard_map/all_to_all | solution.py:476
  101.7 44.6 %copy-start.4 = (s32[75,32,128]{2,1,0:T(8,128)S(1)}, s32[75,32,128]{2,1,0:T(8,128)}, u32[]{:S(2)}) copy-start(s32[75,32,128]{2,1,0:T(8,128)} %param.9) | copy-start | bytes 3686404
  121.6 14.7 %collective-permute-start.12 = (f32[8,256]{1,0:T(8,128)S(1)}, f32[8,256]{1,0:T(8,128)S(1)}, u32[]{:S(2)}, u32[]{:S(2)}) collective-permute-start(f32[8,256]{1,0:T(8,128)S(1)} %get-tuple-element.46), channel_id=1, source_target_pairs={{0,29},{1,30},{2,31},{4,1},{5,2},{6,3},{8,5},{9,6},{10,7},{12,9},{... | collective-permute-start | bytes 24584 | tf_op jit(solution)/shard_map/ppermute | solution.py:460
  126.0 10.8 %collective-permute-start.13 = (f32[8,256]{1,0:T(8,128)S(1)}, f32[8,256]{1,0:T(8,128)S(1)}, u32[]{:S(2)}, u32[]{:S(2)}) collective-permute-start(f32[8,256]{1,0:T(8,128)S(1)} %get-tuple-element.47), channel_id=1, source_target_pairs={{0,5},{1,6},{2,7},{4,9},{5,10},{6,11},{8,13},{9,14},{10,15},{12,17... | collective-permute-start | bytes 24584 | tf_op jit(solution)/shard_map/ppermute | solution.py:460
  128.1 16.0 %collective-permute-start.14 = (f32[8,256]{1,0:T(8,128)S(1)}, f32[8,256]{1,0:T(8,128)S(1)}, u32[]{:S(2)}, u32[]{:S(2)}) collective-permute-start(f32[8,256]{1,0:T(8,128)S(1)} %get-tuple-element.48), channel_id=1, source_target_pairs={{1,28},{2,29},{3,30},{5,0},{6,1},{7,2},{9,4},{10,5},{11,6},{13,8},... | collective-permute-start | bytes 24584 | tf_op jit(solution)/shard_map/ppermute | solution.py:460
  134.3 33.3 %collective-permute-start.15 = (f32[8,256]{1,0:T(8,128)S(1)}, f32[8,256]{1,0:T(8,128)S(1)}, u32[]{:S(2)}, u32[]{:S(2)}) collective-permute-start(f32[8,256]{1,0:T(8,128)S(1)} %get-tuple-element.49), channel_id=1, source_target_pairs={{1,4},{2,5},{3,6},{5,8},{6,9},{7,10},{9,12},{10,13},{11,14},{13,16... | collective-permute-start | bytes 24584 | tf_op jit(solution)/shard_map/ppermute | solution.py:460
  136.2 31.4 %collective-permute-start.10 = (f32[152,128]{1,0:T(8,128)S(1)}, f32[152,128]{1,0:T(8,128)S(1)}, u32[]{:S(2)}, u32[]{:S(2)}) collective-permute-start(f32[152,128]{1,0:T(8,128)S(1)} %get-tuple-element.44), channel_id=1, source_target_pairs={{0,28},{1,29},{2,30},{3,31},{4,0},{5,1},{6,2},{7,3},{8,4},{9,5},{1... | collective-permute-start | bytes 233480 | tf_op jit(solution)/shard_map/ppermute | solution.py:460
  136.3 31.4 %collective-permute-start.11 = (f32[152,128]{1,0:T(8,128)S(1)}, f32[152,128]{1,0:T(8,128)S(1)}, u32[]{:S(2)}, u32[]{:S(2)}) collective-permute-start(f32[152,128]{1,0:T(8,128)S(1)} %get-tuple-element.45), channel_id=1, source_target_pairs={{0,4},{1,5},{2,6},{3,7},{4,8},{5,9},{6,10},{7,11},{8,12},{9,13},{1... | collective-permute-start | bytes 233480 | tf_op jit(solution)/shard_map/ppermute | solution.py:460
  136.8 30.9 %collective-permute-start.8 = (f32[304,128]{1,0:T(8,128)S(1)}, f32[304,128]{1,0:T(8,128)S(1)}, u32[]{:S(2)}, u32[]{:S(2)}) collective-permute-start(f32[304,128]{1,0:T(8,128)S(1)} %get-tuple-element.42), channel_id=1, source_target_pairs={{0,1},{1,2},{2,3},{4,5},{5,6},{6,7},{8,9},{9,10},{10,11},{12,13},{... | collective-permute-start | bytes 466952 | tf_op jit(solution)/shard_map/ppermute | solution.py:460
  144.1 23.6 %collective-permute-start.9 = (f32[304,128]{1,0:T(8,128)S(1)}, f32[304,128]{1,0:T(8,128)S(1)}, u32[]{:S(2)}, u32[]{:S(2)}) collective-permute-start(f32[304,128]{1,0:T(8,128)S(1)} %get-tuple-element.43), channel_id=1, source_target_pairs={{1,0},{2,1},{3,2},{5,4},{6,5},{7,6},{9,8},{10,9},{11,10},{13,12},{... | collective-permute-start | bytes 466952 | tf_op jit(solution)/shard_map/ppermute | solution.py:460
  146.2 21.4 %copy-start.11 = (f32[152,128]{1,0:T(8,128)S(1)}, f32[152,128]{1,0:T(8,128)}, u32[]{:S(2)}) copy-start(f32[152,128]{1,0:T(8,128)} %copy-done.10) | copy-start | bytes 233476
  146.3 21.4 %copy-start.13 = (f32[152,128]{1,0:T(8,128)S(1)}, f32[152,128]{1,0:T(8,128)}, u32[]{:S(2)}) copy-start(f32[152,128]{1,0:T(8,128)} %copy-done.12) | copy-start | bytes 233476
  (12 other events, 38.9 us)
where the time goes:
time: 176 us; the launch traced here: 174 us
  Pallas kernels  79.1 us (45%)
  starting transfers between devices  57.9 us (33%)
  blocking collectives  18.4 us (10%)
  local copies, waits for them, and re-layouts  10.3 us (6%)
  waiting for transfers between devices  7.05 us (4%)
    pallas_call x6, Pallas kernels, call(): pl.pallas_call(kernel, out_shape=[jax.ShapeDtypeStruct(s, d) for s, d in...  59.5 us
    ppermute x16, starting transfers between devices, neighbour(): return lax.ppermute(x, ('lon', 'lat'), pairs)  48.9 us
    all_to_all x1, blocking collectives, across(): lax.all_to_all(x, ('lon', 'lat'), split_axis=0, concat_axis=0, tiled=True)  18.4 us
    pallas_call x1, Pallas kernels, on_device(): pl.pallas_call(functools.partial(owner_kernel, vals, vp, owners), grid=(o...  13.8 us
    unnamed x40, local copies, waits for them, and re-layouts  10.2 us
    all_to_all x1, starting transfers between devices, across(): lax.all_to_all(x, ('lon', 'lat'), split_axis=0, concat_axis=0, tiled=True)  8.99 us
    all_to_all x1, waiting for transfers between devices, across(): lax.all_to_all(x, ('lon', 'lat'), split_axis=0, concat_axis=0, tiled=True)  7.01 us
    pallas_call x1, Pallas kernels, on_device(): pl.pallas_call(weights_kernel, grid=(obs // OBS_BLOCK,), out_shape=[jax.S...  5.87 us
  transfers between devices with their start and end apart: 17, of which 1 were waited for; matrix products, arithmetic and copies ran while one was open for 0% of the time, Pallas kernels for 25%

commit v1 on v0

v1 whole, which is shorter than its diff:
```python
import functools

import jax
import jax.numpy as jnp
from jax import lax
from jax.experimental import pallas as pl
from jax.experimental.pallas import tpu as pltpu
from jax.sharding import PartitionSpec as P

CAP = 24
LANES = 128
GROUPS = 5
ROWS = 32
OBS_BLOCK = 256
F32, BF16 = jnp.float32, jnp.bfloat16
MIB = 1 << 20


def up(n, k):
    return -(-n // k) * k


def roll(x, k):
    k %= LANES
    return x if k == 0 else pltpu.roll(x, k, axis=1)


def lane_of(x):
    return lax.broadcasted_iota(jnp.int32, x.shape, 1)


def tall(x, rows):
    return jnp.concatenate([x, jnp.zeros((rows - x.shape[0], x.shape[1]), x.dtype)], axis=0)


def halves(x):
    hi = x.astype(BF16)
    return hi, (x - hi.astype(F32)).astype(BF16)


def dot(a, b):
    return lax.dot_general(a, b, (((1,), (0,)), ((), ())), preferred_element_type=F32)


def dot_nt(a, b):
    return lax.dot_general(a, b, (((1,), (1,)), ((), ())), preferred_element_type=F32)


def stacked(x):
    return jnp.concatenate(halves(x), axis=0)


def folded(x):
    n = x.shape[0] // 2
    return x[:n] + x[n:]


def row_edges(c):
    east = jnp.where(lane_of(c) == LANES - 1, 0.0, jnp.minimum(c, roll(c, -1)))
    return east, roll(east, 1)


def pack_edges(cp):
    lane = lane_of(cp)
    kind = lane & 3
    inner = jnp.where(kind == 1, roll(cp, 1), roll(cp, -1))
    inner = jnp.where((kind == 1) | (kind == 2), jnp.minimum(cp, inner), 0.0)
    south = jnp.where(lane >= LANES - 4, 0.0, jnp.minimum(cp, roll(cp, -4)))
    return kind, inner, south, roll(south, 4)


def rim_rows(v0, v1, v30, v31, c0, c1, c30, c31):
    out = []
    for v, w, c, d in ((v0, v1, c0, c1), (v31, v30, c31, c30)):
        east, west = row_edges(c)
        out.append(v + east * (roll(v, -1) - v) + west * (roll(v, 1) - v) + jnp.minimum(c, d) * (w - v))
    return out


def rim_pack(vp, cp):
    kind, inner, south, north = pack_edges(cp)
    beside = jnp.where(kind == 1, roll(vp, 1), roll(vp, -1))
    return vp + inner * (beside - vp) + south * (roll(vp, -4) - vp) + north * (roll(vp, 4) - vp)


def pack_messages(vp, cp, pp, north, south):
    lane = lane_of(vp)
    kind = lane & 3
    east = jnp.where(kind == 0, roll(vp, -1), jnp.where(kind == 1, cp, roll(pp, 1)))
    west = jnp.where(kind == 0, roll(vp, -2), jnp.where(kind == 1, roll(cp, -1), pp))
    for k, x in zip((3, 7, 11, 15), (*north, *south)):
        east = jnp.where(lane == k, roll(x, k + 1), east)
        west = jnp.where(lane == k, roll(x, k), west)
    return east, west


def ghost_pack(from_w, from_e):
    one = (lane_of(from_w) & 3) == 1
    v = jnp.where(one, roll(from_e, 1), roll(from_w, 2))
    c = jnp.where(one, from_e, roll(from_w, 1))
    p = jnp.where(one, roll(from_e, -1), from_w)
    return v, c, p


def corner_pack(from_w, from_e):
    lane = lane_of(from_w)
    out = []
    for n, s in ((3, 11), (7, 15)):
        x = jnp.zeros_like(from_w)
        for at, src, k in ((1, from_e, n), (2, from_w, n), (LANES - 3, from_e, s), (LANES - 2, from_w, s)):
            x = jnp.where(lane == at, roll(src, at - k), x)
        out.append(x)
    return out


def rim_correction(own, coef, ghosts):
    v0, v31, p0, p31, vp, pp = own
    c0, c1, c30, c31, cp = coef
    (gvn, gcn, gpn), (gvs, gcs, gps), (gv, gc, gp), (kv, kc) = ghosts
    lane = lane_of(v0)
    ends = (lane == 0) | (lane == LANES - 1)
    kind, inner, south, north = pack_edges(cp)
    mid = (kind == 1) | (kind == 2)
    mg = jnp.where(mid, jnp.minimum(cp, gc), 0.0)
    f = mg * (gv - vp)
    mn, ms = jnp.minimum(c0, gcn), jnp.minimum(c31, gcs)
    fn, fs = mn * (gvn - v0), ms * (gvs - v31)
    ghost = gp - f + jnp.where(mid, jnp.minimum(gc, kc), 0.0) * (kv - gv)
    ghost_n = gpn - fn + jnp.where(ends, jnp.minimum(gcn, roll(kc, -2)), 0.0) * (roll(kv, -2) - gvn)
    ghost_s = gps - fs + jnp.where(ends, jnp.minimum(gcs, roll(kc, 2)), 0.0) * (roll(kv, 2) - gvs)
    whole = pp + f + jnp.where((lane == 1) | (lane == 2), roll(fn, 2), 0.0)
    whole = whole + jnp.where((lane == LANES - 3) | (lane == LANES - 2), roll(fs, -2), 0.0)
    whole_n = p0 + fn + jnp.where(ends, roll(f, -2), 0.0)
    whole_s = p31 + fs + jnp.where(ends, roll(f, 2), 0.0)
    qf = inner * f
    rp = f - qf + south * (roll(f, -4) - f) + north * (roll(f, 4) - f) + mg * (ghost - whole)
    rp = jnp.where(mid, rp, jnp.where(kind == 0, roll(qf, -1), roll(qf, 1)))
    rows = []
    for c, d, m, g, w, x in ((c0, c1, mn, ghost_n, whole_n, fn), (c31, c30, ms, ghost_s, whole_s, fs)):
        east, west = row_edges(c)
        across = jnp.minimum(c, d)
        rows.append(x + east * (roll(x, -1) - x) + west * (roll(x, 1) - x) - across * x + m * (g - w))
        rows.append(across * x)
    return rows[0], rows[1], rows[3], rows[2], rp


def sweep(src, edges, emit):
    east, west, south = edges
    for i in range(ROWS):
        x = src[i]
        y = x + east[i] * (roll(x, -1) - x) + west[i] * (roll(x, 1) - x)
        if i < ROWS - 1:
            y = y + south[i] * (src[i + 1] - x)
        if i > 0:
            y = y + south[i - 1] * (src[i - 1] - x)
        emit(i, y)


def chosen(cells, ids):
    return jnp.where(ids == cells, 1.0, 0.0).astype(BF16)


def rim_ids(n):
    line = lax.broadcasted_iota(jnp.int32, (LANES, n), 0)
    rows = [line + i * LANES for i in (0, 1, ROWS - 2, ROWS - 1)]
    k = line & 3
    pack = (line >> 2) * LANES + jnp.where(k < 2, LANES - 2 + k, k - 2)
    return jnp.concatenate(rows + [pack], axis=0)


def pack_payload(x, out_ref, owners):
    lane = lax.broadcasted_iota(jnp.int32, (ROWS, LANES), 1)
    for o in range(owners):
        a, b = divmod(o, GROUPS)
        block = jnp.zeros((ROWS, LANES), F32)
        for g in range(GROUPS):
            piece = roll(x[ROWS * g : ROWS * (g + 1), LANES * a : LANES * (a + 1)], CAP * (g - b))
            block = jnp.where((lane >= CAP * g) & (lane < CAP * (g + 1)), piece, block)
        out_ref[ROWS * o : ROWS * (o + 1), :] = block


def unpack_payload(in_ref, owners, slots):
    lane = lax.broadcasted_iota(jnp.int32, (ROWS, LANES), 1)
    columns = []
    for a in range(slots // LANES):
        pieces = []
        for g in range(GROUPS):
            piece = jnp.zeros((ROWS, LANES), F32)
            for b in range(GROUPS):
                o = GROUPS * a + b
                if o < owners:
                    block = roll(in_ref[ROWS * o : ROWS * (o + 1), :], CAP * (b - g))
                    piece = jnp.where((lane >= CAP * b) & (lane < CAP * (b + 1)), block, piece)
            pieces.append(piece)
        columns.append(jnp.concatenate(pieces, axis=0))
    return jnp.concatenate(columns, axis=1)


def call(kernel, outs, *args, in_specs=None, scratch=(), vmem=48, flops=0, nbytes=0, **kw):
    any_spec = pl.BlockSpec(memory_space=pltpu.VMEM)
    return pl.pallas_call(
        kernel,
        out_shape=[jax.ShapeDtypeStruct(s, d) for s, d in outs],
        in_specs=in_specs or [any_spec] * len(args),
        scratch_shapes=list(scratch),
        compiler_params=pltpu.CompilerParams(vmem_limit_bytes=vmem * MIB),
        cost_estimate=pl.CostEstimate(flops=flops, bytes_accessed=nbytes, transcendentals=0),
        **kw,
    )(*args)


HBM = pl.BlockSpec(memory_space=pl.ANY)
VMEM = pl.BlockSpec(memory_space=pltpu.VMEM)


def run(copies):
    for c in copies:
        c.start()
    for c in copies:
        c.wait()


def even(axis):
    return lax.rem(lax.axis_index(axis), 2) == 0


def write_parts(ref, parts, rows):
    for k, x in enumerate(parts):
        ref[rows * k : rows * (k + 1), :] = x[:rows]


def parts_of(ref, rows, vp=None):
    out = [ref[rows * k : rows * (k + 1), :] for k in range(ref.shape[0] // rows)]
    return out if vp is None else [tall(x, vp) for x in out]


def write_pair(axis, first, second, up_parts, down_parts, rows):
    for ref, e, o in ((first, down_parts, up_parts), (second, up_parts, down_parts)):
        write_parts(ref, [jnp.where(even(axis), x, y) for x, y in zip(e, o)], rows)


def read_pair(axis, first, second, rows, vp):
    f, s = parts_of(first, rows, vp), parts_of(second, rows, vp)
    before = [jnp.where(even(axis), y, x) for x, y in zip(f, s)]
    after = [jnp.where(even(axis), x, y) for x, y in zip(f, s)]
    return before, after


def prepare_kernel(vals, vp, mp, state, diff, mask, field, coef, m_1, m_2, rv, rc, sv, sd, sm, dt, mt, sems):
    run([pltpu.make_async_copy(r, t, sems.at[k]) for k, (r, t) in enumerate(((state, sv), (diff, sd), (mask, sm)))])
    half = vals // 2
    copies = []
    for i in range(ROWS):
        copies.append(pltpu.make_async_copy(sv.at[:, i], field.at[i, pl.ds(0, vals)], sems.at[3 + 4 * i]))
        copies.append(pltpu.make_async_copy(sd.at[:, i], dt.at[i, pl.ds(0, vals)], sems.at[4 + 4 * i]))
        copies.append(pltpu.make_async_copy(sm.at[:, i], mt.at[i, pl.ds(0, half)], sems.at[5 + 4 * i]))
        copies.append(pltpu.make_async_copy(sm.at[:, i], mt.at[i, pl.ds(half, half)], sems.at[6 + 4 * i]))
    for c in copies:
        c.start()
    for ref in (field, dt, mt):
        ref[:, vals:, :] = jnp.zeros((ROWS, vp - vals, LANES), ref.dtype)
    for c in copies:
        c.wait()
    for i in range(ROWS):
        coef[i] = dt[i] * mt[i].astype(F32)
    ends = (0, 1, ROWS - 2, ROWS - 1)
    v0, v1, v30, v31 = (field[i] for i in ends)
    c0, c1, c30, c31 = (coef[i] for i in ends)
    p0, p31 = rim_rows(v0, v1, v30, v31, c0, c1, c30, c31)
    write_pair("lat", m_1, m_2, (v0, c0, p0), (v31, c31, p31), mp)
    write_parts(rv, (v0, v31, p0, p31), vp)
    write_parts(rc, (c0, c1, c30, c31), vp)


def sweeps_kernel(vp, field, coef, out, east, west, south, pk, mid):
    lane = lax.broadcasted_iota(jnp.int32, (vp, LANES), 1)
    pv = jnp.zeros((vp, LANES), F32)
    pc = jnp.zeros((vp, LANES), F32)
    for i in range(ROWS):
        c = coef[i]
        e = jnp.where(lane == LANES - 1, 0.0, jnp.minimum(c, roll(c, -1)))
        east[i] = e
        west[i] = roll(e, 1)
        south[i] = jnp.minimum(c, coef[i + 1]) if i < ROWS - 1 else jnp.zeros_like(c)
        here = (lane >> 2) == i
        pv = jnp.where(here, roll(field[i], 4 * i + 2), pv)
        pc = jnp.where(here, roll(c, 4 * i + 2), pc)
    write_parts(pk, (pv, pc, rim_pack(pv, pc)), vp)
    edges = (east, west, south)

    def keep(i, y):
        mid[i] = y

    def split(i, y):
        out[:, LANES * i : LANES * (i + 1)] = stacked(y)

    sweep(field, edges, keep)
    sweep(mid, edges, split)


def lon_kernel(vp, mp, g_1, g_2, coefs, pk, m_1, m_2):
    north, south = read_pair("lat", g_1, g_2, mp, vp)
    if coefs:
        pv, pc, pp = parts_of(pk, vp)
        north, south = north[:2], south[:2]
    else:
        pv, pp = parts_of(pk, vp)
        pc = pv
        north, south = (north[0], north[0]), (south[0], south[0])
    east, west = pack_messages(pv, pc, pp, north, south)
    write_pair("lon", m_1, m_2, (west,), (east,), mp)


def select_kernel(smooth, cells, out, hot):
    chunk = hot.shape[1]
    wide = 4 * LANES
    for base in range(0, cells.shape[1], chunk):
        for k in range(0, ROWS * LANES, wide):
            ids = lax.broadcasted_iota(jnp.int32, (wide, chunk), 0) + k
            hot[k : k + wide, :] = chosen(cells[:, base : base + chunk], ids)
        total = jnp.zeros((smooth.shape[0], chunk), F32)
        for k in range(0, ROWS * LANES, wide):
            total = total + dot(smooth[:, k : k + wide], hot[k : k + wide, :])
        out[:, base : base + chunk] = folded(total)


def weights_kernel(slots, weights, hi, lo):
    s = slots[...]
    place = s + 8 * jnp.floor((s.astype(F32) + 0.5) * (1.0 / (CAP * GROUPS))).astype(jnp.int32)
    row = lax.broadcasted_iota(jnp.int32, hi.shape, 0)
    total = jnp.zeros(hi.shape, F32)
    for k in range(slots.shape[0]):
        total = total + jnp.where(row == place[k : k + 1], weights[k : k + 1, :], 0.0)
    hi[...], lo[...] = halves(total)


def read_ghosts(vp, mp, lat, lon):
    north, south = read_pair("lat", *lat, mp, vp)
    west, east = read_pair("lon", *lon, mp, vp)
    return north, south, ghost_pack(west[0], east[0]), corner_pack(west[0], east[0])


def send_kernel(owners, vp, mp, g_1, g_2, h_1, h_2, rv, rc, pk, inner, cells, out):
    ghosts = read_ghosts(vp, mp, (g_1, g_2), (h_1, h_2))
    v0, v31, p0, p31 = parts_of(rv, vp)
    pv, pc, pp = parts_of(pk, vp)
    fix = rim_correction((v0, v31, p0, p31, pv, pp), parts_of(rc, vp) + [pc], ghosts)
    slots = cells.shape[1]
    total = folded(dot(stacked(jnp.concatenate(fix, axis=1)), chosen(cells[...], rim_ids(slots))))
    pack_payload(inner[...] + total, out, owners)


def owner_kernel(vals, vp, owners, got, w_hi, w_lo, prec, equiv, back, r2, w2, acc):
    step = pl.program_id(0)

    @pl.when(step == 0)
    def _():
        r2[...] = stacked(unpack_payload(got, owners, acc.shape[1]))
        w2[...] = jnp.zeros(w2.shape, F32)
        acc[...] = jnp.zeros(acc.shape, F32)

    hi, lo = w_hi[...], w_lo[...]
    e = folded(dot(r2[...], hi)) + dot(r2[:vp, :], lo)
    equiv[...] = e[:vals]
    w2[:vals, :] = prec[...] * e[:vals]
    w = stacked(w2[...])
    acc[...] += folded(dot_nt(w, hi)) + dot_nt(w[:vp], lo)

    @pl.when(step == pl.num_programs(0) - 1)
    def _():
        pack_payload(acc[...], back, owners)


def back_kernel(owners, vp, mp, got, cells, rc, pk, m_1, m_2, inc, ra, pa):
    slots = cells.shape[1]
    x = stacked(unpack_payload(got, owners, slots))
    inc[...] = x
    rims = folded(dot_nt(x, chosen(cells[...], rim_ids(slots))))
    v0, v1, v30, v31, pv = (rims[:, LANES * k : LANES * (k + 1)] for k in range(5))
    p0, p31 = rim_rows(v0, v1, v30, v31, *parts_of(rc, vp))
    write_pair("lat", m_1, m_2, (v0, p0), (v31, p31), mp)
    write_parts(ra, (v0, v31, p0, p31), vp)
    write_parts(pa, (pv, rim_pack(pv, pk[vp : 2 * vp, :])), vp)


def adjoint_kernel(vp, inc, cells, east, west, south, out, adj):
    wide = 2 * LANES
    slots = cells.shape[1]
    for k in range(ROWS // 2):
        ids = lax.broadcasted_iota(jnp.int32, (wide, slots), 0) + k * wide
        x = folded(dot_nt(inc[...], chosen(cells[...], ids)))
        for j in range(2):
            adj[2 * k + j] = x[:, LANES * j : LANES * (j + 1)]

    def keep(i, y):
        out[i] = y

    sweep(adj, (east, west, south), keep)


def second_kernel(mid, east, west, south, field, out):
    def add(i, y):
        out[i] = y + field[i]

    sweep(mid, (east, west, south), add)


def final_kernel(vals, vp, mp, g_1, g_2, h_1, h_2, a_1, a_2, b_1, b_2, ra, rc, pk, pa, part, out, buf, sems):
    gn, gs, (_, gc, _), (_, kc) = read_ghosts(vp, mp, (g_1, g_2), (h_1, h_2))
    an, az, (gv, _, gp), (kv, _) = read_ghosts(vp, mp, (a_1, a_2), (b_1, b_2))
    ghosts = (an[0], gn[1], an[1]), (az[0], gs[1], az[1]), (gv, gc, gp), (kv, kc)
    v0, v31, p0, p31 = parts_of(ra, vp)
    pv, pp = parts_of(pa, vp)
    r0, r1, r30, r31, fix = rim_correction((v0, v31, p0, p31, pv, pp), parts_of(rc, vp) + [pk[vp : 2 * vp, :]], ghosts)
    lane = lax.broadcasted_iota(jnp.int32, (vp, LANES), 1)
    outer = (lane < 2) | (lane >= LANES - 2)
    copies = []
    for i in range(ROWS):
        x = part[i] + jnp.where(outer, roll(fix, -(4 * i + 2)), 0.0)
        row = {0: r0, 1: r1, ROWS - 2: r30, ROWS - 1: r31}.get(i)
        buf[i] = x if row is None else x + row
        copies.append(pltpu.make_async_copy(buf.at[i, pl.ds(0, vals)], out.at[:, i], sems.at[i]))
        copies[-1].start()
    for c in copies:
        c.wait()


def swap(axis, x, first):
    n = lax.axis_size(axis)
    pairs = []
    for i in range(n):
        j = i + 1 if (i % 2 == 0) == first else i - 1
        if axis == "lon":
            j %= n
        if 0 <= j < n:
            pairs.append((i, j))
    return lax.ppermute(x, axis, pairs)


def exchange(axis, m_1, m_2):
    g_2 = swap(axis, m_2, False)
    g_1 = swap(axis, m_1, True)
    return g_1, g_2


def across(x):
    return lax.all_to_all(x, ("lon", "lat"), split_axis=0, concat_axis=0, tiled=True)


def on_device(state, diffusivity, sea_mask, send_cols, obs_slots, obs_weights, obs_precision):
    vals, taps, obs = state.shape[0], obs_slots.shape[0], obs_slots.shape[1]
    owners = send_cols.shape[1] // CAP
    vp, mp = up(vals, ROWS), up(vals, 8)
    tiles = up(owners, 7 * GROUPS) // GROUPS
    slots = tiles * LANES
    cell_count = ROWS * LANES
    cells = jnp.pad(send_cols, ((0, 0), (0, tiles * GROUPS * CAP - owners * CAP)), constant_values=cell_count)
    cells = jnp.pad(cells.reshape(tiles, GROUPS * CAP), ((0, 0), (0, LANES - GROUPS * CAP)), constant_values=cell_count)
    cells = cells.reshape(1, slots)
    lines = lambda n, rows, dtype=F32: ((n * rows, LANES), dtype)
    field = ((ROWS, vp, LANES), F32)

    whole, coef, *lat_out, rv, rc = call(
        functools.partial(prepare_kernel, vals, vp, mp),
        [field, field, lines(3, mp), lines(3, mp), lines(4, vp), lines(4, vp)],
        state, diffusivity, sea_mask,
        in_specs=[HBM] * 3,
        scratch=[pltpu.VMEM(x.shape, x.dtype) for x in (state, diffusivity, sea_mask)]
        + [pltpu.VMEM((ROWS, vp, LANES), F32), pltpu.VMEM((ROWS, vp, LANES), jnp.int32), pltpu.SemaphoreType.DMA((3 + 4 * ROWS,))],
        vmem=24,
    )
    lat_in = exchange("lat", *lat_out)
    w_hi, w_lo = pl.pallas_call(
        weights_kernel,
        grid=(obs // OBS_BLOCK,),
        out_shape=[jax.ShapeDtypeStruct((slots, obs), BF16)] * 2,
        in_specs=[pl.BlockSpec((taps, OBS_BLOCK), lambda j: (0, j))] * 2,
        out_specs=[pl.BlockSpec((slots, OBS_BLOCK), lambda j: (0, j))] * 2,
        compiler_params=pltpu.CompilerParams(vmem_limit_bytes=40 * MIB),
        cost_estimate=pl.CostEstimate(flops=10 * slots * obs, bytes_accessed=4 * slots * obs, transcendentals=0),
    )(obs_slots, obs_weights)
    split, east, west, south, pk = call(
        functools.partial(sweeps_kernel, vp),
        [((2 * vp, cell_count), BF16), field, field, field, lines(3, vp)],
        whole, coef,
        scratch=[pltpu.VMEM((ROWS, vp, LANES), F32)],
        vmem=24,
        flops=10 * vp * cell_count,
        nbytes=24 * MIB,
    )
    lon_out = call(
        lambda g_1, g_2, *refs: lon_kernel(vp, mp, g_1, g_2, True, *refs),
        [lines(1, mp)] * 2, *lat_in, pk,
        vmem=8,
    )
    lon_in = exchange("lon", *lon_out)
    (inner,) = call(
        select_kernel,
        [((vp, slots), F32)],
        split, cells,
        scratch=[pltpu.VMEM((cell_count, 7 * LANES), BF16)],
        vmem=24,
        flops=4 * vp * cell_count * slots,
        nbytes=8 * MIB,
    )
    (payload,) = call(
        functools.partial(send_kernel, owners, vp, mp),
        [((owners * ROWS, LANES), F32)],
        *lat_in, *lon_in, rv, rc, pk, inner, cells,
        vmem=24,
    )
    payload, w_hi, w_lo = lax.optimization_barrier((payload, w_hi, w_lo))
    received = across(payload)
    wide = min(obs, 1024 if slots <= 1024 else 512)
    equivalents, payload = pl.pallas_call(
        functools.partial(owner_kernel, vals, vp, owners),
        grid=(obs // wide,),
        out_shape=[jax.ShapeDtypeStruct((vals, obs), F32), jax.ShapeDtypeStruct((owners * ROWS, LANES), F32)],
        in_specs=[
            pl.BlockSpec((owners * ROWS, LANES), lambda j: (0, 0)),
            pl.BlockSpec((slots, wide), lambda j: (0, j)),
            pl.BlockSpec((slots, wide), lambda j: (0, j)),
            pl.BlockSpec((vals, wide), lambda j: (0, j)),
        ],
        out_specs=[
            pl.BlockSpec((vals, wide), lambda j: (0, j)),
            pl.BlockSpec((owners * ROWS, LANES), lambda j: (0, 0)),
        ],
        scratch_shapes=[pltpu.VMEM((2 * vp, slots), BF16), pltpu.VMEM((vp, wide), F32), pltpu.VMEM((vp, slots), F32)],
        compiler_params=pltpu.CompilerParams(vmem_limit_bytes=48 * MIB),
    )(received, w_hi, w_lo, obs_precision)
    incoming = across(payload)
    *lat_out, inc, ra, pa = call(
        functools.partial(back_kernel, owners, vp, mp),
        [lines(2, mp)] * 2 + [((2 * vp, slots), BF16), lines(4, vp), lines(2, vp)],
        incoming, cells, rc, pk,
        vmem=24,
    )
    lat_back = exchange("lat", *lat_out)
    (mid,) = call(
        functools.partial(adjoint_kernel, vp),
        [field],
        inc, cells, east, west, south,
        scratch=[pltpu.VMEM((ROWS, vp, LANES), F32)],
        vmem=24,
        flops=4 * vp * cell_count * slots,
        nbytes=10 * MIB,
    )
    lon_out = call(
        lambda g_1, g_2, *refs: lon_kernel(vp, mp, g_1, g_2, False, *refs),
        [lines(1, mp)] * 2, *lat_back, pa,
        vmem=8,
    )
    lon_back = exchange("lon", *lon_out)
    (part,) = call(second_kernel, [field], mid, east, west, south, whole, vmem=24, flops=10 * vp * cell_count, nbytes=16 * MIB)
    (product,) = call(
        functools.partial(final_kernel, vals, vp, mp),
        [(state.shape, F32)],
        *lat_in, *lon_in, *lat_back, *lon_back, ra, rc, pk, pa, part,
        scratch=[pltpu.VMEM((ROWS, vp, LANES), F32), pltpu.SemaphoreType.DMA((ROWS,))],
        out_specs=[HBM],
        vmem=16,
    )
    return product, equivalents


def solution(mesh):
    placed = (
        P(None, "lat", "lon"),
        P(None, "lat", "lon"),
        P(None, "lat", "lon"),
        P(("lon", "lat"), None),
        P(None, ("lon", "lat")),
        P(None, ("lon", "lat")),
        P(None, ("lon", "lat")),
    )
    return jax.shard_map(
        on_device,
        mesh=mesh,
        in_specs=placed,
        out_specs=(P(None, "lat", "lon"), P(None, ("lon", "lat"))),
        check_vma=False,
    )
```

time: 176 us -> 116 us (0.66)
  starting transfers between devices: 57.9 us -> 15.7 us
  Pallas kernels: 79.1 us -> 47 us
  blocking collectives: 18.4 us -> 35.1 us
  waiting for transfers between devices: 7.05 us -> 4.72 us
    ppermute x16 -> x8, starting transfers between devices: 48.9 us -> 15.7 us  [swap(): return lax.ppermute(x, axis, pairs)]
    pallas_call x6 -> x10, Pallas kernels: 59.5 us -> 33.6 us  [call(): pl.pallas_call(kernel, out_shape=[jax.ShapeDtypeStruct(s, d) for s, d in...]
    all_to_all x1 -> x2, blocking collectives: 18.4 us -> 35.1 us  [across(): lax.all_to_all(x, ('lon', 'lat'), split_axis=0, concat_axis=0, tiled=True)]
    all_to_all x1 -> x0, starting transfers between devices: 8.99 us -> none  [across(): lax.all_to_all(x, ('lon', 'lat'), split_axis=0, concat_axis=0, tiled=True)]
    all_to_all x1 -> x0, waiting for transfers between devices: 7.01 us -> none  [across(): lax.all_to_all(x, ('lon', 'lat'), split_axis=0, concat_axis=0, tiled=True)]
    pallas_call x1, Pallas kernels: 13.8 us -> 8.48 us  [on_device(): pl.pallas_call(functools.partial(owner_kernel, vals, vp, owners), grid=(o...]
    ppermute x16 -> x8, waiting for transfers between devices: 0.04 us -> 4.72 us  [swap(): return lax.ppermute(x, axis, pairs)]
    unnamed x40 -> x30, local copies, waits for them, and re-layouts: 10.2 us -> 11.9 us
  transfers between devices with their start and end apart: 17 -> 8, of which waited for: 1 -> 2; matrix products, arithmetic and copies ran while one was open for 0% -> 0% of each run, Pallas kernels for 25% -> 18%
where the time goes in v1:
time: 116 us
  Pallas kernels  47 us (41%)
  blocking collectives  35.1 us (30%)
  starting transfers between devices  15.7 us (14%)
  local copies, waits for them, and re-layouts  12 us (10%)
  waiting for transfers between devices  4.72 us (4%)
    all_to_all x2, blocking collectives, across(): lax.all_to_all(x, ('lon', 'lat'), split_axis=0, concat_axis=0, tiled=True)  35.1 us
    pallas_call x10, Pallas kernels, call(): pl.pallas_call(kernel, out_shape=[jax.ShapeDtypeStruct(s, d) for s, d in...  33.6 us
    ppermute x8, starting transfers between devices, swap(): return lax.ppermute(x, axis, pairs)  15.7 us
    unnamed x30, local copies, waits for them, and re-layouts  11.9 us
    pallas_call x1, Pallas kernels, on_device(): pl.pallas_call(functools.partial(owner_kernel, vals, vp, owners), grid=(o...  8.48 us
    pallas_call x1, Pallas kernels, on_device(): pl.pallas_call(weights_kernel, grid=(obs // OBS_BLOCK,), out_shape=[jax.S...  4.92 us
    ppermute x8, waiting for transfers between devices, swap(): return lax.ppermute(x, axis, pairs)  4.72 us
  transfers between devices with their start and end apart: 8, of which 2 were waited for; matrix products, arithmetic and copies ran while one was open for 0% of the time, Pallas kernels for 18%

profile of v1, /device:TPU:2, one launch (start us, length us, event | category | flops | bytes accessed | tf_op | source)
XLA Modules:
  0.0 115.5 jit_solution(2101845995154967911)
XLA Ops:
  0.6 1.7 %copy-done.5 = f32[150,32,128]{2,1,0:T(8,128)S(1)} copy-done((f32[150,32,128]{2,1,0:T(8,128)S(1)}, f32[150,32,128]{2,1,0:T(8,128)}, u32[]{:S(2)}) %copy-start.5) | copy-done | bytes 2457624
  2.3 1.7 %copy-done.6 = f32[150,32,128]{2,1,0:T(8,128)S(1)} copy-done((f32[150,32,128]{2,1,0:T(8,128)S(1)}, f32[150,32,128]{2,1,0:T(8,128)}, u32[]{:S(2)}) %copy-start.6) | copy-done | bytes 2457624
  5.3 11.2 %shard_map.86 = (f32[32,160,128]{2,1,0:T(8,128)S(1)}, f32[32,160,128]{2,1,0:T(8,128)S(1)}, f32[456,128]{1,0:T(8,128)}, f32[456,128]{1,0:T(8,128)}, f32[640,128]{1,0:T(8,128)S(1)}, /*index=5*/f32[640,128]{1,0:T(8,128)S(1)}) custom-call(f32[150,32,128]{2,1,0:T(8,128)S(1)} %copy-done.5, f32[150,32,128]{2,1,0:T(8,128)S(1)} %copy-done.6, s32[75,32,128]{2,1,0:T(8,128)S(1)} %copy-done.8), custom_call_target="tpu_custom_call" | custom-call | tf_op jit(solution)/shard_map/pallas_call | solution.py:201
  16.6 1.5 %copy-done.3 = f32[32,160,128]{2,1,0:T(8,128)} copy-done((f32[32,160,128]{2,1,0:T(8,128)}, f32[32,160,128]{2,1,0:T(8,128)S(1)}, u32[]{:S(2)}) %copy-start.3) | copy-done | bytes 2621464
  18.8 5.1 %collective-permute-start.1 = (f32[456,128]{1,0:T(8,128)}, f32[456,128]{1,0:T(8,128)S(1)}, u32[]{:S(2)}, u32[]{:S(2)}) collective-permute-start(f32[456,128]{1,0:T(8,128)} %get-tuple-element.30), channel_id=1, source_target_pairs={{1,2},{2,1},{5,6},{6,5},{9,10},{10,9},{13,14},{14,13},{17,18},{18,... | collective-permute-start | bytes 700424 | tf_op jit(solution)/shard_map/ppermute | solution.py:437
  24.0 1.7 %copy-done.4 = f32[32,160,128]{2,1,0:T(8,128)S(1)} copy-done((f32[32,160,128]{2,1,0:T(8,128)S(1)}, f32[32,160,128]{2,1,0:T(8,128)}, u32[]{:S(2)}) %copy-start.4) | copy-done | bytes 2621464
  25.7 8.3 %shard_map.87 = (bf16[320,4096]{1,0:T(8,128)(2,1)S(1)}, f32[32,160,128]{2,1,0:T(8,128)S(1)}, f32[32,160,128]{2,1,0:T(8,128)S(1)}, f32[32,160,128]{2,1,0:T(8,128)S(1)}, f32[480,128]{1,0:T(8,128)S(1)}) custom-call(f32[32,160,128]{2,1,0:T(8,128)S(1)} %get-tuple-element.31.field, f32[32,160,128]{2,1,0:T(8,128)S(1)} %copy-done.4), custom_call_target="tpu_custom_call" | custom-call | flops 6553600 | bytes 25165824 | tf_op jit(solution)/shard_map/pallas_call | solution.py:201
  34.0 1.5 %copy-done = f32[32,160,128]{2,1,0:T(8,128)} copy-done((f32[32,160,128]{2,1,0:T(8,128)}, f32[32,160,128]{2,1,0:T(8,128)S(1)}, u32[]{:S(2)}) %copy-start) | copy-done | bytes 2621464
  35.9 3.7 %collective-permute-start.3 = (f32[152,128]{1,0:T(8,128)S(1)}, f32[152,128]{1,0:T(8,128)S(1)}, u32[]{:S(2)}, u32[]{:S(2)}) collective-permute-start(f32[152,128]{1,0:T(8,128)S(1)} %get-tuple-element.35), channel_id=1, source_target_pairs={{0,28},{4,8},{8,4},{12,16},{16,12},{20,24},{24,20},{28,0},{1,29},{... | collective-permute-start | bytes 233480 | tf_op jit(solution)/shard_map/ppermute | solution.py:437
  39.6 2.9 %shard_map.89.inner = f32[160,896]{1,0:T(8,128)S(1)} custom-call(bf16[320,4096]{1,0:T(8,128)(2,1)S(1)} %get-tuple-element.38.smooth, s32[1,896]{1,0:T(1,128)S(1)} %bitcast.14), custom_call_target="tpu_custom_call" | custom-call | flops 2348810240 | bytes 8388608 | tf_op jit(solution)/shard_map/pallas_call | solution.py:201
  42.6 4.9 %shard_map.91 = (bf16[896,2048]{1,0:T(8,128)(2,1)S(1)}, bf16[896,2048]{1,0:T(8,128)(2,1)S(1)}) custom-call(s32[4,2048]{1,0:T(4,128)S(1)} %copy-done.11, f32[4,2048]{1,0:T(4,128)S(1)} %copy-done.12), custom_call_target="tpu_custom_call" | custom-call | flops 18350080 | bytes 7340032 | tf_op jit(solution)/shard_map/pallas_call | solution.py:473
  47.5 1.8 %copy-done.2 = bf16[896,2048]{1,0:T(8,128)(2,1)} copy-done((bf16[896,2048]{1,0:T(8,128)(2,1)}, bf16[896,2048]{1,0:T(8,128)(2,1)S(1)}, u32[]{:S(2)}) %copy-start.2) | copy-done | bytes 3670040
  49.3 1.9 %shard_map.90 = f32[1024,128]{1,0:T(8,128)S(1)} custom-call(f32[456,128]{1,0:T(8,128)S(1)} %collective-permute-done.g_1, f32[456,128]{1,0:T(8,128)S(1)} %collective-permute-done.1.g_2, f32[152,128]{1,0:T(8,128)S(1)} %collective-permute-done.2.h_1, f32[152,128]{1,0:T(8,128)S(1)} %collective-permute-done.3.h_2, f32[640,128]{1,0:T(8,128)S(1)} %copy-done.10, ...), custom_call_target="tpu_custom_call" | custom-call | tf_op jit(solution)/shard_map/pallas_call | solution.py:201
  51.2 16.6 %all_to_all.22 = f32[32,32,128]{2,1,0:T(8,128)S(1)} all-to-all(f32[32,32,128]{2,1,0:T(8,128)S(1)} %bitcast.12), channel_id=1, replica_groups=mesh['lon'=8,'lat'=4] {'lon','lat'}, dimensions={0} | all-to-all | bytes 1048576 | tf_op jit(solution)/shard_map/all_to_all | solution.py:447
  67.8 8.5 %shard_map.92 = (f32[150,2048]{1,0:T(8,128)}, f32[1024,128]{1,0:T(8,128)S(1)}) custom-call(f32[1024,128]{1,0:T(8,128)S(1)} %bitcast.10, bf16[896,2048]{1,0:T(8,128)(2,1)S(1)} %get-tuple-element.42.w_hi, bf16[896,2048]{1,0:T(8,128)(2,1)} %copy-done.2, f32[150,2048]{1,0:T(8,128)S(1)} %copy-done.7), custom_call_target="tpu_custom_call" | custom-call | tf_op jit(solution)/shard_map/pallas_call | solution.py:515
  76.3 18.4 %all_to_all.23 = f32[32,32,128]{2,1,0:T(8,128)S(1)} all-to-all(f32[32,32,128]{2,1,0:T(8,128)S(1)} %bitcast.13), channel_id=1, replica_groups=mesh['lon'=8,'lat'=4] {'lon','lat'}, dimensions={0} | all-to-all | bytes 1048576 | tf_op jit(solution)/shard_map/all_to_all | solution.py:447
  94.7 1.3 %shard_map.93 = (f32[304,128]{1,0:T(8,128)S(1)}, f32[304,128]{1,0:T(8,128)S(1)}, bf16[320,896]{1,0:T(8,128)(2,1)S(1)}, f32[640,128]{1,0:T(8,128)S(1)}, f32[320,128]{1,0:T(8,128)S(1)}) custom-call(f32[1024,128]{1,0:T(8,128)S(1)} %bitcast.11, s32[1,896]{1,0:T(1,128)S(1)} %bitcast.16, f32[640,128]{1,0:T(8,128)S(1)} %get-tuple-element.37.rc, ...), custom_call_target="tpu_custom_call" | custom-call | tf_op jit(solution)/shard_map/pallas_call | solution.py:201
  96.0 1.9 %collective-permute-start.4 = (f32[304,128]{1,0:T(8,128)S(1)}, f32[304,128]{1,0:T(8,128)S(1)}, u32[]{:S(2)}, u32[]{:S(2)}) collective-permute-start(f32[304,128]{1,0:T(8,128)S(1)} %get-tuple-element.45), channel_id=1, source_target_pairs={{0,1},{1,0},{2,3},{3,2},{4,5},{5,4},{6,7},{7,6},{8,9},{9,8},{10,11... | collective-permute-start | bytes 466952 | tf_op jit(solution)/shard_map/ppermute | solution.py:437
  97.9 3.3 %collective-permute-start.5 = (f32[304,128]{1,0:T(8,128)S(1)}, f32[304,128]{1,0:T(8,128)S(1)}, u32[]{:S(2)}, u32[]{:S(2)}) collective-permute-start(f32[304,128]{1,0:T(8,128)S(1)} %get-tuple-element.46), channel_id=1, source_target_pairs={{1,2},{2,1},{5,6},{6,5},{9,10},{10,9},{13,14},{14,13},{17,18},{18,... | collective-permute-start | bytes 466952 | tf_op jit(solution)/shard_map/ppermute | solution.py:437
  101.8 4.1 %collective-permute-done.5.g_2.a_2 = f32[304,128]{1,0:T(8,128)S(1)} collective-permute-done((f32[304,128]{1,0:T(8,128)S(1)}, f32[304,128]{1,0:T(8,128)S(1)}, u32[]{:S(2)}, u32[]{:S(2)}) %collective-permute-start.5) | collective-permute-done | bytes 155680 | tf_op jit(solution)/shard_map/ppermute | solution.py:437
  106.3 1.6 %collective-permute-start.7 = (f32[152,128]{1,0:T(8,128)S(1)}, f32[152,128]{1,0:T(8,128)S(1)}, u32[]{:S(2)}, u32[]{:S(2)}) collective-permute-start(f32[152,128]{1,0:T(8,128)S(1)} %get-tuple-element.49), channel_id=1, source_target_pairs={{0,28},{4,8},{8,4},{12,16},{16,12},{20,24},{24,20},{28,0},{1,29},{... | collective-permute-start | bytes 233480 | tf_op jit(solution)/shard_map/ppermute | solution.py:437
  107.9 3.1 %shard_map.95.mid = f32[32,160,128]{2,1,0:T(8,128)S(1)} custom-call(bf16[320,896]{1,0:T(8,128)(2,1)S(1)} %get-tuple-element.51.inc, s32[1,896]{1,0:T(1,128)S(1)} %bitcast.17, f32[32,160,128]{2,1,0:T(8,128)S(1)} %get-tuple-element.52.east, f32[32,160,128]{2,1,0:T(8,128)S(1)} %get-tuple-element.53.west, f32[32,160,128]{2,1,0:T(8,128)S(1)} %copy-done.1), custom_call_target="tpu_custom_call" | custom-call | flops 2348810240 | bytes 10485760 | tf_op jit(solution)/shard_map/pallas_call | solution.py:201
  111.0 1.5 %shard_map.96.part = f32[32,160,128]{2,1,0:T(8,128)S(1)} custom-call(f32[32,160,128]{2,1,0:T(8,128)S(1)} %shard_map.95.mid, f32[32,160,128]{2,1,0:T(8,128)S(1)} %get-tuple-element.52.east, f32[32,160,128]{2,1,0:T(8,128)S(1)} %get-tuple-element.53.west, f32[32,160,128]{2,1,0:T(8,128)S(1)} %copy-done.1, f32[32,160,128]{2,1,0:T(8,128)S(1)} %get-tuple-element.31.field), custom_call_target="tpu_custom_call" | custom-call | flops 6553600 | bytes 16777216 | tf_op jit(solution)/shard_map/pallas_call | solution.py:201
  112.6 2.8 %shard_map.97 = f32[150,32,128]{2,1,0:T(8,128)} custom-call(f32[456,128]{1,0:T(8,128)S(1)} %collective-permute-done.g_1, f32[456,128]{1,0:T(8,128)S(1)} %collective-permute-done.1.g_2, f32[152,128]{1,0:T(8,128)S(1)} %collective-permute-done.2.h_1, f32[152,128]{1,0:T(8,128)S(1)} %collective-permute-done.3.h_2, f32[304,128]{1,0:T(8,128)S(1)} %collective-permute-done.4.g_1.a_1, ...), custom_call_target="tpu_custom_call" | custom-call | tf_op jit(solution)/shard_map/pallas_call | solution.py:201
  (38 shorter events, 3.5 us)
Async XLA Ops:
  0.6 1.7 %copy-start.5 = (f32[150,32,128]{2,1,0:T(8,128)S(1)}, f32[150,32,128]{2,1,0:T(8,128)}, u32[]{:S(2)}) copy-start(f32[150,32,128]{2,1,0:T(8,128)} %state.1) | copy-start | bytes 7372804
  2.3 1.7 %copy-start.6 = (f32[150,32,128]{2,1,0:T(8,128)S(1)}, f32[150,32,128]{2,1,0:T(8,128)}, u32[]{:S(2)}) copy-start(f32[150,32,128]{2,1,0:T(8,128)} %diff.1) | copy-start | bytes 7372804
  4.0 1.3 %copy-start.8 = (s32[75,32,128]{2,1,0:T(8,128)S(1)}, s32[75,32,128]{2,1,0:T(8,128)}, u32[]{:S(2)}) copy-start(s32[75,32,128]{2,1,0:T(8,128)} %mask.1) | copy-start | bytes 3686404
  5.3 18.5 %copy-start.13 = (s32[1,768]{1,0:T(1,128)S(1)}, s32[1,768]{1,0:T(1,128)}, u32[]{:S(2)}) copy-start(s32[1,768]{1,0:T(1,128)} %param.10) | copy-start | bytes 9220
  16.6 1.5 %copy-start.3 = (f32[32,160,128]{2,1,0:T(8,128)}, f32[32,160,128]{2,1,0:T(8,128)S(1)}, u32[]{:S(2)}) copy-start(f32[32,160,128]{2,1,0:T(8,128)S(1)} %get-tuple-element.32.coef) | copy-start | bytes 7864324
  18.1 0.7 copy-start.9
  18.8 16.7 %collective-permute-start = (f32[456,128]{1,0:T(8,128)}, f32[456,128]{1,0:T(8,128)S(1)}, u32[]{:S(2)}, u32[]{:S(2)}) collective-permute-start(f32[456,128]{1,0:T(8,128)} %get-tuple-element.29), channel_id=1, source_target_pairs={{0,1},{1,0},{2,3},{3,2},{4,5},{5,4},{6,7},{7,6},{8,9},{9,8},{10,11... | collective-permute-start | bytes 700424 | tf_op jit(solution)/shard_map/ppermute | solution.py:437
  18.8 16.7 %collective-permute-start.1 = (f32[456,128]{1,0:T(8,128)}, f32[456,128]{1,0:T(8,128)S(1)}, u32[]{:S(2)}, u32[]{:S(2)}) collective-permute-start(f32[456,128]{1,0:T(8,128)} %get-tuple-element.30), channel_id=1, source_target_pairs={{1,2},{2,1},{5,6},{6,5},{9,10},{10,9},{13,14},{14,13},{17,18},{18,... | collective-permute-start | bytes 700424 | tf_op jit(solution)/shard_map/ppermute | solution.py:437
  24.0 1.7 %copy-start.4 = (f32[32,160,128]{2,1,0:T(8,128)S(1)}, f32[32,160,128]{2,1,0:T(8,128)}, u32[]{:S(2)}) copy-start(f32[32,160,128]{2,1,0:T(8,128)} %copy-done.3) | copy-start | bytes 7864324
  34.0 1.5 %copy-start = (f32[32,160,128]{2,1,0:T(8,128)}, f32[32,160,128]{2,1,0:T(8,128)S(1)}, u32[]{:S(2)}) copy-start(f32[32,160,128]{2,1,0:T(8,128)S(1)} %get-tuple-element.54.south) | copy-start | bytes 7864324
  35.8 13.4 %collective-permute-start.2 = (f32[152,128]{1,0:T(8,128)S(1)}, f32[152,128]{1,0:T(8,128)S(1)}, u32[]{:S(2)}, u32[]{:S(2)}) collective-permute-start(f32[152,128]{1,0:T(8,128)S(1)} %get-tuple-element.34), channel_id=1, source_target_pairs={{0,4},{4,0},{8,12},{12,8},{16,20},{20,16},{24,28},{28,24},{1,5},{5... | collective-permute-start | bytes 233480 | tf_op jit(solution)/shard_map/ppermute | solution.py:437
  35.9 13.4 %collective-permute-start.3 = (f32[152,128]{1,0:T(8,128)S(1)}, f32[152,128]{1,0:T(8,128)S(1)}, u32[]{:S(2)}, u32[]{:S(2)}) collective-permute-start(f32[152,128]{1,0:T(8,128)S(1)} %get-tuple-element.35), channel_id=1, source_target_pairs={{0,28},{4,8},{8,4},{12,16},{16,12},{20,24},{24,20},{28,0},{1,29},{... | collective-permute-start | bytes 233480 | tf_op jit(solution)/shard_map/ppermute | solution.py:437
  39.6 2.9 %copy-start.11 = (s32[4,2048]{1,0:T(4,128)S(1)}, s32[4,2048]{1,0:T(4,128)}, u32[]{:S(2)}) copy-start(s32[4,2048]{1,0:T(4,128)} %slots.1) | copy-start | bytes 98308
  39.6 2.9 %copy-start.12 = (f32[4,2048]{1,0:T(4,128)S(1)}, f32[4,2048]{1,0:T(4,128)}, u32[]{:S(2)}) copy-start(f32[4,2048]{1,0:T(4,128)} %weights.1) | copy-start | bytes 98308
  39.6 9.7 %copy-start.10 = (f32[640,128]{1,0:T(8,128)S(1)}, f32[640,128]{1,0:T(8,128)}, u32[]{:S(2)}) copy-start(f32[640,128]{1,0:T(8,128)} %copy-done.9) | copy-start | bytes 983044
  42.5 25.3 %copy-start.7 = (f32[150,2048]{1,0:T(8,128)S(1)}, f32[150,2048]{1,0:T(8,128)}, u32[]{:S(2)}) copy-start(f32[150,2048]{1,0:T(8,128)} %prec.1) | copy-start | bytes 3686404
  47.5 1.8 %copy-start.2 = (bf16[896,2048]{1,0:T(8,128)(2,1)}, bf16[896,2048]{1,0:T(8,128)(2,1)S(1)}, u32[]{:S(2)}) copy-start(bf16[896,2048]{1,0:T(8,128)(2,1)S(1)} %get-tuple-element.43.w_lo) | copy-start | bytes 11010052
  76.3 31.6 %copy-start.1 = (f32[32,160,128]{2,1,0:T(8,128)S(1)}, f32[32,160,128]{2,1,0:T(8,128)}, u32[]{:S(2)}) copy-start(f32[32,160,128]{2,1,0:T(8,128)} %copy-done) | copy-start | bytes 7864324
  96.0 5.8 %collective-permute-start.4 = (f32[304,128]{1,0:T(8,128)S(1)}, f32[304,128]{1,0:T(8,128)S(1)}, u32[]{:S(2)}, u32[]{:S(2)}) collective-permute-start(f32[304,128]{1,0:T(8,128)S(1)} %get-tuple-element.45), channel_id=1, source_target_pairs={{0,1},{1,0},{2,3},{3,2},{4,5},{5,4},{6,7},{7,6},{8,9},{9,8},{10,11... | collective-permute-start | bytes 466952 | tf_op jit(solution)/shard_map/ppermute | solution.py:437
  97.9 8.0 %collective-permute-start.5 = (f32[304,128]{1,0:T(8,128)S(1)}, f32[304,128]{1,0:T(8,128)S(1)}, u32[]{:S(2)}, u32[]{:S(2)}) collective-permute-start(f32[304,128]{1,0:T(8,128)S(1)} %get-tuple-element.46), channel_id=1, source_target_pairs={{1,2},{2,1},{5,6},{6,5},{9,10},{10,9},{13,14},{14,13},{17,18},{18,... | collective-permute-start | bytes 466952 | tf_op jit(solution)/shard_map/ppermute | solution.py:437
  106.2 6.3 %collective-permute-start.6 = (f32[152,128]{1,0:T(8,128)S(1)}, f32[152,128]{1,0:T(8,128)S(1)}, u32[]{:S(2)}, u32[]{:S(2)}) collective-permute-start(f32[152,128]{1,0:T(8,128)S(1)} %get-tuple-element.48), channel_id=1, source_target_pairs={{0,4},{4,0},{8,12},{12,8},{16,20},{20,16},{24,28},{28,24},{1,5},{5... | collective-permute-start | bytes 233480 | tf_op jit(solution)/shard_map/ppermute | solution.py:437
  106.3 6.3 %collective-permute-start.7 = (f32[152,128]{1,0:T(8,128)S(1)}, f32[152,128]{1,0:T(8,128)S(1)}, u32[]{:S(2)}, u32[]{:S(2)}) collective-permute-start(f32[152,128]{1,0:T(8,128)S(1)} %get-tuple-element.49), channel_id=1, source_target_pairs={{0,28},{4,8},{8,4},{12,16},{16,12},{20,24},{24,20},{28,0},{1,29},{... | collective-permute-start | bytes 233480 | tf_op jit(solution)/shard_map/ppermute | solution.py:437

commit v2 on v1

--- a/solution.py
+++ b/solution.py
@@ -168,10 +168,10 @@
     return jnp.concatenate(rows + [pack], axis=0)
 
 
-def pack_payload(x, out_ref, owners):
+def pack_payload(x, out_ref, first, last):
     lane = lax.broadcasted_iota(jnp.int32, (ROWS, LANES), 1)
-    for o in range(owners):
-        a, b = divmod(o, GROUPS)
+    for o in range(first, last):
+        a, b = divmod(o - first, GROUPS)
         block = jnp.zeros((ROWS, LANES), F32)
         for g in range(GROUPS):
             piece = roll(x[ROWS * g : ROWS * (g + 1), LANES * a : LANES * (a + 1)], CAP * (g - b))
@@ -196,7 +196,11 @@
     return jnp.concatenate(columns, axis=1)
 
 
-def call(kernel, outs, *args, in_specs=None, scratch=(), vmem=48, flops=0, nbytes=0, **kw):
+def takes(us):
+    return pl.CostEstimate(flops=MIB, bytes_accessed=int(us * 3.3e6), transcendentals=0)
+
+
+def call(kernel, outs, *args, in_specs=None, scratch=(), vmem=48, us=1, **kw):
     any_spec = pl.BlockSpec(memory_space=pltpu.VMEM)
     return pl.pallas_call(
         kernel,
@@ -204,20 +208,13 @@
         in_specs=in_specs or [any_spec] * len(args),
         scratch_shapes=list(scratch),
         compiler_params=pltpu.CompilerParams(vmem_limit_bytes=vmem * MIB),
-        cost_estimate=pl.CostEstimate(flops=flops, bytes_accessed=nbytes, transcendentals=0),
+        cost_estimate=takes(us),
         **kw,
     )(*args)
 
 
 HBM = pl.BlockSpec(memory_space=pl.ANY)
 VMEM = pl.BlockSpec(memory_space=pltpu.VMEM)
-
-
-def run(copies):
-    for c in copies:
-        c.start()
-    for c in copies:
-        c.wait()
 
 
 def even(axis):
@@ -246,45 +243,83 @@
     return before, after
 
 
-def prepare_kernel(vals, vp, mp, state, diff, mask, field, coef, m_1, m_2, rv, rc, sv, sd, sm, dt, mt, sems):
-    run([pltpu.make_async_copy(r, t, sems.at[k]) for k, (r, t) in enumerate(((state, sv), (diff, sd), (mask, sm)))])
+def start_loads(vals, state, diff, mask, sv, sd, sm, sems, rows):
     half = vals // 2
     copies = []
-    for i in range(ROWS):
-        copies.append(pltpu.make_async_copy(sv.at[:, i], field.at[i, pl.ds(0, vals)], sems.at[3 + 4 * i]))
-        copies.append(pltpu.make_async_copy(sd.at[:, i], dt.at[i, pl.ds(0, vals)], sems.at[4 + 4 * i]))
-        copies.append(pltpu.make_async_copy(sm.at[:, i], mt.at[i, pl.ds(0, half)], sems.at[5 + 4 * i]))
-        copies.append(pltpu.make_async_copy(sm.at[:, i], mt.at[i, pl.ds(half, half)], sems.at[6 + 4 * i]))
-    for c in copies:
-        c.start()
-    for ref in (field, dt, mt):
-        ref[:, vals:, :] = jnp.zeros((ROWS, vp - vals, LANES), ref.dtype)
-    for c in copies:
+    for k, i in enumerate(rows):
+        for src, dst in (
+            (state, sv.at[k, pl.ds(0, vals)]),
+            (diff, sd.at[k, pl.ds(0, vals)]),
+            (mask, sm.at[k, pl.ds(0, half)]),
+            (mask, sm.at[k, pl.ds(half, half)]),
+        ):
+            copies.append(pltpu.make_async_copy(src.at[:, i], dst, sems.at[len(copies)]))
+            copies[-1].start()
+    for ref in (sv, sd, sm):
+        ref[:, vals:, :] = jnp.zeros((ref.shape[0], ref.shape[1] - vals, LANES), ref.dtype)
+    return copies
+
+
+ENDS = (0, 1, ROWS - 2, ROWS - 1)
+
+
+def rows_kernel(vals, vp, mp, state, diff, mask, m_1, m_2, rv, rc, done, sv, sd, sm, sems):
+    done[...] = jnp.zeros(done.shape, F32)
+    for c in start_loads(vals, state, diff, mask, sv, sd, sm, sems, ENDS):
         c.wait()
-    for i in range(ROWS):
-        coef[i] = dt[i] * mt[i].astype(F32)
-    ends = (0, 1, ROWS - 2, ROWS - 1)
-    v0, v1, v30, v31 = (field[i] for i in ends)
-    c0, c1, c30, c31 = (coef[i] for i in ends)
+    v0, v1, v30, v31 = (sv[k] for k in range(4))
+    c0, c1, c30, c31 = (sd[k] * sm[k].astype(F32) for k in range(4))
     p0, p31 = rim_rows(v0, v1, v30, v31, c0, c1, c30, c31)
     write_pair("lat", m_1, m_2, (v0, c0, p0), (v31, c31, p31), mp)
     write_parts(rv, (v0, v31, p0, p31), vp)
     write_parts(rc, (c0, c1, c30, c31), vp)
 
 
-def sweeps_kernel(vp, field, coef, out, east, west, south, pk, mid):
+def by_grid_row(x, dst, first):
+    n = x.shape[0]
+    if n < 8:
+        x = jnp.concatenate([x, jnp.zeros((8 - n, *x.shape[1:]), x.dtype)], axis=0)
+    y = jnp.swapaxes(x, 0, 1)
+    v, i = first
+    for k in range(8):
+        dst[i + k, v : v + 8, :] = y[k]
+
+
+def sweeps_kernel(vals, vp, state, diff, mask, after, field, out, east, west, south, pk, coef, mid):
+    half = vals // 2
+    for v in range(0, vp, 8):
+        if v >= vals:
+            for ref in (field, coef):
+                ref[:, v : v + 8, :] = jnp.zeros((ROWS, 8, LANES), F32)
+            continue
+        end = min(v + 8, vals)
+        for i in range(0, ROWS, 8):
+            rows = slice(i, i + 8)
+            if end <= half:
+                m = mask[v:end, rows, :]
+            elif v >= half:
+                m = mask[v - half : end - half, rows, :]
+            else:
+                m = jnp.concatenate([mask[v:half, rows, :], mask[: end - half, rows, :]], axis=0)
+            by_grid_row(state[v:end, rows, :], field, (v, i))
+            by_grid_row(diff[v:end, rows, :] * m.astype(F32), coef, (v, i))
     lane = lax.broadcasted_iota(jnp.int32, (vp, LANES), 1)
     pv = jnp.zeros((vp, LANES), F32)
     pc = jnp.zeros((vp, LANES), F32)
+    c = coef[0]
     for i in range(ROWS):
-        c = coef[i]
+        if i < ROWS - 1:
+            cn = coef[i + 1]
+            south[i] = jnp.minimum(c, cn)
+        else:
+            south[i] = jnp.zeros_like(c)
         e = jnp.where(lane == LANES - 1, 0.0, jnp.minimum(c, roll(c, -1)))
         east[i] = e
         west[i] = roll(e, 1)
-        south[i] = jnp.minimum(c, coef[i + 1]) if i < ROWS - 1 else jnp.zeros_like(c)
         here = (lane >> 2) == i
         pv = jnp.where(here, roll(field[i], 4 * i + 2), pv)
         pc = jnp.where(here, roll(c, 4 * i + 2), pc)
+        c = cn
     write_parts(pk, (pv, pc, rim_pack(pv, pc)), vp)
     edges = (east, west, south)
 
@@ -327,11 +362,25 @@
 def weights_kernel(slots, weights, hi, lo):
     s = slots[...]
     place = s + 8 * jnp.floor((s.astype(F32) + 0.5) * (1.0 / (CAP * GROUPS))).astype(jnp.int32)
-    row = lax.broadcasted_iota(jnp.int32, hi.shape, 0)
-    total = jnp.zeros(hi.shape, F32)
-    for k in range(slots.shape[0]):
-        total = total + jnp.where(row == place[k : k + 1], weights[k : k + 1, :], 0.0)
-    hi[...], lo[...] = halves(total)
+    taps = range(slots.shape[0])
+    at = [place[k : k + 1] for k in taps]
+    w = [weights[k : k + 1, :] for k in taps]
+    for a in taps:
+        for b in range(a + 1, len(taps)):
+            same = at[a] == at[b]
+            w[a] = w[a] + jnp.where(same, w[b], 0.0)
+            at[b] = jnp.where(same, -1, at[b])
+    at = [x.astype(jnp.int16) for x in at]
+    parts = [halves(x) for x in w]
+    shape = (LANES, hi.shape[1])
+    for r in range(0, hi.shape[0], LANES):
+        row = (lax.broadcasted_iota(jnp.int32, shape, 0) + r).astype(jnp.int16)
+        h = l = jnp.zeros(shape, BF16)
+        for k in taps:
+            here = row == at[k]
+            h, l = jnp.where(here, parts[k][0], h), jnp.where(here, parts[k][1], l)
+        hi[r : r + LANES, :] = h
+        lo[r : r + LANES, :] = l
 
 
 def read_ghosts(vp, mp, lat, lon):
@@ -347,28 +396,22 @@
     fix = rim_correction((v0, v31, p0, p31, pv, pp), parts_of(rc, vp) + [pc], ghosts)
     slots = cells.shape[1]
     total = folded(dot(stacked(jnp.concatenate(fix, axis=1)), chosen(cells[...], rim_ids(slots))))
-    pack_payload(inner[...] + total, out, owners)
-
-
-def owner_kernel(vals, vp, owners, got, w_hi, w_lo, prec, equiv, back, r2, w2, acc):
-    step = pl.program_id(0)
-
-    @pl.when(step == 0)
-    def _():
-        r2[...] = stacked(unpack_payload(got, owners, acc.shape[1]))
-        w2[...] = jnp.zeros(w2.shape, F32)
-        acc[...] = jnp.zeros(acc.shape, F32)
-
-    hi, lo = w_hi[...], w_lo[...]
-    e = folded(dot(r2[...], hi)) + dot(r2[:vp, :], lo)
-    equiv[...] = e[:vals]
-    w2[:vals, :] = prec[...] * e[:vals]
-    w = stacked(w2[...])
-    acc[...] += folded(dot_nt(w, hi)) + dot_nt(w[:vp], lo)
-
-    @pl.when(step == pl.num_programs(0) - 1)
-    def _():
-        pack_payload(acc[...], back, owners)
+    pack_payload(inner[...] + total, out, 0, owners)
+
+
+def owner_kernel(vals, vp, owners, got, w_hi, w_lo, prec, equiv, back, r2, w2):
+    r2[...] = stacked(unpack_payload(got, owners, r2.shape[1]))
+    wide = min(512, equiv.shape[1])
+    for q in range(0, equiv.shape[1], wide):
+        at = slice(q, q + wide)
+        e = (folded(dot(r2[...], w_hi[:, at])) + dot(r2[:vp, :], w_lo[:, at]))[:vals]
+        equiv[:, at] = e
+        w2[:, at] = stacked(tall(prec[:, at] * e, vp))
+    for o in range(0, r2.shape[1], 7 * LANES):
+        at = slice(o, o + 7 * LANES)
+        x = folded(dot_nt(w2[...], w_hi[at, :])) + dot_nt(w2[:vp, :], w_lo[at, :])
+        n = 7 * GROUPS * (o // (7 * LANES))
+        pack_payload(x, back, n, min(owners, n + 7 * GROUPS))
 
 
 def back_kernel(owners, vp, mp, got, cells, rc, pk, m_1, m_2, inc, ra, pa):
@@ -460,33 +503,38 @@
     lines = lambda n, rows, dtype=F32: ((n * rows, LANES), dtype)
     field = ((ROWS, vp, LANES), F32)
 
-    whole, coef, *lat_out, rv, rc = call(
-        functools.partial(prepare_kernel, vals, vp, mp),
-        [field, field, lines(3, mp), lines(3, mp), lines(4, vp), lines(4, vp)],
+    def loads(n):
+        block = (n, vp, LANES)
+        return [pltpu.VMEM(block, F32), pltpu.VMEM(block, F32), pltpu.VMEM(block, jnp.int32), pltpu.SemaphoreType.DMA((4 * n,))]
+
+    *lat_out, rv, rc, done = call(
+        functools.partial(rows_kernel, vals, vp, mp),
+        [lines(3, mp), lines(3, mp), lines(4, vp), lines(4, vp), lines(1, 8)],
         state, diffusivity, sea_mask,
         in_specs=[HBM] * 3,
-        scratch=[pltpu.VMEM(x.shape, x.dtype) for x in (state, diffusivity, sea_mask)]
-        + [pltpu.VMEM((ROWS, vp, LANES), F32), pltpu.VMEM((ROWS, vp, LANES), jnp.int32), pltpu.SemaphoreType.DMA((3 + 4 * ROWS,))],
-        vmem=24,
+        scratch=loads(len(ENDS)),
+        vmem=62,
     )
     lat_in = exchange("lat", *lat_out)
+    wide = min(obs, 1024 if slots <= 1024 else 512)
+    obs_weights, done = lax.optimization_barrier((obs_weights, done))
     w_hi, w_lo = pl.pallas_call(
         weights_kernel,
-        grid=(obs // OBS_BLOCK,),
+        grid=(obs // wide,),
         out_shape=[jax.ShapeDtypeStruct((slots, obs), BF16)] * 2,
-        in_specs=[pl.BlockSpec((taps, OBS_BLOCK), lambda j: (0, j))] * 2,
-        out_specs=[pl.BlockSpec((slots, OBS_BLOCK), lambda j: (0, j))] * 2,
-        compiler_params=pltpu.CompilerParams(vmem_limit_bytes=40 * MIB),
-        cost_estimate=pl.CostEstimate(flops=10 * slots * obs, bytes_accessed=4 * slots * obs, transcendentals=0),
+        in_specs=[pl.BlockSpec((taps, wide), lambda j: (0, j))] * 2,
+        out_specs=[pl.BlockSpec((slots, wide), lambda j: (0, j))] * 2,
+        compiler_params=pltpu.CompilerParams(vmem_limit_bytes=20 * MIB),
+        cost_estimate=pl.CostEstimate(flops=int(4e9), bytes_accessed=int(80e6), transcendentals=0),
     )(obs_slots, obs_weights)
-    split, east, west, south, pk = call(
-        functools.partial(sweeps_kernel, vp),
-        [((2 * vp, cell_count), BF16), field, field, field, lines(3, vp)],
-        whole, coef,
-        scratch=[pltpu.VMEM((ROWS, vp, LANES), F32)],
+    whole, split, east, west, south, pk = call(
+        functools.partial(sweeps_kernel, vals, vp),
+        [field, ((2 * vp, cell_count), BF16), field, field, field, lines(3, vp)],
+        state, diffusivity, sea_mask, w_hi,
+        in_specs=[VMEM] * 3 + [HBM],
+        scratch=[pltpu.VMEM((ROWS, vp, LANES), F32)] * 2,
         vmem=24,
-        flops=10 * vp * cell_count,
-        nbytes=24 * MIB,
+        us=8,
     )
     lon_out = call(
         lambda g_1, g_2, *refs: lon_kernel(vp, mp, g_1, g_2, True, *refs),
@@ -500,8 +548,7 @@
         split, cells,
         scratch=[pltpu.VMEM((cell_count, 7 * LANES), BF16)],
         vmem=24,
-        flops=4 * vp * cell_count * slots,
-        nbytes=8 * MIB,
+        us=3,
     )
     (payload,) = call(
         functools.partial(send_kernel, owners, vp, mp),
@@ -511,24 +558,14 @@
     )
     payload, w_hi, w_lo = lax.optimization_barrier((payload, w_hi, w_lo))
     received = across(payload)
-    wide = min(obs, 1024 if slots <= 1024 else 512)
-    equivalents, payload = pl.pallas_call(
+    matrix = 4 * slots * obs // MIB
+    equivalents, payload = call(
         functools.partial(owner_kernel, vals, vp, owners),
-        grid=(obs // wide,),
-        out_shape=[jax.ShapeDtypeStruct((vals, obs), F32), jax.ShapeDtypeStruct((owners * ROWS, LANES), F32)],
-        in_specs=[
-            pl.BlockSpec((owners * ROWS, LANES), lambda j: (0, 0)),
-            pl.BlockSpec((slots, wide), lambda j: (0, j)),
-            pl.BlockSpec((slots, wide), lambda j: (0, j)),
-            pl.BlockSpec((vals, wide), lambda j: (0, j)),
-        ],
-        out_specs=[
-            pl.BlockSpec((vals, wide), lambda j: (0, j)),
-            pl.BlockSpec((owners * ROWS, LANES), lambda j: (0, 0)),
-        ],
-        scratch_shapes=[pltpu.VMEM((2 * vp, slots), BF16), pltpu.VMEM((vp, wide), F32), pltpu.VMEM((vp, slots), F32)],
-        compiler_params=pltpu.CompilerParams(vmem_limit_bytes=48 * MIB),
-    )(received, w_hi, w_lo, obs_precision)
+        [((vals, obs), F32), ((owners * ROWS, LANES), F32)],
+        received, w_hi, w_lo, obs_precision,
+        scratch=[pltpu.VMEM((2 * vp, slots), BF16), pltpu.VMEM((2 * vp, obs), BF16)],
+        vmem=20 + matrix,
+    )
     incoming = across(payload)
     *lat_out, inc, ra, pa = call(
         functools.partial(back_kernel, owners, vp, mp),
@@ -543,16 +580,16 @@
         inc, cells, east, west, south,
         scratch=[pltpu.VMEM((ROWS, vp, LANES), F32)],
         vmem=24,
-        flops=4 * vp * cell_count * slots,
-        nbytes=10 * MIB,
-    )
+        us=4,
+    )
+    lat_back, mid = lax.optimization_barrier((lat_back, mid))
     lon_out = call(
         lambda g_1, g_2, *refs: lon_kernel(vp, mp, g_1, g_2, False, *refs),
         [lines(1, mp)] * 2, *lat_back, pa,
         vmem=8,
     )
     lon_back = exchange("lon", *lon_out)
-    (part,) = call(second_kernel, [field], mid, east, west, south, whole, vmem=24, flops=10 * vp * cell_count, nbytes=16 * MIB)
+    (part,) = call(second_kernel, [field], mid, east, west, south, whole, vmem=20, us=2)
     (product,) = call(
         functools.partial(final_kernel, vals, vp, mp),
         [(state.shape, F32)],

time: 116 us -> 93.2 us (0.80)
  Pallas kernels: 47 us -> 35 us
  local copies, waits for them, and re-layouts: 12 us -> 0.15 us
  blocking collectives: 35.1 us -> 37.2 us
    unnamed x30 -> x20, local copies, waits for them, and re-layouts: 11.9 us -> 0.06 us
    pallas_call x2 -> x1, Pallas kernels: 13.4 us -> 2.9 us  [on_device(): pl.pallas_call(weights_kernel, grid=(obs // wide,), out_shape=[jax.ShapeD...]
    all_to_all x2, blocking collectives: 35.1 us -> 37.2 us  [across(): lax.all_to_all(x, ('lon', 'lat'), split_axis=0, concat_axis=0, tiled=True)]
    pallas_call x10 -> x11, Pallas kernels: 33.6 us -> 32.1 us  [call(): pl.pallas_call(kernel, out_shape=[jax.ShapeDtypeStruct(s, d) for s, d in...]
  transfers between devices with their start and end apart: 8 -> 8, of which waited for: 2 -> 2; matrix products, arithmetic and copies ran while one was open for 0% -> 0% of each run, Pallas kernels for 18% -> 21%
where the time goes in v2:
time: 93.2 us; the launch traced here: 93 us
  blocking collectives  37.2 us (40%)
  Pallas kernels  35 us (38%)
  starting transfers between devices  15.5 us (17%)
  waiting for transfers between devices  4.1 us (4%)
  between operations  1.11 us (1%)
    all_to_all x2, blocking collectives, across(): lax.all_to_all(x, ('lon', 'lat'), split_axis=0, concat_axis=0, tiled=True)  37.2 us
    pallas_call x11, Pallas kernels, call(): pl.pallas_call(kernel, out_shape=[jax.ShapeDtypeStruct(s, d) for s, d in...  32.1 us
    ppermute x8, starting transfers between devices, swap(): return lax.ppermute(x, axis, pairs)  15.5 us
    ppermute x8, waiting for transfers between devices, swap(): return lax.ppermute(x, axis, pairs)  4.1 us
    pallas_call x1, Pallas kernels, on_device(): pl.pallas_call(weights_kernel, grid=(obs // wide,), out_shape=[jax.ShapeD...  2.9 us
  transfers between devices with their start and end apart: 8, of which 2 were waited for; matrix products, arithmetic and copies ran while one was open for 0% of the time, Pallas kernels for 21%

profile of v2, /device:TPU:2, one launch (start us, length us, event | category | flops | bytes accessed | tf_op | source)
XLA Modules:
  0.0 93.0 jit_solution(16627482064586984494)
XLA Ops:
  0.7 2.7 %shard_map.86 = (f32[456,128]{1,0:T(8,128)}, f32[456,128]{1,0:T(8,128)}, f32[640,128]{1,0:T(8,128)}, f32[640,128]{1,0:T(8,128)}, f32[8,128]{1,0:T(8,128)}) custom-call(f32[150,32,128]{2,1,0:T(8,128)} %state.3, f32[150,32,128]{2,1,0:T(8,128)} %diff.3, s32[75,32,128]{2,1,0:T(8,128)} %mask.3), custom_call_target="tpu_custom_call" | custom-call | flops 1048576 | bytes 3300000 | tf_op jit(solution)/shard_map/pallas_call | solution.py:205
  3.4 4.9 %collective-permute-start.1 = (f32[456,128]{1,0:T(8,128)}, f32[456,128]{1,0:T(8,128)S(1)}, u32[]{:S(2)}, u32[]{:S(2)}) collective-permute-start(f32[456,128]{1,0:T(8,128)} %get-tuple-element.32), channel_id=1, source_target_pairs={{1,2},{2,1},{5,6},{6,5},{9,10},{10,9},{13,14},{14,13},{17,18},{18,... | collective-permute-start | bytes 700424 | tf_op jit(solution)/shard_map/ppermute | solution.py:480
  8.3 0.1 reshape.14
  8.5 2.9 %shard_map.87 = (bf16[896,2048]{1,0:T(8,128)(2,1)S(1)}, bf16[896,2048]{1,0:T(8,128)(2,1)S(1)}) custom-call(s32[4,2048]{1,0:T(4,128)S(1)} %copy-done.6, f32[4,2048]{1,0:T(4,128)S(1)} %copy-done.7), custom_call_target="tpu_custom_call" | custom-call | flops 4000000000 | bytes 80000000 | tf_op jit(solution)/shard_map/pallas_call | solution.py:521
  11.4 8.7 %shard_map.88 = (f32[32,160,128]{2,1,0:T(8,128)S(1)}, bf16[320,4096]{1,0:T(8,128)(2,1)S(1)}, f32[32,160,128]{2,1,0:T(8,128)S(1)}, f32[32,160,128]{2,1,0:T(8,128)...) custom-call(f32[150,32,128]{2,1,0:T(8,128)S(1)} %copy-done, f32[150,32,128]{2,1,0:T(8,128)S(1)} %copy-done.1, ...), custom_call_target="tpu_custom_call" | custom-call | flops 1048576 | bytes 26400000 | tf_op jit(solution)/shard_map/pallas_call | solution.py:205
  20.2 0.3 shard_map.89
  20.5 0.1 collective-permute-start.2
  20.6 3.7 %collective-permute-start.3 = (f32[152,128]{1,0:T(8,128)S(1)}, f32[152,128]{1,0:T(8,128)S(1)}, u32[]{:S(2)}, u32[]{:S(2)}) collective-permute-start(f32[152,128]{1,0:T(8,128)S(1)} %get-tuple-element.36), channel_id=1, source_target_pairs={{0,28},{4,8},{8,4},{12,16},{16,12},{20,24},{24,20},{28,0},{1,29},{... | collective-permute-start | bytes 233480 | tf_op jit(solution)/shard_map/ppermute | solution.py:480
  24.3 2.9 %shard_map.90.inner = f32[160,896]{1,0:T(8,128)S(1)} custom-call(bf16[320,4096]{1,0:T(8,128)(2,1)S(1)} %get-tuple-element.39.smooth, s32[1,896]{1,0:T(1,128)S(1)} %bitcast.14), custom_call_target="tpu_custom_call" | custom-call | flops 1048576 | bytes 9900000 | tf_op jit(solution)/shard_map/pallas_call | solution.py:205
  27.3 2.1 %shard_map.91 = f32[1024,128]{1,0:T(8,128)S(1)} custom-call(f32[456,128]{1,0:T(8,128)S(1)} %collective-permute-done.g_1, f32[456,128]{1,0:T(8,128)S(1)} %collective-permute-done.1.g_2, f32[152,128]{1,0:T(8,128)S(1)} %collective-permute-done.2.h_1, f32[152,128]{1,0:T(8,128)S(1)} %collective-permute-done.3.h_2, f32[640,128]{1,0:T(8,128)S(1)} %copy-done.5, ...), custom_call_target="tpu_custom_call" | custom-call | flops 1048576 | bytes 3300000 | tf_op jit(solution)/shard_map/pallas_call | solution.py:205
  29.3 18.7 %all_to_all.22 = f32[32,32,128]{2,1,0:T(8,128)S(1)} all-to-all(f32[32,32,128]{2,1,0:T(8,128)S(1)} %bitcast.12), channel_id=1, replica_groups=mesh['lon'=8,'lat'=4] {'lon','lat'}, dimensions={0} | all-to-all | bytes 1048576 | tf_op jit(solution)/shard_map/all_to_all | solution.py:490
  48.1 6.2 %shard_map.92 = (f32[150,2048]{1,0:T(8,128)}, f32[1024,128]{1,0:T(8,128)S(1)}) custom-call(f32[1024,128]{1,0:T(8,128)S(1)} %bitcast.10, bf16[896,2048]{1,0:T(8,128)(2,1)S(1)} %get-tuple-element.42.after.w_hi, bf16[896,2048]{1,0:T(8,128)(2,1)S(1)} %get-tuple-element.43.w_lo, f32[150,2048]{1,0:T(8,128)S(1)} %copy-done.4), custom_call_target="tpu_custom_call" | custom-call | flops 1048576 | bytes 3300000 | tf_op jit(solution)/shard_map/pallas_call | solution.py:205
  54.3 18.4 %all_to_all.23 = f32[32,32,128]{2,1,0:T(8,128)S(1)} all-to-all(f32[32,32,128]{2,1,0:T(8,128)S(1)} %bitcast.13), channel_id=1, replica_groups=mesh['lon'=8,'lat'=4] {'lon','lat'}, dimensions={0} | all-to-all | bytes 1048576 | tf_op jit(solution)/shard_map/all_to_all | solution.py:490
  72.7 1.3 %shard_map.93 = (f32[304,128]{1,0:T(8,128)S(1)}, f32[304,128]{1,0:T(8,128)S(1)}, bf16[320,896]{1,0:T(8,128)(2,1)S(1)}, f32[640,128]{1,0:T(8,128)S(1)}, f32[320,128]{1,0:T(8,128)S(1)}) custom-call(f32[1024,128]{1,0:T(8,128)S(1)} %bitcast.11, s32[1,896]{1,0:T(1,128)S(1)} %bitcast.16, f32[640,128]{1,0:T(8,128)S(1)} %copy-done.3, ...), custom_call_target="tpu_custom_call" | custom-call | flops 1048576 | bytes 3300000 | tf_op jit(solution)/shard_map/pallas_call | solution.py:205
  74.0 1.9 %collective-permute-start.4 = (f32[304,128]{1,0:T(8,128)S(1)}, f32[304,128]{1,0:T(8,128)S(1)}, u32[]{:S(2)}, u32[]{:S(2)}) collective-permute-start(f32[304,128]{1,0:T(8,128)S(1)} %get-tuple-element.45), channel_id=1, source_target_pairs={{0,1},{1,0},{2,3},{3,2},{4,5},{5,4},{6,7},{7,6},{8,9},{9,8},{10,11... | collective-permute-start | bytes 466952 | tf_op jit(solution)/shard_map/ppermute | solution.py:480
  75.9 3.3 %collective-permute-start.5 = (f32[304,128]{1,0:T(8,128)S(1)}, f32[304,128]{1,0:T(8,128)S(1)}, u32[]{:S(2)}, u32[]{:S(2)}) collective-permute-start(f32[304,128]{1,0:T(8,128)S(1)} %get-tuple-element.46), channel_id=1, source_target_pairs={{1,2},{2,1},{5,6},{6,5},{9,10},{10,9},{13,14},{14,13},{17,18},{18,... | collective-permute-start | bytes 466952 | tf_op jit(solution)/shard_map/ppermute | solution.py:480
  79.2 3.3 %shard_map.94.mid = f32[32,160,128]{2,1,0:T(8,128)S(1)} custom-call(bf16[320,896]{1,0:T(8,128)(2,1)S(1)} %get-tuple-element.47.inc, s32[1,896]{1,0:T(1,128)S(1)} %bitcast.17, f32[32,160,128]{2,1,0:T(8,128)S(1)} %get-tuple-element.48.east, f32[32,160,128]{2,1,0:T(8,128)S(1)} %get-tuple-element.49.west, f32[32,160,128]{2,1,0:T(8,128)S(1)} %get-tuple-element.50.south), custom_call_target="tpu_custom_call" | custom-call | flops 1048576 | bytes 13200000 | tf_op jit(solution)/shard_map/pallas_call | solution.py:205
  82.5 1.4 %collective-permute-done.5.g_2.a_2 = f32[304,128]{1,0:T(8,128)S(1)} collective-permute-done((f32[304,128]{1,0:T(8,128)S(1)}, f32[304,128]{1,0:T(8,128)S(1)}, u32[]{:S(2)}, u32[]{:S(2)}) %collective-permute-start.5) | collective-permute-done | bytes 155680 | tf_op jit(solution)/shard_map/ppermute | solution.py:480
  83.9 0.3 shard_map.95
  84.2 0.1 collective-permute-start.6
  84.3 1.6 %collective-permute-start.7 = (f32[152,128]{1,0:T(8,128)S(1)}, f32[152,128]{1,0:T(8,128)S(1)}, u32[]{:S(2)}, u32[]{:S(2)}) collective-permute-start(f32[152,128]{1,0:T(8,128)S(1)} %get-tuple-element.55), channel_id=1, source_target_pairs={{0,28},{4,8},{8,4},{12,16},{16,12},{20,24},{24,20},{28,0},{1,29},{... | collective-permute-start | bytes 233480 | tf_op jit(solution)/shard_map/ppermute | solution.py:480
  85.9 1.5 %shard_map.96.part = f32[32,160,128]{2,1,0:T(8,128)S(1)} custom-call(f32[32,160,128]{2,1,0:T(8,128)S(1)} %shard_map.94.mid, f32[32,160,128]{2,1,0:T(8,128)S(1)} %get-tuple-element.48.east, f32[32,160,128]{2,1,0:T(8,128)S(1)} %get-tuple-element.49.west, f32[32,160,128]{2,1,0:T(8,128)S(1)} %get-tuple-element.50.south, f32[32,160,128]{2,1,0:T(8,128)S(1)} %get-tuple-element.58.field), custom_call_target="tpu_custom_call" | custom-call | flops 1048576 | bytes 6600000 | tf_op jit(solution)/shard_map/pallas_call | solution.py:205
  87.4 2.6 %collective-permute-done.7.b_2 = f32[152,128]{1,0:T(8,128)S(1)} collective-permute-done((f32[152,128]{1,0:T(8,128)S(1)}, f32[152,128]{1,0:T(8,128)S(1)}, u32[]{:S(2)}, u32[]{:S(2)}) %collective-permute-start.7) | collective-permute-done | bytes 77856 | tf_op jit(solution)/shard_map/ppermute | solution.py:480
  90.0 2.8 %shard_map.97 = f32[150,32,128]{2,1,0:T(8,128)} custom-call(f32[456,128]{1,0:T(8,128)S(1)} %collective-permute-done.g_1, f32[456,128]{1,0:T(8,128)S(1)} %collective-permute-done.1.g_2, f32[152,128]{1,0:T(8,128)S(1)} %collective-permute-done.2.h_1, f32[152,128]{1,0:T(8,128)S(1)} %collective-permute-done.3.h_2, f32[304,128]{1,0:T(8,128)S(1)} %collective-permute-done.4.g_1.a_1, ...), custom_call_target="tpu_custom_call" | custom-call | flops 1048576 | bytes 3300000 | tf_op jit(solution)/shard_map/pallas_call | solution.py:205
  (28 shorter events, 0.2 us)
Async XLA Ops:
  0.6 7.8 %copy-start.7 = (f32[4,2048]{1,0:T(4,128)S(1)}, f32[4,2048]{1,0:T(4,128)}, u32[]{:S(2)}) copy-start(f32[4,2048]{1,0:T(4,128)} %weights) | copy-start | bytes 98308
  0.6 7.7 %copy-start.8 = (s32[1,768]{1,0:T(1,128)S(1)}, s32[1,768]{1,0:T(1,128)}, u32[]{:S(2)}) copy-start(s32[1,768]{1,0:T(1,128)} %param.10) | copy-start | bytes 9220
  0.7 7.8 %copy-start.6 = (s32[4,2048]{1,0:T(4,128)S(1)}, s32[4,2048]{1,0:T(4,128)}, u32[]{:S(2)}) copy-start(s32[4,2048]{1,0:T(4,128)} %slots.1) | copy-start | bytes 98308
  3.4 16.8 %collective-permute-start = (f32[456,128]{1,0:T(8,128)}, f32[456,128]{1,0:T(8,128)S(1)}, u32[]{:S(2)}, u32[]{:S(2)}) collective-permute-start(f32[456,128]{1,0:T(8,128)} %get-tuple-element.31), channel_id=1, source_target_pairs={{0,1},{1,0},{2,3},{3,2},{4,5},{5,4},{6,7},{7,6},{8,9},{9,8},{10,11... | collective-permute-start | bytes 700424 | tf_op jit(solution)/shard_map/ppermute | solution.py:480
  3.4 16.7 %collective-permute-start.1 = (f32[456,128]{1,0:T(8,128)}, f32[456,128]{1,0:T(8,128)S(1)}, u32[]{:S(2)}, u32[]{:S(2)}) collective-permute-start(f32[456,128]{1,0:T(8,128)} %get-tuple-element.32), channel_id=1, source_target_pairs={{1,2},{2,1},{5,6},{6,5},{9,10},{10,9},{13,14},{14,13},{17,18},{18,... | collective-permute-start | bytes 700424 | tf_op jit(solution)/shard_map/ppermute | solution.py:480
  8.4 2.9 %copy-start = (f32[150,32,128]{2,1,0:T(8,128)S(1)}, f32[150,32,128]{2,1,0:T(8,128)}, u32[]{:S(2)}) copy-start(f32[150,32,128]{2,1,0:T(8,128)} %state.3) | copy-start | bytes 7372804
  8.4 2.9 %copy-start.1 = (f32[150,32,128]{2,1,0:T(8,128)S(1)}, f32[150,32,128]{2,1,0:T(8,128)}, u32[]{:S(2)}) copy-start(f32[150,32,128]{2,1,0:T(8,128)} %diff.3) | copy-start | bytes 7372804
  8.5 2.9 %copy-start.2 = (s32[75,32,128]{2,1,0:T(8,128)S(1)}, s32[75,32,128]{2,1,0:T(8,128)}, u32[]{:S(2)}) copy-start(s32[75,32,128]{2,1,0:T(8,128)} %mask.3) | copy-start | bytes 3686404
  20.1 7.1 %copy-start.3 = (f32[640,128]{1,0:T(8,128)S(1)}, f32[640,128]{1,0:T(8,128)}, u32[]{:S(2)}) copy-start(f32[640,128]{1,0:T(8,128)} %get-tuple-element.38.rc) | copy-start | bytes 983044
  20.2 7.1 %copy-start.5 = (f32[640,128]{1,0:T(8,128)S(1)}, f32[640,128]{1,0:T(8,128)}, u32[]{:S(2)}) copy-start(f32[640,128]{1,0:T(8,128)} %get-tuple-element.37.rv) | copy-start | bytes 983044
  20.5 6.7 %collective-permute-start.2 = (f32[152,128]{1,0:T(8,128)S(1)}, f32[152,128]{1,0:T(8,128)S(1)}, u32[]{:S(2)}, u32[]{:S(2)}) collective-permute-start(f32[152,128]{1,0:T(8,128)S(1)} %get-tuple-element.35), channel_id=1, source_target_pairs={{0,4},{4,0},{8,12},{12,8},{16,20},{20,16},{24,28},{28,24},{1,5},{5... | collective-permute-start | bytes 233480 | tf_op jit(solution)/shard_map/ppermute | solution.py:480
  20.6 6.6 %collective-permute-start.3 = (f32[152,128]{1,0:T(8,128)S(1)}, f32[152,128]{1,0:T(8,128)S(1)}, u32[]{:S(2)}, u32[]{:S(2)}) collective-permute-start(f32[152,128]{1,0:T(8,128)S(1)} %get-tuple-element.36), channel_id=1, source_target_pairs={{0,28},{4,8},{8,4},{12,16},{16,12},{20,24},{24,20},{28,0},{1,29},{... | collective-permute-start | bytes 233480 | tf_op jit(solution)/shard_map/ppermute | solution.py:480
  27.2 20.9 %copy-start.4 = (f32[150,2048]{1,0:T(8,128)S(1)}, f32[150,2048]{1,0:T(8,128)}, u32[]{:S(2)}) copy-start(f32[150,2048]{1,0:T(8,128)} %prec.1) | copy-start | bytes 3686404
  74.0 8.4 %collective-permute-start.4 = (f32[304,128]{1,0:T(8,128)S(1)}, f32[304,128]{1,0:T(8,128)S(1)}, u32[]{:S(2)}, u32[]{:S(2)}) collective-permute-start(f32[304,128]{1,0:T(8,128)S(1)} %get-tuple-element.45), channel_id=1, source_target_pairs={{0,1},{1,0},{2,3},{3,2},{4,5},{5,4},{6,7},{7,6},{8,9},{9,8},{10,11... | collective-permute-start | bytes 466952 | tf_op jit(solution)/shard_map/ppermute | solution.py:480
  75.9 8.0 %collective-permute-start.5 = (f32[304,128]{1,0:T(8,128)S(1)}, f32[304,128]{1,0:T(8,128)S(1)}, u32[]{:S(2)}, u32[]{:S(2)}) collective-permute-start(f32[304,128]{1,0:T(8,128)S(1)} %get-tuple-element.46), channel_id=1, source_target_pairs={{1,2},{2,1},{5,6},{6,5},{9,10},{10,9},{13,14},{14,13},{17,18},{18,... | collective-permute-start | bytes 466952 | tf_op jit(solution)/shard_map/ppermute | solution.py:480
  84.2 3.2 %collective-permute-start.6 = (f32[152,128]{1,0:T(8,128)S(1)}, f32[152,128]{1,0:T(8,128)S(1)}, u32[]{:S(2)}, u32[]{:S(2)}) collective-permute-start(f32[152,128]{1,0:T(8,128)S(1)} %get-tuple-element.54), channel_id=1, source_target_pairs={{0,4},{4,0},{8,12},{12,8},{16,20},{20,16},{24,28},{28,24},{1,5},{5... | collective-permute-start | bytes 233480 | tf_op jit(solution)/shard_map/ppermute | solution.py:480
  84.3 5.7 %collective-permute-start.7 = (f32[152,128]{1,0:T(8,128)S(1)}, f32[152,128]{1,0:T(8,128)S(1)}, u32[]{:S(2)}, u32[]{:S(2)}) collective-permute-start(f32[152,128]{1,0:T(8,128)S(1)} %get-tuple-element.55), channel_id=1, source_target_pairs={{0,28},{4,8},{8,4},{12,16},{16,12},{20,24},{24,20},{28,0},{1,29},{... | collective-permute-start | bytes 233480 | tf_op jit(solution)/shard_map/ppermute | solution.py:480

commit v3 on v2

--- a/solution.py
+++ b/solution.py
@@ -10,7 +10,9 @@
 CAP = 24
 LANES = 128
 GROUPS = 5
+CHUNK = 32 * CAP
 ROWS = 32
+SENT = 30
 OBS_BLOCK = 256
 F32, BF16 = jnp.float32, jnp.bfloat16
 MIB = 1 << 20
@@ -168,32 +170,51 @@
     return jnp.concatenate(rows + [pack], axis=0)
 
 
-def pack_payload(x, out_ref, first, last):
+def spans(o):
+    a, lane = divmod(CAP * o, LANES)
+    if lane + CAP <= LANES:
+        return [(a, lane, 0, CAP)]
+    return [(a, lane, 0, LANES - lane), (a + 1, lane - LANES, LANES - lane, CAP)]
+
+
+def pack_payload(columns, out_ref, first, last):
     lane = lax.broadcasted_iota(jnp.int32, (ROWS, LANES), 1)
+    tail = ROWS - 2 * (GROUPS - 1) - 2
+    tiles = []
     for o in range(first, last):
-        a, b = divmod(o - first, GROUPS)
+        while len(tiles) <= spans(o - first)[-1][0]:
+            x = columns(len(tiles) // 2)
+            rest = [x[ROWS * g + SENT : ROWS * (g + 1)] for g in range(GROUPS - 1)]
+            groups = [x[ROWS * g : ROWS * (g + 1)] for g in range(GROUPS - 1)]
+            groups.append(jnp.concatenate([x[ROWS * (GROUPS - 1) :][:tail], *rest, jnp.zeros((2, x.shape[1]), F32)], axis=0))
+            tiles += [[g[:, :LANES] for g in groups], [g[:, LANES:] for g in groups]]
         block = jnp.zeros((ROWS, LANES), F32)
-        for g in range(GROUPS):
-            piece = roll(x[ROWS * g : ROWS * (g + 1), LANES * a : LANES * (a + 1)], CAP * (g - b))
-            block = jnp.where((lane >= CAP * g) & (lane < CAP * (g + 1)), piece, block)
-        out_ref[ROWS * o : ROWS * (o + 1), :] = block
+        for a, at, p, q in spans(o - first):
+            for g in range(GROUPS):
+                piece = roll(tiles[a][g], CAP * g - at)
+                block = jnp.where((lane >= CAP * g + p) & (lane < CAP * g + q), piece, block)
+        out_ref[SENT * o : SENT * (o + 1), :] = block[:SENT]
 
 
 def unpack_payload(in_ref, owners, slots):
     lane = lax.broadcasted_iota(jnp.int32, (ROWS, LANES), 1)
-    columns = []
-    for a in range(slots // LANES):
-        pieces = []
-        for g in range(GROUPS):
-            piece = jnp.zeros((ROWS, LANES), F32)
-            for b in range(GROUPS):
-                o = GROUPS * a + b
-                if o < owners:
-                    block = roll(in_ref[ROWS * o : ROWS * (o + 1), :], CAP * (b - g))
-                    piece = jnp.where((lane >= CAP * b) & (lane < CAP * (b + 1)), block, piece)
-            pieces.append(piece)
-        columns.append(jnp.concatenate(pieces, axis=0))
-    return jnp.concatenate(columns, axis=1)
+    pieces = [[jnp.zeros((ROWS, LANES), F32) for _ in range(slots // LANES)] for _ in range(GROUPS)]
+    for o in range(owners):
+        if o < owners - 1:
+            block = in_ref[SENT * o : SENT * o + ROWS, :]
+        else:
+            block = tall(in_ref[SENT * o :, :], ROWS)
+        for a, at, p, q in spans(o):
+            for g in range(GROUPS):
+                here = (lane >= at + p) & (lane < at + q)
+                pieces[g][a] = jnp.where(here, roll(block, at - CAP * g), pieces[g][a])
+    groups = [jnp.concatenate(x, axis=1) for x in pieces]
+    tail = ROWS - 2 * (GROUPS - 1) - 2
+    out = []
+    for g in range(GROUPS - 1):
+        out += [groups[g][:SENT], groups[-1][tail + 2 * g : tail + 2 * (g + 1)]]
+    out += [groups[-1][:tail], jnp.zeros((ROWS - tail, slots), F32)]
+    return jnp.concatenate(out, axis=0)
 
 
 def takes(us):
@@ -360,10 +381,8 @@
 
 
 def weights_kernel(slots, weights, hi, lo):
-    s = slots[...]
-    place = s + 8 * jnp.floor((s.astype(F32) + 0.5) * (1.0 / (CAP * GROUPS))).astype(jnp.int32)
     taps = range(slots.shape[0])
-    at = [place[k : k + 1] for k in taps]
+    at = [slots[k : k + 1, :] for k in taps]
     w = [weights[k : k + 1, :] for k in taps]
     for a in taps:
         for b in range(a + 1, len(taps)):
@@ -394,9 +413,15 @@
     v0, v31, p0, p31 = parts_of(rv, vp)
     pv, pc, pp = parts_of(pk, vp)
     fix = rim_correction((v0, v31, p0, p31, pv, pp), parts_of(rc, vp) + [pc], ghosts)
-    slots = cells.shape[1]
-    total = folded(dot(stacked(jnp.concatenate(fix, axis=1)), chosen(cells[...], rim_ids(slots))))
-    pack_payload(inner[...] + total, out, 0, owners)
+    wide = 2 * LANES
+    fix = stacked(jnp.concatenate(fix, axis=1))
+    ids = rim_ids(wide)
+
+    def columns(k):
+        at = slice(wide * k, wide * (k + 1))
+        return inner[:, at] + folded(dot(fix, chosen(cells[:, at], ids)))
+
+    pack_payload(columns, out, 0, owners)
 
 
 def owner_kernel(vals, vp, owners, got, w_hi, w_lo, prec, equiv, back, r2, w2):
@@ -407,11 +432,13 @@
         e = (folded(dot(r2[...], w_hi[:, at])) + dot(r2[:vp, :], w_lo[:, at]))[:vals]
         equiv[:, at] = e
         w2[:, at] = stacked(tall(prec[:, at] * e, vp))
-    for o in range(0, r2.shape[1], 7 * LANES):
-        at = slice(o, o + 7 * LANES)
-        x = folded(dot_nt(w2[...], w_hi[at, :])) + dot_nt(w2[:vp, :], w_lo[at, :])
-        n = 7 * GROUPS * (o // (7 * LANES))
-        pack_payload(x, back, n, min(owners, n + 7 * GROUPS))
+    for o in range(0, r2.shape[1], CHUNK):
+
+        def columns(k):
+            at = slice(o + 2 * LANES * k, o + 2 * LANES * (k + 1))
+            return folded(dot_nt(w2[...], w_hi[at, :])) + dot_nt(w2[:vp, :], w_lo[at, :])
+
+        pack_payload(columns, back, o // CAP, (o + CHUNK) // CAP)
 
 
 def back_kernel(owners, vp, mp, got, cells, rc, pk, m_1, m_2, inc, ra, pa):
@@ -487,19 +514,18 @@
 
 
 def across(x):
-    return lax.all_to_all(x, ("lon", "lat"), split_axis=0, concat_axis=0, tiled=True)
+    flat = x.reshape(lax.axis_size(("lon", "lat")), 1, SENT * LANES)
+    return lax.all_to_all(flat, ("lon", "lat"), split_axis=0, concat_axis=0, tiled=True).reshape(x.shape)
 
 
 def on_device(state, diffusivity, sea_mask, send_cols, obs_slots, obs_weights, obs_precision):
     vals, taps, obs = state.shape[0], obs_slots.shape[0], obs_slots.shape[1]
     owners = send_cols.shape[1] // CAP
     vp, mp = up(vals, ROWS), up(vals, 8)
-    tiles = up(owners, 7 * GROUPS) // GROUPS
-    slots = tiles * LANES
+    slots = owners * CAP
     cell_count = ROWS * LANES
-    cells = jnp.pad(send_cols, ((0, 0), (0, tiles * GROUPS * CAP - owners * CAP)), constant_values=cell_count)
-    cells = jnp.pad(cells.reshape(tiles, GROUPS * CAP), ((0, 0), (0, LANES - GROUPS * CAP)), constant_values=cell_count)
-    cells = cells.reshape(1, slots)
+    cells = send_cols
+    blocks = ((owners * SENT, LANES), F32)
     lines = lambda n, rows, dtype=F32: ((n * rows, LANES), dtype)
     field = ((ROWS, vp, LANES), F32)
 
@@ -516,7 +542,7 @@
         vmem=62,
     )
     lat_in = exchange("lat", *lat_out)
-    wide = min(obs, 1024 if slots <= 1024 else 512)
+    wide = obs if slots <= 1024 else 512
     obs_weights, done = lax.optimization_barrier((obs_weights, done))
     w_hi, w_lo = pl.pallas_call(
         weights_kernel,
@@ -546,13 +572,13 @@
         select_kernel,
         [((vp, slots), F32)],
         split, cells,
-        scratch=[pltpu.VMEM((cell_count, 7 * LANES), BF16)],
+        scratch=[pltpu.VMEM((cell_count, CHUNK), BF16)],
         vmem=24,
         us=3,
     )
     (payload,) = call(
         functools.partial(send_kernel, owners, vp, mp),
-        [((owners * ROWS, LANES), F32)],
+        [blocks],
         *lat_in, *lon_in, rv, rc, pk, inner, cells,
         vmem=24,
     )
@@ -561,7 +587,7 @@
     matrix = 4 * slots * obs // MIB
     equivalents, payload = call(
         functools.partial(owner_kernel, vals, vp, owners),
-        [((vals, obs), F32), ((owners * ROWS, LANES), F32)],
+        [((vals, obs), F32), blocks],
         received, w_hi, w_lo, obs_precision,
         scratch=[pltpu.VMEM((2 * vp, slots), BF16), pltpu.VMEM((2 * vp, obs), BF16)],
         vmem=20 + matrix,

time: 93.2 us -> 91.1 us (0.977)
  Pallas kernels: 35 us -> 32.9 us
    pallas_call x11, Pallas kernels: 32.1 us -> 30.8 us  [call(): pl.pallas_call(kernel, out_shape=[jax.ShapeDtypeStruct(s, d) for s, d in...]
  transfers between devices with their start and end apart: 8 -> 8, of which waited for: 2 -> 2; matrix products, arithmetic and copies ran while one was open for 0% -> 0% of each run, Pallas kernels for 21% -> 19%
where the time goes in v3:
time: 91.1 us; the launch traced here: 90.9 us
  blocking collectives  36.3 us (40%)
  Pallas kernels  32.9 us (36%)
  starting transfers between devices  15.7 us (17%)
  waiting for transfers between devices  4.82 us (5%)
  between operations  1.1 us (1%)
    all_to_all x2, blocking collectives, across(): lax.all_to_all(flat, ('lon', 'lat'), split_axis=0, concat_axis=0, tiled=T...  36.3 us
    pallas_call x11, Pallas kernels, call(): pl.pallas_call(kernel, out_shape=[jax.ShapeDtypeStruct(s, d) for s, d in...  30.8 us
    ppermute x8, starting transfers between devices, swap(): return lax.ppermute(x, axis, pairs)  15.7 us
    ppermute x8, waiting for transfers between devices, swap(): return lax.ppermute(x, axis, pairs)  4.82 us
    pallas_call x1, Pallas kernels, on_device(): pl.pallas_call(weights_kernel, grid=(obs // wide,), out_shape=[jax.ShapeD...  2.15 us
  transfers between devices with their start and end apart: 8, of which 2 were waited for; matrix products, arithmetic and copies ran while one was open for 0% of the time, Pallas kernels for 19%

profile of v3, /device:TPU:2, one launch (start us, length us, event | category | flops | bytes accessed | tf_op | source)
XLA Modules:
  0.0 90.9 jit_solution(2845633536818737819)
XLA Ops:
  0.6 2.7 %shard_map.86 = (f32[456,128]{1,0:T(8,128)}, f32[456,128]{1,0:T(8,128)}, f32[640,128]{1,0:T(8,128)}, f32[640,128]{1,0:T(8,128)}, f32[8,128]{1,0:T(8,128)}) custom-call(f32[150,32,128]{2,1,0:T(8,128)} %state.3, f32[150,32,128]{2,1,0:T(8,128)} %diff.3, s32[75,32,128]{2,1,0:T(8,128)} %mask.3), custom_call_target="tpu_custom_call" | custom-call | flops 1048576 | bytes 3300000 | tf_op jit(solution)/shard_map/pallas_call | solution.py:226
  3.4 0.1 collective-permute-start
  3.5 5.1 %collective-permute-start.1 = (f32[456,128]{1,0:T(8,128)}, f32[456,128]{1,0:T(8,128)S(1)}, u32[]{:S(2)}, u32[]{:S(2)}) collective-permute-start(f32[456,128]{1,0:T(8,128)} %get-tuple-element.32), channel_id=1, source_target_pairs={{1,2},{2,1},{5,6},{6,5},{9,10},{10,9},{13,14},{14,13},{17,18},{18,... | collective-permute-start | bytes 700424 | tf_op jit(solution)/shard_map/ppermute | solution.py:507
  8.6 2.2 %shard_map.87 = (bf16[768,2048]{1,0:T(8,128)(2,1)S(1)}, bf16[768,2048]{1,0:T(8,128)(2,1)S(1)}) custom-call(s32[4,2048]{1,0:T(4,128)S(1)} %copy-done.7, f32[4,2048]{1,0:T(4,128)S(1)} %copy-done.8), custom_call_target="tpu_custom_call" | custom-call | flops 4000000000 | bytes 80000000 | tf_op jit(solution)/shard_map/pallas_call | solution.py:547
  10.8 8.7 %shard_map.88 = (f32[32,160,128]{2,1,0:T(8,128)S(1)}, bf16[320,4096]{1,0:T(8,128)(2,1)S(1)}, f32[32,160,128]{2,1,0:T(8,128)S(1)}, f32[32,160,128]{2,1,0:T(8,128)...) custom-call(f32[150,32,128]{2,1,0:T(8,128)S(1)} %copy-done, f32[150,32,128]{2,1,0:T(8,128)S(1)} %copy-done.1, ...), custom_call_target="tpu_custom_call" | custom-call | flops 1048576 | bytes 26400000 | tf_op jit(solution)/shard_map/pallas_call | solution.py:226
  19.6 0.3 shard_map.89
  19.9 0.1 collective-permute-start.2
  20.0 3.7 %collective-permute-start.3 = (f32[152,128]{1,0:T(8,128)S(1)}, f32[152,128]{1,0:T(8,128)S(1)}, u32[]{:S(2)}, u32[]{:S(2)}) collective-permute-start(f32[152,128]{1,0:T(8,128)S(1)} %get-tuple-element.36), channel_id=1, source_target_pairs={{0,28},{4,8},{8,4},{12,16},{16,12},{20,24},{24,20},{28,0},{1,29},{... | collective-permute-start | bytes 233480 | tf_op jit(solution)/shard_map/ppermute | solution.py:507
  23.7 2.4 %shard_map.90.inner = f32[160,768]{1,0:T(8,128)S(1)} custom-call(bf16[320,4096]{1,0:T(8,128)(2,1)S(1)} %get-tuple-element.39.smooth, s32[1,768]{1,0:T(1,128)S(1)} %copy-done.6), custom_call_target="tpu_custom_call" | custom-call | flops 1048576 | bytes 9900000 | tf_op jit(solution)/shard_map/pallas_call | solution.py:226
  26.1 2.1 %shard_map.91 = f32[960,128]{1,0:T(8,128)S(1)} custom-call(f32[456,128]{1,0:T(8,128)S(1)} %collective-permute-done.g_1, f32[456,128]{1,0:T(8,128)S(1)} %collective-permute-done.1.g_2, f32[152,128]{1,0:T(8,128)S(1)} %collective-permute-done.2.h_1, f32[152,128]{1,0:T(8,128)S(1)} %collective-permute-done.3.h_2, f32[640,128]{1,0:T(8,128)S(1)} %copy-done.5, ...), custom_call_target="tpu_custom_call" | custom-call | flops 1048576 | bytes 3300000 | tf_op jit(solution)/shard_map/pallas_call | solution.py:226
  28.2 18.5 %all_to_all.10 = f32[32,1,3840]{2,1,0:T(1,128)S(1)} all-to-all(f32[32,1,3840]{2,1,0:T(1,128)S(1)} %bitcast.5), channel_id=1, replica_groups=mesh['lon'=8,'lat'=4] {'lon','lat'}, dimensions={0} | all-to-all | bytes 983040 | tf_op jit(solution)/shard_map/all_to_all | solution.py:518
  46.7 6.0 %shard_map.92 = (f32[150,2048]{1,0:T(8,128)}, f32[960,128]{1,0:T(8,128)S(1)}) custom-call(f32[960,128]{1,0:T(8,128)S(1)} %bitcast.6, bf16[768,2048]{1,0:T(8,128)(2,1)S(1)} %get-tuple-element.42.after.w_hi, bf16[768,2048]{1,0:T(8,128)(2,1)S(1)} %get-tuple-element.43.w_lo, f32[150,2048]{1,0:T(8,128)S(1)} %copy-done.4), custom_call_target="tpu_custom_call" | custom-call | flops 1048576 | bytes 3300000 | tf_op jit(solution)/shard_map/pallas_call | solution.py:226
  52.8 17.7 %all_to_all.11 = f32[32,1,3840]{2,1,0:T(1,128)S(1)} all-to-all(f32[32,1,3840]{2,1,0:T(1,128)S(1)} %bitcast.7), channel_id=1, replica_groups=mesh['lon'=8,'lat'=4] {'lon','lat'}, dimensions={0} | all-to-all | bytes 983040 | tf_op jit(solution)/shard_map/all_to_all | solution.py:518
  70.5 1.4 %shard_map.93 = (f32[304,128]{1,0:T(8,128)S(1)}, f32[304,128]{1,0:T(8,128)S(1)}, bf16[320,768]{1,0:T(8,128)(2,1)S(1)}, f32[640,128]{1,0:T(8,128)S(1)}, f32[320,128]{1,0:T(8,128)S(1)}) custom-call(f32[960,128]{1,0:T(8,128)S(1)} %bitcast.4, s32[1,768]{1,0:T(1,128)S(1)} %copy-done.6, f32[640,128]{1,0:T(8,128)S(1)} %copy-done.3, ...), custom_call_target="tpu_custom_call" | custom-call | flops 1048576 | bytes 3300000 | tf_op jit(solution)/shard_map/pallas_call | solution.py:226
  71.9 1.9 %collective-permute-start.4 = (f32[304,128]{1,0:T(8,128)S(1)}, f32[304,128]{1,0:T(8,128)S(1)}, u32[]{:S(2)}, u32[]{:S(2)}) collective-permute-start(f32[304,128]{1,0:T(8,128)S(1)} %get-tuple-element.45), channel_id=1, source_target_pairs={{0,1},{1,0},{2,3},{3,2},{4,5},{5,4},{6,7},{7,6},{8,9},{9,8},{10,11... | collective-permute-start | bytes 466952 | tf_op jit(solution)/shard_map/ppermute | solution.py:507
  73.8 3.2 %collective-permute-start.5 = (f32[304,128]{1,0:T(8,128)S(1)}, f32[304,128]{1,0:T(8,128)S(1)}, u32[]{:S(2)}, u32[]{:S(2)}) collective-permute-start(f32[304,128]{1,0:T(8,128)S(1)} %get-tuple-element.46), channel_id=1, source_target_pairs={{1,2},{2,1},{5,6},{6,5},{9,10},{10,9},{13,14},{14,13},{17,18},{18,... | collective-permute-start | bytes 466952 | tf_op jit(solution)/shard_map/ppermute | solution.py:507
  77.0 2.6 %shard_map.94.mid = f32[32,160,128]{2,1,0:T(8,128)S(1)} custom-call(bf16[320,768]{1,0:T(8,128)(2,1)S(1)} %get-tuple-element.47.inc, s32[1,768]{1,0:T(1,128)S(1)} %copy-done.6, f32[32,160,128]{2,1,0:T(8,128)S(1)} %get-tuple-element.48.east, f32[32,160,128]{2,1,0:T(8,128)S(1)} %get-tuple-element.49.west, f32[32,160,128]{2,1,0:T(8,128)S(1)} %get-tuple-element.50.south), custom_call_target="tpu_custom_call" | custom-call | flops 1048576 | bytes 13200000 | tf_op jit(solution)/shard_map/pallas_call | solution.py:226
  79.7 2.2 %collective-permute-done.5.g_2.a_2 = f32[304,128]{1,0:T(8,128)S(1)} collective-permute-done((f32[304,128]{1,0:T(8,128)S(1)}, f32[304,128]{1,0:T(8,128)S(1)}, u32[]{:S(2)}, u32[]{:S(2)}) %collective-permute-start.5) | collective-permute-done | bytes 155680 | tf_op jit(solution)/shard_map/ppermute | solution.py:507
  81.9 0.3 shard_map.95
  82.2 0.1 collective-permute-start.6
  82.2 1.5 %collective-permute-start.7 = (f32[152,128]{1,0:T(8,128)S(1)}, f32[152,128]{1,0:T(8,128)S(1)}, u32[]{:S(2)}, u32[]{:S(2)}) collective-permute-start(f32[152,128]{1,0:T(8,128)S(1)} %get-tuple-element.55), channel_id=1, source_target_pairs={{0,28},{4,8},{8,4},{12,16},{16,12},{20,24},{24,20},{28,0},{1,29},{... | collective-permute-start | bytes 233480 | tf_op jit(solution)/shard_map/ppermute | solution.py:507
  83.8 1.5 %shard_map.96.part = f32[32,160,128]{2,1,0:T(8,128)S(1)} custom-call(f32[32,160,128]{2,1,0:T(8,128)S(1)} %shard_map.94.mid, f32[32,160,128]{2,1,0:T(8,128)S(1)} %get-tuple-element.48.east, f32[32,160,128]{2,1,0:T(8,128)S(1)} %get-tuple-element.49.west, f32[32,160,128]{2,1,0:T(8,128)S(1)} %get-tuple-element.50.south, f32[32,160,128]{2,1,0:T(8,128)S(1)} %get-tuple-element.58.field), custom_call_target="tpu_custom_call" | custom-call | flops 1048576 | bytes 6600000 | tf_op jit(solution)/shard_map/pallas_call | solution.py:226
  85.3 2.6 %collective-permute-done.7.b_2 = f32[152,128]{1,0:T(8,128)S(1)} collective-permute-done((f32[152,128]{1,0:T(8,128)S(1)}, f32[152,128]{1,0:T(8,128)S(1)}, u32[]{:S(2)}, u32[]{:S(2)}) %collective-permute-start.7) | collective-permute-done | bytes 77856 | tf_op jit(solution)/shard_map/ppermute | solution.py:507
  87.9 2.8 %shard_map.97 = f32[150,32,128]{2,1,0:T(8,128)} custom-call(f32[456,128]{1,0:T(8,128)S(1)} %collective-permute-done.g_1, f32[456,128]{1,0:T(8,128)S(1)} %collective-permute-done.1.g_2, f32[152,128]{1,0:T(8,128)S(1)} %collective-permute-done.2.h_1, f32[152,128]{1,0:T(8,128)S(1)} %collective-permute-done.3.h_2, f32[304,128]{1,0:T(8,128)S(1)} %collective-permute-done.4.g_1.a_1, ...), custom_call_target="tpu_custom_call" | custom-call | flops 1048576 | bytes 3300000 | tf_op jit(solution)/shard_map/pallas_call | solution.py:226
  (24 shorter events, 0.1 us)
Async XLA Ops:
  0.6 7.9 %copy-start.8 = (f32[4,2048]{1,0:T(4,128)S(1)}, f32[4,2048]{1,0:T(4,128)}, u32[]{:S(2)}) copy-start(f32[4,2048]{1,0:T(4,128)} %weights) | copy-start | bytes 98308
  0.6 7.9 %copy-start.7 = (s32[4,2048]{1,0:T(4,128)S(1)}, s32[4,2048]{1,0:T(4,128)}, u32[]{:S(2)}) copy-start(s32[4,2048]{1,0:T(4,128)} %slots.1) | copy-start | bytes 98308
  3.4 16.2 %collective-permute-start = (f32[456,128]{1,0:T(8,128)}, f32[456,128]{1,0:T(8,128)S(1)}, u32[]{:S(2)}, u32[]{:S(2)}) collective-permute-start(f32[456,128]{1,0:T(8,128)} %get-tuple-element.31), channel_id=1, source_target_pairs={{0,1},{1,0},{2,3},{3,2},{4,5},{5,4},{6,7},{7,6},{8,9},{9,8},{10,11... | collective-permute-start | bytes 700424 | tf_op jit(solution)/shard_map/ppermute | solution.py:507
  3.4 7.3 %copy-start = (f32[150,32,128]{2,1,0:T(8,128)S(1)}, f32[150,32,128]{2,1,0:T(8,128)}, u32[]{:S(2)}) copy-start(f32[150,32,128]{2,1,0:T(8,128)} %state.3) | copy-start | bytes 7372804
  3.4 7.3 %copy-start.1 = (f32[150,32,128]{2,1,0:T(8,128)S(1)}, f32[150,32,128]{2,1,0:T(8,128)}, u32[]{:S(2)}) copy-start(f32[150,32,128]{2,1,0:T(8,128)} %diff.3) | copy-start | bytes 7372804
  3.5 7.3 %copy-start.2 = (s32[75,32,128]{2,1,0:T(8,128)S(1)}, s32[75,32,128]{2,1,0:T(8,128)}, u32[]{:S(2)}) copy-start(s32[75,32,128]{2,1,0:T(8,128)} %mask.3) | copy-start | bytes 3686404
  3.5 16.1 %collective-permute-start.1 = (f32[456,128]{1,0:T(8,128)}, f32[456,128]{1,0:T(8,128)S(1)}, u32[]{:S(2)}, u32[]{:S(2)}) collective-permute-start(f32[456,128]{1,0:T(8,128)} %get-tuple-element.32), channel_id=1, source_target_pairs={{1,2},{2,1},{5,6},{6,5},{9,10},{10,9},{13,14},{14,13},{17,18},{18,... | collective-permute-start | bytes 700424 | tf_op jit(solution)/shard_map/ppermute | solution.py:507
  10.8 12.9 %copy-start.6 = (s32[1,768]{1,0:T(1,128)S(1)}, s32[1,768]{1,0:T(1,128)}, u32[]{:S(2)}) copy-start(s32[1,768]{1,0:T(1,128)} %cells.7) | copy-start | bytes 9220
  19.5 6.6 %copy-start.3 = (f32[640,128]{1,0:T(8,128)S(1)}, f32[640,128]{1,0:T(8,128)}, u32[]{:S(2)}) copy-start(f32[640,128]{1,0:T(8,128)} %get-tuple-element.38.rc) | copy-start | bytes 983044
  19.5 6.6 %copy-start.5 = (f32[640,128]{1,0:T(8,128)S(1)}, f32[640,128]{1,0:T(8,128)}, u32[]{:S(2)}) copy-start(f32[640,128]{1,0:T(8,128)} %get-tuple-element.37.rv) | copy-start | bytes 983044
  19.9 6.2 %collective-permute-start.2 = (f32[152,128]{1,0:T(8,128)S(1)}, f32[152,128]{1,0:T(8,128)S(1)}, u32[]{:S(2)}, u32[]{:S(2)}) collective-permute-start(f32[152,128]{1,0:T(8,128)S(1)} %get-tuple-element.35), channel_id=1, source_target_pairs={{0,4},{4,0},{8,12},{12,8},{16,20},{20,16},{24,28},{28,24},{1,5},{5... | collective-permute-start | bytes 233480 | tf_op jit(solution)/shard_map/ppermute | solution.py:507
  20.0 6.1 %collective-permute-start.3 = (f32[152,128]{1,0:T(8,128)S(1)}, f32[152,128]{1,0:T(8,128)S(1)}, u32[]{:S(2)}, u32[]{:S(2)}) collective-permute-start(f32[152,128]{1,0:T(8,128)S(1)} %get-tuple-element.36), channel_id=1, source_target_pairs={{0,28},{4,8},{8,4},{12,16},{16,12},{20,24},{24,20},{28,0},{1,29},{... | collective-permute-start | bytes 233480 | tf_op jit(solution)/shard_map/ppermute | solution.py:507
  23.7 23.1 %copy-start.4 = (f32[150,2048]{1,0:T(8,128)S(1)}, f32[150,2048]{1,0:T(8,128)}, u32[]{:S(2)}) copy-start(f32[150,2048]{1,0:T(8,128)} %prec.1) | copy-start | bytes 3686404
  71.9 7.8 %collective-permute-start.4 = (f32[304,128]{1,0:T(8,128)S(1)}, f32[304,128]{1,0:T(8,128)S(1)}, u32[]{:S(2)}, u32[]{:S(2)}) collective-permute-start(f32[304,128]{1,0:T(8,128)S(1)} %get-tuple-element.45), channel_id=1, source_target_pairs={{0,1},{1,0},{2,3},{3,2},{4,5},{5,4},{6,7},{7,6},{8,9},{9,8},{10,11... | collective-permute-start | bytes 466952 | tf_op jit(solution)/shard_map/ppermute | solution.py:507
  73.8 8.0 %collective-permute-start.5 = (f32[304,128]{1,0:T(8,128)S(1)}, f32[304,128]{1,0:T(8,128)S(1)}, u32[]{:S(2)}, u32[]{:S(2)}) collective-permute-start(f32[304,128]{1,0:T(8,128)S(1)} %get-tuple-element.46), channel_id=1, source_target_pairs={{1,2},{2,1},{5,6},{6,5},{9,10},{10,9},{13,14},{14,13},{17,18},{18,... | collective-permute-start | bytes 466952 | tf_op jit(solution)/shard_map/ppermute | solution.py:507
  82.2 3.1 %collective-permute-start.6 = (f32[152,128]{1,0:T(8,128)S(1)}, f32[152,128]{1,0:T(8,128)S(1)}, u32[]{:S(2)}, u32[]{:S(2)}) collective-permute-start(f32[152,128]{1,0:T(8,128)S(1)} %get-tuple-element.54), channel_id=1, source_target_pairs={{0,4},{4,0},{8,12},{12,8},{16,20},{20,16},{24,28},{28,24},{1,5},{5... | collective-permute-start | bytes 233480 | tf_op jit(solution)/shard_map/ppermute | solution.py:507
  82.2 5.7 %collective-permute-start.7 = (f32[152,128]{1,0:T(8,128)S(1)}, f32[152,128]{1,0:T(8,128)S(1)}, u32[]{:S(2)}, u32[]{:S(2)}) collective-permute-start(f32[152,128]{1,0:T(8,128)S(1)} %get-tuple-element.55), channel_id=1, source_target_pairs={{0,28},{4,8},{8,4},{12,16},{16,12},{20,24},{24,20},{28,0},{1,29},{... | collective-permute-start | bytes 233480 | tf_op jit(solution)/shard_map/ppermute | solution.py:507

commit v4 on v3

--- a/solution.py
+++ b/solution.py
@@ -32,6 +32,8 @@
 
 
 def tall(x, rows):
+    if x.shape[0] == rows:
+        return x
     return jnp.concatenate([x, jnp.zeros((rows - x.shape[0], x.shape[1]), x.dtype)], axis=0)
 
 
@@ -85,7 +87,7 @@
     return vp + inner * (beside - vp) + south * (roll(vp, -4) - vp) + north * (roll(vp, 4) - vp)
 
 
-def pack_messages(vp, cp, pp, north, south):
+def pack_messages(vp, cp, pp, north=(), south=()):
     lane = lane_of(vp)
     kind = lane & 3
     east = jnp.where(kind == 0, roll(vp, -1), jnp.where(kind == 1, cp, roll(pp, 1)))
@@ -115,28 +117,35 @@
     return out
 
 
-def rim_correction(own, coef, ghosts):
+def pack_correction(vp, pp, cp, gv, gc, gp, more_ghost=0.0, more_whole=0.0):
+    kind, inner, south, north = pack_edges(cp)
+    mid = (kind == 1) | (kind == 2)
+    mg = jnp.where(mid, jnp.minimum(cp, gc), 0.0)
+    f = mg * (gv - vp)
+    qf = inner * f
+    again = mg * (gp - f + more_ghost - (pp + f + more_whole))
+    rp = f - qf + south * (roll(f, -4) - f) + north * (roll(f, 4) - f) + again
+    return jnp.where(mid, rp, jnp.where(kind == 0, roll(qf, -1), roll(qf, 1))), f
+
+
+def rim_correction(own, coef, ghosts, complete=False):
     v0, v31, p0, p31, vp, pp = own
     c0, c1, c30, c31, cp = coef
     (gvn, gcn, gpn), (gvs, gcs, gps), (gv, gc, gp), (kv, kc) = ghosts
     lane = lane_of(v0)
     ends = (lane == 0) | (lane == LANES - 1)
-    kind, inner, south, north = pack_edges(cp)
-    mid = (kind == 1) | (kind == 2)
-    mg = jnp.where(mid, jnp.minimum(cp, gc), 0.0)
-    f = mg * (gv - vp)
     mn, ms = jnp.minimum(c0, gcn), jnp.minimum(c31, gcs)
     fn, fs = mn * (gvn - v0), ms * (gvs - v31)
-    ghost = gp - f + jnp.where(mid, jnp.minimum(gc, kc), 0.0) * (kv - gv)
-    ghost_n = gpn - fn + jnp.where(ends, jnp.minimum(gcn, roll(kc, -2)), 0.0) * (roll(kv, -2) - gvn)
-    ghost_s = gps - fs + jnp.where(ends, jnp.minimum(gcs, roll(kc, 2)), 0.0) * (roll(kv, 2) - gvs)
-    whole = pp + f + jnp.where((lane == 1) | (lane == 2), roll(fn, 2), 0.0)
-    whole = whole + jnp.where((lane == LANES - 3) | (lane == LANES - 2), roll(fs, -2), 0.0)
+    more_ghost = jnp.where(((lane & 3) == 1) | ((lane & 3) == 2), jnp.minimum(gc, kc), 0.0) * (kv - gv)
+    more_whole = jnp.where((lane == 1) | (lane == 2), roll(fn, 2), 0.0)
+    more_whole = more_whole + jnp.where((lane == LANES - 3) | (lane == LANES - 2), roll(fs, -2), 0.0)
+    rp, f = pack_correction(vp, pp, cp, gv, gc, gp, more_ghost, more_whole)
+    ghost_n, ghost_s = gpn - fn, gps - fs
+    if not complete:
+        ghost_n = ghost_n + jnp.where(ends, jnp.minimum(gcn, roll(kc, -2)), 0.0) * (roll(kv, -2) - gvn)
+        ghost_s = ghost_s + jnp.where(ends, jnp.minimum(gcs, roll(kc, 2)), 0.0) * (roll(kv, 2) - gvs)
     whole_n = p0 + fn + jnp.where(ends, roll(f, -2), 0.0)
     whole_s = p31 + fs + jnp.where(ends, roll(f, 2), 0.0)
-    qf = inner * f
-    rp = f - qf + south * (roll(f, -4) - f) + north * (roll(f, 4) - f) + mg * (ghost - whole)
-    rp = jnp.where(mid, rp, jnp.where(kind == 0, roll(qf, -1), roll(qf, 1)))
     rows = []
     for c, d, m, g, w, x in ((c0, c1, mn, ghost_n, whole_n, fn), (c31, c30, ms, ghost_s, whole_s, fs)):
         east, west = row_edges(c)
@@ -177,37 +186,59 @@
     return [(a, lane, 0, LANES - lane), (a + 1, lane - LANES, LANES - lane, CAP)]
 
 
+def merged(old, new, lo, hi):
+    if old is None:
+        return new
+    lane = lane_of(new)
+    return jnp.where((lane >= lo) & (lane < hi), new, old)
+
+
+def by_shift(pairs, a):
+    out = {}
+    for o in pairs:
+        for tile, at, p, q in spans(o):
+            if tile == a:
+                for g in range(GROUPS):
+                    out.setdefault(g - o, []).append((o, g, at + p, CAP * g + p, q - p))
+    return out
+
+
 def pack_payload(columns, out_ref, first, last):
-    lane = lax.broadcasted_iota(jnp.int32, (ROWS, LANES), 1)
     tail = ROWS - 2 * (GROUPS - 1) - 2
-    tiles = []
-    for o in range(first, last):
-        while len(tiles) <= spans(o - first)[-1][0]:
-            x = columns(len(tiles) // 2)
-            rest = [x[ROWS * g + SENT : ROWS * (g + 1)] for g in range(GROUPS - 1)]
-            groups = [x[ROWS * g : ROWS * (g + 1)] for g in range(GROUPS - 1)]
-            groups.append(jnp.concatenate([x[ROWS * (GROUPS - 1) :][:tail], *rest, jnp.zeros((2, x.shape[1]), F32)], axis=0))
-            tiles += [[g[:, :LANES] for g in groups], [g[:, LANES:] for g in groups]]
-        block = jnp.zeros((ROWS, LANES), F32)
-        for a, at, p, q in spans(o - first):
-            for g in range(GROUPS):
-                piece = roll(tiles[a][g], CAP * g - at)
-                block = jnp.where((lane >= CAP * g + p) & (lane < CAP * g + q), piece, block)
-        out_ref[SENT * o : SENT * (o + 1), :] = block[:SENT]
+    pairs = range(last - first)
+    blocks = [None for _ in pairs]
+    for a in range(spans(pairs[-1])[-1][0] + 1):
+        if a % 2 == 0:
+            both = columns(a // 2)
+        x = both[:, LANES * (a % 2) : LANES * (a % 2 + 1)]
+        rest = [x[ROWS * g + SENT : ROWS * (g + 1)] for g in range(GROUPS - 1)]
+        groups = [x[ROWS * g : ROWS * (g + 1)] for g in range(GROUPS - 1)]
+        groups.append(jnp.concatenate([x[ROWS * (GROUPS - 1) :][:tail], *rest, jnp.zeros((2, LANES), F32)], axis=0))
+        for d, moves in by_shift(pairs, a).items():
+            z = None
+            for o, g, src, dst, n in moves:
+                z = merged(z, groups[g], src, src + n)
+            z = roll(z, CAP * d)
+            for o, g, src, dst, n in moves:
+                blocks[o] = merged(blocks[o], z, dst, dst + n)
+        for o in pairs:
+            if spans(o)[-1][0] == a:
+                at = SENT * (first + o)
+                out_ref[at : at + SENT, :] = blocks[o][:SENT]
 
 
 def unpack_payload(in_ref, owners, slots):
-    lane = lax.broadcasted_iota(jnp.int32, (ROWS, LANES), 1)
-    pieces = [[jnp.zeros((ROWS, LANES), F32) for _ in range(slots // LANES)] for _ in range(GROUPS)]
-    for o in range(owners):
-        if o < owners - 1:
-            block = in_ref[SENT * o : SENT * o + ROWS, :]
-        else:
-            block = tall(in_ref[SENT * o :, :], ROWS)
-        for a, at, p, q in spans(o):
-            for g in range(GROUPS):
-                here = (lane >= at + p) & (lane < at + q)
-                pieces[g][a] = jnp.where(here, roll(block, at - CAP * g), pieces[g][a])
+    pairs = range(owners)
+    blocks = [in_ref[SENT * o : SENT * o + ROWS, :] if o < owners - 1 else tall(in_ref[SENT * o :, :], ROWS) for o in pairs]
+    pieces = [[None for _ in range(slots // LANES)] for _ in range(GROUPS)]
+    for a in range(slots // LANES):
+        for d, moves in by_shift(pairs, a).items():
+            z = None
+            for o, g, dst, src, n in moves:
+                z = merged(z, blocks[o], src, src + n)
+            z = roll(z, -CAP * d)
+            for o, g, dst, src, n in moves:
+                pieces[g][a] = merged(pieces[g][a], z, dst, dst + n)
     groups = [jnp.concatenate(x, axis=1) for x in pieces]
     tail = ROWS - 2 * (GROUPS - 1) - 2
     out = []
@@ -304,6 +335,17 @@
     v, i = first
     for k in range(8):
         dst[i + k, v : v + 8, :] = y[k]
+
+
+def outer_columns(ref):
+    total = jnp.zeros((2 * ref.shape[1], LANES), F32)
+    r = lax.broadcasted_iota(jnp.int32, (2 * LANES, LANES), 0)
+    lane = lax.broadcasted_iota(jnp.int32, (2 * LANES, LANES), 1)
+    source = (lane >> 2) * LANES + jnp.where((lane & 3) < 2, LANES - 2 + (lane & 3), (lane & 3) - 2)
+    for i in range(0, ROWS, 2):
+        take = jnp.where(r == source - i * LANES, 1.0, 0.0).astype(BF16)
+        total = total + dot(stacked(jnp.concatenate([ref[i], ref[i + 1]], axis=1)), take)
+    return folded(total)
 
 
 def sweeps_kernel(vals, vp, state, diff, mask, after, field, out, east, west, south, pk, coef, mid):
@@ -325,8 +367,6 @@
             by_grid_row(state[v:end, rows, :], field, (v, i))
             by_grid_row(diff[v:end, rows, :] * m.astype(F32), coef, (v, i))
     lane = lax.broadcasted_iota(jnp.int32, (vp, LANES), 1)
-    pv = jnp.zeros((vp, LANES), F32)
-    pc = jnp.zeros((vp, LANES), F32)
     c = coef[0]
     for i in range(ROWS):
         if i < ROWS - 1:
@@ -337,10 +377,8 @@
         e = jnp.where(lane == LANES - 1, 0.0, jnp.minimum(c, roll(c, -1)))
         east[i] = e
         west[i] = roll(e, 1)
-        here = (lane >> 2) == i
-        pv = jnp.where(here, roll(field[i], 4 * i + 2), pv)
-        pc = jnp.where(here, roll(c, 4 * i + 2), pc)
         c = cn
+    pv, pc = outer_columns(field), outer_columns(coef)
     write_parts(pk, (pv, pc, rim_pack(pv, pc)), vp)
     edges = (east, west, south)
 
@@ -354,16 +392,9 @@
     sweep(mid, edges, split)
 
 
-def lon_kernel(vp, mp, g_1, g_2, coefs, pk, m_1, m_2):
+def lon_kernel(vp, mp, g_1, g_2, pk, m_1, m_2):
     north, south = read_pair("lat", g_1, g_2, mp, vp)
-    if coefs:
-        pv, pc, pp = parts_of(pk, vp)
-        north, south = north[:2], south[:2]
-    else:
-        pv, pp = parts_of(pk, vp)
-        pc = pv
-        north, south = (north[0], north[0]), (south[0], south[0])
-    east, west = pack_messages(pv, pc, pp, north, south)
+    east, west = pack_messages(*parts_of(pk, vp), north[:2], south[:2])
     write_pair("lon", m_1, m_2, (west,), (east,), mp)
 
 
@@ -447,10 +478,45 @@
     inc[...] = x
     rims = folded(dot_nt(x, chosen(cells[...], rim_ids(slots))))
     v0, v1, v30, v31, pv = (rims[:, LANES * k : LANES * (k + 1)] for k in range(5))
-    p0, p31 = rim_rows(v0, v1, v30, v31, *parts_of(rc, vp))
-    write_pair("lat", m_1, m_2, (v0, p0), (v31, p31), mp)
-    write_parts(ra, (v0, v31, p0, p31), vp)
-    write_parts(pa, (pv, rim_pack(pv, pk[vp : 2 * vp, :])), vp)
+    pc = pk[vp : 2 * vp, :]
+    pp = rim_pack(pv, pc)
+    east, west = pack_messages(pv, pc, pp)
+    write_pair("lon", m_1, m_2, (west,), (east,), mp)
+    write_parts(ra, (v0, v31, *rim_rows(v0, v1, v30, v31, *parts_of(rc, vp))), vp)
+    write_parts(pa, (pv, pp), vp)
+
+
+def back_ghosts(vp, mp, lon, lon_back):
+    west, east = read_pair("lon", *lon, mp, vp)
+    _, gc, _ = ghost_pack(west[0], east[0])
+    west, east = read_pair("lon", *lon_back, mp, vp)
+    gv, _, gp = ghost_pack(west[0], east[0])
+    return gv, gc, gp
+
+
+def lat_kernel(vals, vp, mp, h_1, h_2, b_1, b_2, pk, ra, pa, m_1, m_2):
+    ghosts = back_ghosts(vp, mp, (h_1, h_2), (b_1, b_2))
+    pv, pp = parts_of(pa, vp)
+    v0, v31, p0, p31 = parts_of(ra, vp)
+    _, f = pack_correction(pv, pp, pk[vp : 2 * vp, :], *ghosts)
+    lane = lane_of(f)
+    ends = (lane == 0) | (lane == LANES - 1)
+    t = tall(ghosts[0], 2 * LANES).T
+
+    def part(x, k):
+        return tall(jnp.concatenate([x[:vals], t[k : k + 1, :LANES], t[k : k + 1, LANES:]], axis=0), mp)
+
+    north = part(v0, 2), part(p0 + jnp.where(ends, roll(f, -2), 0.0), 1)
+    south = part(v31, LANES - 2), part(p31 + jnp.where(ends, roll(f, 2), 0.0), LANES - 3)
+    write_pair("lat", m_1, m_2, north, south, mp)
+
+
+def lat_corners(vals, vp, north, south):
+    row = lax.broadcasted_iota(jnp.int32, (LANES, 2 * LANES), 0)
+    t = jnp.zeros((LANES, 2 * LANES), F32)
+    for k, x in ((2, north[0]), (1, north[1]), (LANES - 2, south[0]), (LANES - 3, south[1])):
+        t = jnp.where(row == k, jnp.concatenate([x[vals : vals + 1], x[vals + 1 : vals + 2]], axis=1), t)
+    return t.T[:vp]
 
 
 def adjoint_kernel(vp, inc, cells, east, west, south, out, adj):
@@ -468,28 +534,42 @@
     sweep(adj, (east, west, south), keep)
 
 
-def second_kernel(mid, east, west, south, field, out):
+def second_kernel(vals, vp, mp, mid, east, west, south, field, h_1, h_2, b_1, b_2, pk, pa, out, part, buf, sems):
+    pv, pp = parts_of(pa, vp)
+    fix, _ = pack_correction(pv, pp, pk[vp : 2 * vp, :], *back_ghosts(vp, mp, (h_1, h_2), (b_1, b_2)))
+    lane = lane_of(fix)
+    outer = (lane < 2) | (lane >= LANES - 2)
+    copies = []
+
     def add(i, y):
-        out[i] = y + field[i]
+        x = y + field[i]
+        if i in ENDS:
+            part[ENDS.index(i)] = x
+            return
+        buf[i] = x + jnp.where(outer, roll(fix, -(4 * i + 2)), 0.0)
+        copies.append(pltpu.make_async_copy(buf.at[i, pl.ds(0, vals)], out.at[:, i], sems.at[i]))
+        copies[-1].start()
 
     sweep(mid, (east, west, south), add)
-
-
-def final_kernel(vals, vp, mp, g_1, g_2, h_1, h_2, a_1, a_2, b_1, b_2, ra, rc, pk, pa, part, out, buf, sems):
-    gn, gs, (_, gc, _), (_, kc) = read_ghosts(vp, mp, (g_1, g_2), (h_1, h_2))
-    an, az, (gv, _, gp), (kv, _) = read_ghosts(vp, mp, (a_1, a_2), (b_1, b_2))
-    ghosts = (an[0], gn[1], an[1]), (az[0], gs[1], az[1]), (gv, gc, gp), (kv, kc)
+    for c in copies:
+        c.wait()
+
+
+def final_kernel(vals, vp, mp, most, g_1, g_2, h_1, h_2, a_1, a_2, b_1, b_2, ra, rc, pk, pa, part, out, buf, sems):
+    gn, gs, _, (_, kc) = read_ghosts(vp, mp, (g_1, g_2), (h_1, h_2))
+    an, az = read_pair("lat", a_1, a_2, mp, vp)
+    beside = back_ghosts(vp, mp, (h_1, h_2), (b_1, b_2))
+    ghosts = (an[0], gn[1], an[1]), (az[0], gs[1], az[1]), beside, (lat_corners(vals, vp, an, az), kc)
     v0, v31, p0, p31 = parts_of(ra, vp)
     pv, pp = parts_of(pa, vp)
-    r0, r1, r30, r31, fix = rim_correction((v0, v31, p0, p31, pv, pp), parts_of(rc, vp) + [pk[vp : 2 * vp, :]], ghosts)
-    lane = lax.broadcasted_iota(jnp.int32, (vp, LANES), 1)
+    coef = parts_of(rc, vp) + [pk[vp : 2 * vp, :]]
+    *rows, fix = rim_correction((v0, v31, p0, p31, pv, pp), coef, ghosts, complete=True)
+    lane = lane_of(fix)
     outer = (lane < 2) | (lane >= LANES - 2)
     copies = []
-    for i in range(ROWS):
-        x = part[i] + jnp.where(outer, roll(fix, -(4 * i + 2)), 0.0)
-        row = {0: r0, 1: r1, ROWS - 2: r30, ROWS - 1: r31}.get(i)
-        buf[i] = x if row is None else x + row
-        copies.append(pltpu.make_async_copy(buf.at[i, pl.ds(0, vals)], out.at[:, i], sems.at[i]))
+    for k, i in enumerate(ENDS):
+        buf[k] = part[k] + rows[k] + jnp.where(outer, roll(fix, -(4 * i + 2)), 0.0)
+        copies.append(pltpu.make_async_copy(buf.at[k, pl.ds(0, vals)], out.at[:, i], sems.at[k]))
         copies[-1].start()
     for c in copies:
         c.wait()
@@ -521,7 +601,7 @@
 def on_device(state, diffusivity, sea_mask, send_cols, obs_slots, obs_weights, obs_precision):
     vals, taps, obs = state.shape[0], obs_slots.shape[0], obs_slots.shape[1]
     owners = send_cols.shape[1] // CAP
-    vp, mp = up(vals, ROWS), up(vals, 8)
+    vp, mp = up(vals, ROWS), up(vals + 2, 8)
     slots = owners * CAP
     cell_count = ROWS * LANES
     cells = send_cols
@@ -563,7 +643,7 @@
         us=8,
     )
     lon_out = call(
-        lambda g_1, g_2, *refs: lon_kernel(vp, mp, g_1, g_2, True, *refs),
+        functools.partial(lon_kernel, vp, mp),
         [lines(1, mp)] * 2, *lat_in, pk,
         vmem=8,
     )
@@ -593,13 +673,13 @@
         vmem=20 + matrix,
     )
     incoming = across(payload)
-    *lat_out, inc, ra, pa = call(
+    *lon_out, inc, ra, pa = call(
         functools.partial(back_kernel, owners, vp, mp),
-        [lines(2, mp)] * 2 + [((2 * vp, slots), BF16), lines(4, vp), lines(2, vp)],
+        [lines(1, mp)] * 2 + [((2 * vp, slots), BF16), lines(4, vp), lines(2, vp)],
         incoming, cells, rc, pk,
         vmem=24,
     )
-    lat_back = exchange("lat", *lat_out)
+    lon_back = exchange("lon", *lon_out)
     (mid,) = call(
         functools.partial(adjoint_kernel, vp),
         [field],
@@ -608,20 +688,30 @@
         vmem=24,
         us=4,
     )
-    lat_back, mid = lax.optimization_barrier((lat_back, mid))
-    lon_out = call(
-        lambda g_1, g_2, *refs: lon_kernel(vp, mp, g_1, g_2, False, *refs),
-        [lines(1, mp)] * 2, *lat_back, pa,
+    lon_back, mid = lax.optimization_barrier((lon_back, mid))
+    lat_out = call(
+        functools.partial(lat_kernel, vals, vp, mp),
+        [lines(2, mp)] * 2, *lon_in, *lon_back, pk, ra, pa,
         vmem=8,
     )
-    lon_back = exchange("lon", *lon_out)
-    (part,) = call(second_kernel, [field], mid, east, west, south, whole, vmem=20, us=2)
+    lat_back = exchange("lat", *lat_out)
+    most, part = call(
+        functools.partial(second_kernel, vals, vp, mp),
+        [(state.shape, F32), ((len(ENDS), vp, LANES), F32)],
+        mid, east, west, south, whole, *lon_in, *lon_back, pk, pa,
+        scratch=[pltpu.VMEM((ROWS, vp, LANES), F32), pltpu.SemaphoreType.DMA((ROWS,))],
+        out_specs=[HBM, VMEM],
+        vmem=20,
+        us=4,
+    )
     (product,) = call(
         functools.partial(final_kernel, vals, vp, mp),
         [(state.shape, F32)],
-        *lat_in, *lon_in, *lat_back, *lon_back, ra, rc, pk, pa, part,
-        scratch=[pltpu.VMEM((ROWS, vp, LANES), F32), pltpu.SemaphoreType.DMA((ROWS,))],
+        most, *lat_in, *lon_in, *lat_back, *lon_back, ra, rc, pk, pa, part,
+        in_specs=[HBM] + [VMEM] * 13,
+        scratch=[pltpu.VMEM((len(ENDS), vp, LANES), F32), pltpu.SemaphoreType.DMA((len(ENDS),))],
         out_specs=[HBM],
+        input_output_aliases={0: 0},
         vmem=16,
     )
     return product, equivalents

time: 91.1 us -> 87.8 us (0.964)
  waiting for transfers between devices: 4.82 us -> 2.97 us
  Pallas kernels: 32.9 us -> 31.4 us
    ppermute x8, waiting for transfers between devices: 4.82 us -> 2.97 us  [swap(): return lax.ppermute(x, axis, pairs)]
    pallas_call x11, Pallas kernels: 30.8 us -> 29.3 us  [call(): pl.pallas_call(kernel, out_shape=[jax.ShapeDtypeStruct(s, d) for s, d in...]
  transfers between devices with their start and end apart: 8 -> 8, of which waited for: 2 -> 2; matrix products, arithmetic and copies ran while one was open for 0% -> 0% of each run, Pallas kernels for 19% -> 21%
where the time goes in v4:
time: 87.8 us; the launch traced here: 87.6 us
  blocking collectives  36.4 us (41%)
  Pallas kernels  31.4 us (36%)
  starting transfers between devices  15.7 us (18%)
  waiting for transfers between devices  2.97 us (3%)
  between operations  1.09 us (1%)
    all_to_all x2, blocking collectives, across(): lax.all_to_all(flat, ('lon', 'lat'), split_axis=0, concat_axis=0, tiled=T...  36.4 us
    pallas_call x11, Pallas kernels, call(): pl.pallas_call(kernel, out_shape=[jax.ShapeDtypeStruct(s, d) for s, d in...  29.3 us
    ppermute x8, starting transfers between devices, swap(): return lax.ppermute(x, axis, pairs)  15.7 us
    ppermute x8, waiting for transfers between devices, swap(): return lax.ppermute(x, axis, pairs)  2.97 us
    pallas_call x1, Pallas kernels, on_device(): pl.pallas_call(weights_kernel, grid=(obs // wide,), out_shape=[jax.ShapeD...  2.15 us
  transfers between devices with their start and end apart: 8, of which 2 were waited for; matrix products, arithmetic and copies ran while one was open for 0% of the time, Pallas kernels for 21%

profile of v4, /device:TPU:2, one launch (start us, length us, event | category | flops | bytes accessed | tf_op | source)
XLA Modules:
  0.0 87.6 jit_solution(17343578304349535047)
XLA Ops:
  0.6 2.7 %shard_map.86 = (f32[456,128]{1,0:T(8,128)}, f32[456,128]{1,0:T(8,128)}, f32[640,128]{1,0:T(8,128)}, f32[640,128]{1,0:T(8,128)}, f32[8,128]{1,0:T(8,128)}) custom-call(f32[150,32,128]{2,1,0:T(8,128)} %state.3, f32[150,32,128]{2,1,0:T(8,128)} %diff.3, s32[75,32,128]{2,1,0:T(8,128)} %mask.3), custom_call_target="tpu_custom_call" | custom-call | flops 1048576 | bytes 3300000 | tf_op jit(solution)/shard_map/pallas_call | solution.py:257
  3.4 0.1 collective-permute-start
  3.5 5.1 %collective-permute-start.1 = (f32[456,128]{1,0:T(8,128)}, f32[456,128]{1,0:T(8,128)S(1)}, u32[]{:S(2)}, u32[]{:S(2)}) collective-permute-start(f32[456,128]{1,0:T(8,128)} %get-tuple-element.34), channel_id=1, source_target_pairs={{1,2},{2,1},{5,6},{6,5},{9,10},{10,9},{13,14},{14,13},{17,18},{18,... | collective-permute-start | bytes 700424 | tf_op jit(solution)/shard_map/ppermute | solution.py:587
  8.6 2.2 %shard_map.87 = (bf16[768,2048]{1,0:T(8,128)(2,1)S(1)}, bf16[768,2048]{1,0:T(8,128)(2,1)S(1)}) custom-call(s32[4,2048]{1,0:T(4,128)S(1)} %copy-done.7, f32[4,2048]{1,0:T(4,128)S(1)} %copy-done.8), custom_call_target="tpu_custom_call" | custom-call | flops 4000000000 | bytes 80000000 | tf_op jit(solution)/shard_map/pallas_call | solution.py:627
  10.8 7.7 %shard_map.88 = (f32[32,160,128]{2,1,0:T(8,128)S(1)}, bf16[320,4096]{1,0:T(8,128)(2,1)S(1)}, f32[32,160,128]{2,1,0:T(8,128)S(1)}, f32[32,160,128]{2,1,0:T(8,128)...) custom-call(f32[150,32,128]{2,1,0:T(8,128)S(1)} %copy-done, f32[150,32,128]{2,1,0:T(8,128)S(1)} %copy-done.1, ...), custom_call_target="tpu_custom_call" | custom-call | flops 1048576 | bytes 26400000 | tf_op jit(solution)/shard_map/pallas_call | solution.py:257
  18.6 0.3 shard_map.89
  18.9 0.1 collective-permute-start.2
  19.0 3.7 %collective-permute-start.3 = (f32[152,128]{1,0:T(8,128)S(1)}, f32[152,128]{1,0:T(8,128)S(1)}, u32[]{:S(2)}, u32[]{:S(2)}) collective-permute-start(f32[152,128]{1,0:T(8,128)S(1)} %get-tuple-element.38), channel_id=1, source_target_pairs={{0,28},{4,8},{8,4},{12,16},{16,12},{20,24},{24,20},{28,0},{1,29},{... | collective-permute-start | bytes 233480 | tf_op jit(solution)/shard_map/ppermute | solution.py:587
  22.7 2.2 %shard_map.90.inner = f32[160,768]{1,0:T(8,128)S(1)} custom-call(bf16[320,4096]{1,0:T(8,128)(2,1)S(1)} %get-tuple-element.41.smooth, s32[1,768]{1,0:T(1,128)S(1)} %copy-done.6), custom_call_target="tpu_custom_call" | custom-call | flops 1048576 | bytes 9900000 | tf_op jit(solution)/shard_map/pallas_call | solution.py:257
  24.9 1.8 %shard_map.91 = f32[960,128]{1,0:T(8,128)S(1)} custom-call(f32[456,128]{1,0:T(8,128)S(1)} %collective-permute-done.g_1, f32[456,128]{1,0:T(8,128)S(1)} %collective-permute-done.1.g_2, f32[152,128]{1,0:T(8,128)S(1)} %collective-permute-done.2.h_1, f32[152,128]{1,0:T(8,128)S(1)} %collective-permute-done.3.h_2, f32[640,128]{1,0:T(8,128)S(1)} %copy-done.5, ...), custom_call_target="tpu_custom_call" | custom-call | flops 1048576 | bytes 3300000 | tf_op jit(solution)/shard_map/pallas_call | solution.py:257
  26.8 18.7 %all_to_all.10 = f32[32,1,3840]{2,1,0:T(1,128)S(1)} all-to-all(f32[32,1,3840]{2,1,0:T(1,128)S(1)} %bitcast.5), channel_id=1, replica_groups=mesh['lon'=8,'lat'=4] {'lon','lat'}, dimensions={0} | all-to-all | bytes 983040 | tf_op jit(solution)/shard_map/all_to_all | solution.py:598
  45.5 5.5 %shard_map.92 = (f32[150,2048]{1,0:T(8,128)}, f32[960,128]{1,0:T(8,128)S(1)}) custom-call(f32[960,128]{1,0:T(8,128)S(1)} %bitcast.6, bf16[768,2048]{1,0:T(8,128)(2,1)S(1)} %get-tuple-element.44.after.w_hi, bf16[768,2048]{1,0:T(8,128)(2,1)S(1)} %get-tuple-element.45.w_lo, f32[150,2048]{1,0:T(8,128)S(1)} %copy-done.4), custom_call_target="tpu_custom_call" | custom-call | flops 1048576 | bytes 3300000 | tf_op jit(solution)/shard_map/pallas_call | solution.py:257
  51.0 17.7 %all_to_all.11 = f32[32,1,3840]{2,1,0:T(1,128)S(1)} all-to-all(f32[32,1,3840]{2,1,0:T(1,128)S(1)} %bitcast.7), channel_id=1, replica_groups=mesh['lon'=8,'lat'=4] {'lon','lat'}, dimensions={0} | all-to-all | bytes 983040 | tf_op jit(solution)/shard_map/all_to_all | solution.py:598
  68.7 1.0 %shard_map.93 = (f32[152,128]{1,0:T(8,128)S(1)}, f32[152,128]{1,0:T(8,128)S(1)}, bf16[320,768]{1,0:T(8,128)(2,1)S(1)}, f32[640,128]{1,0:T(8,128)S(1)}, f32[320,128]{1,0:T(8,128)S(1)}) custom-call(f32[960,128]{1,0:T(8,128)S(1)} %bitcast.4, s32[1,768]{1,0:T(1,128)S(1)} %copy-done.6, f32[640,128]{1,0:T(8,128)S(1)} %copy-done.3, f32[480,128]{1,0:T(8,128)S(1)} %get-tuple-element.36.pk), custom_call_target="tpu_custom_call" | custom-call | flops 1048576 | bytes 3300000 | tf_op jit(solution)/shard_map/pallas_call | solution.py:257
  69.7 0.1 collective-permute-start.4
  69.8 1.6 %collective-permute-start.5 = (f32[152,128]{1,0:T(8,128)S(1)}, f32[152,128]{1,0:T(8,128)S(1)}, u32[]{:S(2)}, u32[]{:S(2)}) collective-permute-start(f32[152,128]{1,0:T(8,128)S(1)} %get-tuple-element.48), channel_id=1, source_target_pairs={{0,28},{4,8},{8,4},{12,16},{16,12},{20,24},{24,20},{28,0},{1,29},{... | collective-permute-start | bytes 233480 | tf_op jit(solution)/shard_map/ppermute | solution.py:587
  71.3 2.7 %shard_map.94.mid = f32[32,160,128]{2,1,0:T(8,128)S(1)} custom-call(bf16[320,768]{1,0:T(8,128)(2,1)S(1)} %get-tuple-element.49.inc, s32[1,768]{1,0:T(1,128)S(1)} %copy-done.6, f32[32,160,128]{2,1,0:T(8,128)S(1)} %get-tuple-element.50.east, f32[32,160,128]{2,1,0:T(8,128)S(1)} %get-tuple-element.51.west, f32[32,160,128]{2,1,0:T(8,128)S(1)} %get-tuple-element.52.south), custom_call_target="tpu_custom_call" | custom-call | flops 1048576 | bytes 13200000 | tf_op jit(solution)/shard_map/pallas_call | solution.py:257
  74.0 1.5 %collective-permute-done.5.b_2 = f32[152,128]{1,0:T(8,128)S(1)} collective-permute-done((f32[152,128]{1,0:T(8,128)S(1)}, f32[152,128]{1,0:T(8,128)S(1)}, u32[]{:S(2)}, u32[]{:S(2)}) %collective-permute-start.5) | collective-permute-done | bytes 77856 | tf_op jit(solution)/shard_map/ppermute | solution.py:587
  75.5 0.3 shard_map.96
  75.8 1.9 %collective-permute-start.6 = (f32[304,128]{1,0:T(8,128)S(1)}, f32[304,128]{1,0:T(8,128)S(1)}, u32[]{:S(2)}, u32[]{:S(2)}) collective-permute-start(f32[304,128]{1,0:T(8,128)S(1)} %get-tuple-element.60), channel_id=1, source_target_pairs={{0,1},{1,0},{2,3},{3,2},{4,5},{5,4},{6,7},{7,6},{8,9},{9,8},{10,11... | collective-permute-start | bytes 466952 | tf_op jit(solution)/shard_map/ppermute | solution.py:587
  77.7 3.2 %collective-permute-start.7 = (f32[304,128]{1,0:T(8,128)S(1)}, f32[304,128]{1,0:T(8,128)S(1)}, u32[]{:S(2)}, u32[]{:S(2)}) collective-permute-start(f32[304,128]{1,0:T(8,128)S(1)} %get-tuple-element.61), channel_id=1, source_target_pairs={{1,2},{2,1},{5,6},{6,5},{9,10},{10,9},{13,14},{14,13},{17,18},{18,... | collective-permute-start | bytes 466952 | tf_op jit(solution)/shard_map/ppermute | solution.py:587
  80.9 3.3 %shard_map.95 = (f32[150,32,128]{2,1,0:T(8,128)}, f32[4,160,128]{2,1,0:T(8,128)S(1)}) custom-call(f32[32,160,128]{2,1,0:T(8,128)S(1)} %shard_map.94.mid, f32[32,160,128]{2,1,0:T(8,128)S(1)} %get-tuple-element.50.east, f32[32,160,128]{2,1,0:T(8,128)S(1)} %get-tuple-element.51.west, f32[32,160,128]{2,1,0:T(8,128)S(1)} %get-tuple-element.52.south, ...), custom_call_target="tpu_custom_call" | custom-call | flops 1048576 | bytes 13200000 | tf_op jit(solution)/shard_map/pallas_call | solution.py:257
  84.2 1.5 %collective-permute-done.7.a_2 = f32[304,128]{1,0:T(8,128)S(1)} collective-permute-done((f32[304,128]{1,0:T(8,128)S(1)}, f32[304,128]{1,0:T(8,128)S(1)}, u32[]{:S(2)}, u32[]{:S(2)}) %collective-permute-start.7) | collective-permute-done | bytes 155680 | tf_op jit(solution)/shard_map/ppermute | solution.py:587
  85.7 1.7 %shard_map.97 = f32[150,32,128]{2,1,0:T(8,128)} custom-call(f32[150,32,128]{2,1,0:T(8,128)} %get-tuple-element.58.most, f32[456,128]{1,0:T(8,128)S(1)} %collective-permute-done.g_1, f32[456,128]{1,0:T(8,128)S(1)} %collective-permute-done.1.g_2, f32[152,128]{1,0:T(8,128)S(1)} %collective-permute-done.2.h_1, ...), custom_call_target="tpu_custom_call", output_to_operand_aliasing={{}: (0, {})} | custom-call | flops 1048576 | bytes 3300000 | tf_op jit(solution)/shard_map/pallas_call | solution.py:257
  (24 shorter events, 0.1 us)
Async XLA Ops:
  0.6 7.9 %copy-start.8 = (f32[4,2048]{1,0:T(4,128)S(1)}, f32[4,2048]{1,0:T(4,128)}, u32[]{:S(2)}) copy-start(f32[4,2048]{1,0:T(4,128)} %weights) | copy-start | bytes 98308
  0.6 7.9 %copy-start.7 = (s32[4,2048]{1,0:T(4,128)S(1)}, s32[4,2048]{1,0:T(4,128)}, u32[]{:S(2)}) copy-start(s32[4,2048]{1,0:T(4,128)} %slots.1) | copy-start | bytes 98308
  3.4 15.2 %collective-permute-start = (f32[456,128]{1,0:T(8,128)}, f32[456,128]{1,0:T(8,128)S(1)}, u32[]{:S(2)}, u32[]{:S(2)}) collective-permute-start(f32[456,128]{1,0:T(8,128)} %get-tuple-element.33), channel_id=1, source_target_pairs={{0,1},{1,0},{2,3},{3,2},{4,5},{5,4},{6,7},{7,6},{8,9},{9,8},{10,11... | collective-permute-start | bytes 700424 | tf_op jit(solution)/shard_map/ppermute | solution.py:587
  3.4 7.3 %copy-start = (f32[150,32,128]{2,1,0:T(8,128)S(1)}, f32[150,32,128]{2,1,0:T(8,128)}, u32[]{:S(2)}) copy-start(f32[150,32,128]{2,1,0:T(8,128)} %state.3) | copy-start | bytes 7372804
  3.4 7.3 %copy-start.1 = (f32[150,32,128]{2,1,0:T(8,128)S(1)}, f32[150,32,128]{2,1,0:T(8,128)}, u32[]{:S(2)}) copy-start(f32[150,32,128]{2,1,0:T(8,128)} %diff.3) | copy-start | bytes 7372804
  3.5 7.3 %copy-start.2 = (s32[75,32,128]{2,1,0:T(8,128)S(1)}, s32[75,32,128]{2,1,0:T(8,128)}, u32[]{:S(2)}) copy-start(s32[75,32,128]{2,1,0:T(8,128)} %mask.3) | copy-start | bytes 3686404
  3.5 15.1 %collective-permute-start.1 = (f32[456,128]{1,0:T(8,128)}, f32[456,128]{1,0:T(8,128)S(1)}, u32[]{:S(2)}, u32[]{:S(2)}) collective-permute-start(f32[456,128]{1,0:T(8,128)} %get-tuple-element.34), channel_id=1, source_target_pairs={{1,2},{2,1},{5,6},{6,5},{9,10},{10,9},{13,14},{14,13},{17,18},{18,... | collective-permute-start | bytes 700424 | tf_op jit(solution)/shard_map/ppermute | solution.py:587
  10.8 11.9 %copy-start.6 = (s32[1,768]{1,0:T(1,128)S(1)}, s32[1,768]{1,0:T(1,128)}, u32[]{:S(2)}) copy-start(s32[1,768]{1,0:T(1,128)} %cells.7) | copy-start | bytes 9220
  18.5 6.4 %copy-start.3 = (f32[640,128]{1,0:T(8,128)S(1)}, f32[640,128]{1,0:T(8,128)}, u32[]{:S(2)}) copy-start(f32[640,128]{1,0:T(8,128)} %get-tuple-element.40.rc) | copy-start | bytes 983044
  18.6 6.4 %copy-start.5 = (f32[640,128]{1,0:T(8,128)S(1)}, f32[640,128]{1,0:T(8,128)}, u32[]{:S(2)}) copy-start(f32[640,128]{1,0:T(8,128)} %get-tuple-element.39.rv) | copy-start | bytes 983044
  18.9 6.0 %collective-permute-start.2 = (f32[152,128]{1,0:T(8,128)S(1)}, f32[152,128]{1,0:T(8,128)S(1)}, u32[]{:S(2)}, u32[]{:S(2)}) collective-permute-start(f32[152,128]{1,0:T(8,128)S(1)} %get-tuple-element.37), channel_id=1, source_target_pairs={{0,4},{4,0},{8,12},{12,8},{16,20},{20,16},{24,28},{28,24},{1,5},{5... | collective-permute-start | bytes 233480 | tf_op jit(solution)/shard_map/ppermute | solution.py:587
  19.0 5.9 %collective-permute-start.3 = (f32[152,128]{1,0:T(8,128)S(1)}, f32[152,128]{1,0:T(8,128)S(1)}, u32[]{:S(2)}, u32[]{:S(2)}) collective-permute-start(f32[152,128]{1,0:T(8,128)S(1)} %get-tuple-element.38), channel_id=1, source_target_pairs={{0,28},{4,8},{8,4},{12,16},{16,12},{20,24},{24,20},{28,0},{1,29},{... | collective-permute-start | bytes 233480 | tf_op jit(solution)/shard_map/ppermute | solution.py:587
  22.7 22.8 %copy-start.4 = (f32[150,2048]{1,0:T(8,128)S(1)}, f32[150,2048]{1,0:T(8,128)}, u32[]{:S(2)}) copy-start(f32[150,2048]{1,0:T(8,128)} %prec.1) | copy-start | bytes 3686404
  69.7 4.3 %collective-permute-start.4 = (f32[152,128]{1,0:T(8,128)S(1)}, f32[152,128]{1,0:T(8,128)S(1)}, u32[]{:S(2)}, u32[]{:S(2)}) collective-permute-start(f32[152,128]{1,0:T(8,128)S(1)} %get-tuple-element.47), channel_id=1, source_target_pairs={{0,4},{4,0},{8,12},{12,8},{16,20},{20,16},{24,28},{28,24},{1,5},{5... | collective-permute-start | bytes 233480 | tf_op jit(solution)/shard_map/ppermute | solution.py:587
  69.8 5.7 %collective-permute-start.5 = (f32[152,128]{1,0:T(8,128)S(1)}, f32[152,128]{1,0:T(8,128)S(1)}, u32[]{:S(2)}, u32[]{:S(2)}) collective-permute-start(f32[152,128]{1,0:T(8,128)S(1)} %get-tuple-element.48), channel_id=1, source_target_pairs={{0,28},{4,8},{8,4},{12,16},{16,12},{20,24},{24,20},{28,0},{1,29},{... | collective-permute-start | bytes 233480 | tf_op jit(solution)/shard_map/ppermute | solution.py:587
  75.8 8.4 %collective-permute-start.6 = (f32[304,128]{1,0:T(8,128)S(1)}, f32[304,128]{1,0:T(8,128)S(1)}, u32[]{:S(2)}, u32[]{:S(2)}) collective-permute-start(f32[304,128]{1,0:T(8,128)S(1)} %get-tuple-element.60), channel_id=1, source_target_pairs={{0,1},{1,0},{2,3},{3,2},{4,5},{5,4},{6,7},{7,6},{8,9},{9,8},{10,11... | collective-permute-start | bytes 466952 | tf_op jit(solution)/shard_map/ppermute | solution.py:587
  77.7 8.0 %collective-permute-start.7 = (f32[304,128]{1,0:T(8,128)S(1)}, f32[304,128]{1,0:T(8,128)S(1)}, u32[]{:S(2)}, u32[]{:S(2)}) collective-permute-start(f32[304,128]{1,0:T(8,128)S(1)} %get-tuple-element.61), channel_id=1, source_target_pairs={{1,2},{2,1},{5,6},{6,5},{9,10},{10,9},{13,14},{14,13},{17,18},{18,... | collective-permute-start | bytes 466952 | tf_op jit(solution)/shard_map/ppermute | solution.py:587

commit v5 on v4

--- a/solution.py
+++ b/solution.py
@@ -295,32 +295,42 @@
     return before, after
 
 
-def start_loads(vals, state, diff, mask, sv, sd, sm, sems, rows):
-    half = vals // 2
-    copies = []
-    for k, i in enumerate(rows):
-        for src, dst in (
-            (state, sv.at[k, pl.ds(0, vals)]),
-            (diff, sd.at[k, pl.ds(0, vals)]),
-            (mask, sm.at[k, pl.ds(0, half)]),
-            (mask, sm.at[k, pl.ds(half, half)]),
-        ):
-            copies.append(pltpu.make_async_copy(src.at[:, i], dst, sems.at[len(copies)]))
-            copies[-1].start()
-    for ref in (sv, sd, sm):
-        ref[:, vals:, :] = jnp.zeros((ref.shape[0], ref.shape[1] - vals, LANES), ref.dtype)
-    return copies
-
-
 ENDS = (0, 1, ROWS - 2, ROWS - 1)
+
+
+def mask_of(mask, vals, v, rows):
+    half, end = vals // 2, min(v + 8, vals)
+    if end <= half:
+        return mask[v:end, rows, :]
+    if v >= half:
+        return mask[v - half : end - half, rows, :]
+    return jnp.concatenate([mask[v:half, rows, :], mask[: end - half, rows, :]], axis=0)
+
+
+def eight(x):
+    n = x.shape[0]
+    return x if n == 8 else jnp.concatenate([x, jnp.zeros((8 - n, *x.shape[1:]), x.dtype)], axis=0)
 
 
 def rows_kernel(vals, vp, mp, state, diff, mask, m_1, m_2, rv, rc, done, sv, sd, sm, sems):
     done[...] = jnp.zeros(done.shape, F32)
-    for c in start_loads(vals, state, diff, mask, sv, sd, sm, sems, ENDS):
+    copies = []
+    for src, dst, n in ((state, sv, vals), (diff, sd, vals), (mask, sm, vals // 2)):
+        for k, i in enumerate((0, ROWS - 2)):
+            at = dst.at[pl.ds(0, n), pl.ds(2 * k, 2)]
+            copies.append(pltpu.make_async_copy(src.at[:, pl.ds(i, 2)], at, sems.at[len(copies)]))
+            copies[-1].start()
+    for c in copies:
         c.wait()
-    v0, v1, v30, v31 = (sv[k] for k in range(4))
-    c0, c1, c30, c31 = (sd[k] * sm[k].astype(F32) for k in range(4))
+    v_tiles, c_tiles = [], []
+    for v in range(0, vals, 8):
+        end = min(v + 8, vals)
+        c = sd[v:end] * mask_of(sm, vals, v, slice(0, 8)).astype(F32)
+        for tiles, x in ((v_tiles, sv[v:end]), (c_tiles, c)):
+            y = jnp.swapaxes(eight(x), 0, 1)
+            tiles.append([y[k] for k in range(4)])
+    v0, v1, v30, v31 = (tall(jnp.concatenate([t[k] for t in v_tiles], axis=0), vp) for k in range(4))
+    c0, c1, c30, c31 = (tall(jnp.concatenate([t[k] for t in c_tiles], axis=0), vp) for k in range(4))
     p0, p31 = rim_rows(v0, v1, v30, v31, c0, c1, c30, c31)
     write_pair("lat", m_1, m_2, (v0, c0, p0), (v31, c31, p31), mp)
     write_parts(rv, (v0, v31, p0, p31), vp)
@@ -328,10 +338,7 @@
 
 
 def by_grid_row(x, dst, first):
-    n = x.shape[0]
-    if n < 8:
-        x = jnp.concatenate([x, jnp.zeros((8 - n, *x.shape[1:]), x.dtype)], axis=0)
-    y = jnp.swapaxes(x, 0, 1)
+    y = jnp.swapaxes(eight(x), 0, 1)
     v, i = first
     for k in range(8):
         dst[i + k, v : v + 8, :] = y[k]
@@ -358,12 +365,7 @@
         end = min(v + 8, vals)
         for i in range(0, ROWS, 8):
             rows = slice(i, i + 8)
-            if end <= half:
-                m = mask[v:end, rows, :]
-            elif v >= half:
-                m = mask[v - half : end - half, rows, :]
-            else:
-                m = jnp.concatenate([mask[v:half, rows, :], mask[: end - half, rows, :]], axis=0)
+            m = mask_of(mask, vals, v, rows)
             by_grid_row(state[v:end, rows, :], field, (v, i))
             by_grid_row(diff[v:end, rows, :] * m.astype(F32), coef, (v, i))
     lane = lax.broadcasted_iota(jnp.int32, (vp, LANES), 1)
@@ -375,20 +377,23 @@
         else:
             south[i] = jnp.zeros_like(c)
         e = jnp.where(lane == LANES - 1, 0.0, jnp.minimum(c, roll(c, -1)))
-        east[i] = e
-        west[i] = roll(e, 1)
+        w = roll(e, 1)
+        east[i], west[i] = e, w
+        x = field[i]
+        y = x + e * (roll(x, -1) - x) + w * (roll(x, 1) - x)
+        if i < ROWS - 1:
+            y = y + south[i] * (field[i + 1] - x)
+        if i > 0:
+            y = y + south[i - 1] * (field[i - 1] - x)
+        mid[i] = y
         c = cn
     pv, pc = outer_columns(field), outer_columns(coef)
     write_parts(pk, (pv, pc, rim_pack(pv, pc)), vp)
     edges = (east, west, south)
 
-    def keep(i, y):
-        mid[i] = y
-
     def split(i, y):
         out[:, LANES * i : LANES * (i + 1)] = stacked(y)
 
-    sweep(field, edges, keep)
     sweep(mid, edges, split)
 
 
@@ -609,16 +614,13 @@
     lines = lambda n, rows, dtype=F32: ((n * rows, LANES), dtype)
     field = ((ROWS, vp, LANES), F32)
 
-    def loads(n):
-        block = (n, vp, LANES)
-        return [pltpu.VMEM(block, F32), pltpu.VMEM(block, F32), pltpu.VMEM(block, jnp.int32), pltpu.SemaphoreType.DMA((4 * n,))]
-
     *lat_out, rv, rc, done = call(
         functools.partial(rows_kernel, vals, vp, mp),
         [lines(3, mp), lines(3, mp), lines(4, vp), lines(4, vp), lines(1, 8)],
         state, diffusivity, sea_mask,
         in_specs=[HBM] * 3,
-        scratch=loads(len(ENDS)),
+        scratch=[pltpu.VMEM((n, 8, LANES), d) for n, d in ((vp, F32), (vp, F32), (vp // 2, jnp.int32))]
+        + [pltpu.SemaphoreType.DMA((6,))],
         vmem=62,
     )
     lat_in = exchange("lat", *lat_out)

time: 87.8 us -> 87.4 us (level)
  transfers between devices with their start and end apart: 8 -> 8, of which waited for: 2 -> 2; matrix products, arithmetic and copies ran while one was open for 0% -> 0% of each run, Pallas kernels for 21% -> 20%
where the time goes in v5:
time: 87.4 us; the launch traced here: 87.2 us
  blocking collectives  36.4 us (42%)
  Pallas kernels  31 us (35%)
  starting transfers between devices  15.7 us (18%)
  waiting for transfers between devices  2.97 us (3%)
  between operations  1.09 us (1%)
    all_to_all x2, blocking collectives, across(): lax.all_to_all(flat, ('lon', 'lat'), split_axis=0, concat_axis=0, tiled=T...  36.4 us
    pallas_call x11, Pallas kernels, call(): pl.pallas_call(kernel, out_shape=[jax.ShapeDtypeStruct(s, d) for s, d in...  28.8 us
    ppermute x8, starting transfers between devices, swap(): return lax.ppermute(x, axis, pairs)  15.7 us
    ppermute x8, waiting for transfers between devices, swap(): return lax.ppermute(x, axis, pairs)  2.97 us
    pallas_call x1, Pallas kernels, on_device(): pl.pallas_call(weights_kernel, grid=(obs // wide,), out_shape=[jax.ShapeD...  2.15 us
  transfers between devices with their start and end apart: 8, of which 2 were waited for; matrix products, arithmetic and copies ran while one was open for 0% of the time, Pallas kernels for 20%

profile of v5, /device:TPU:2, one launch (start us, length us, event | category | flops | bytes accessed | tf_op | source)
XLA Modules:
  0.0 87.2 jit_solution(14248644549386322822)
XLA Ops:
  0.6 2.6 %shard_map.86 = (f32[456,128]{1,0:T(8,128)}, f32[456,128]{1,0:T(8,128)}, f32[640,128]{1,0:T(8,128)}, f32[640,128]{1,0:T(8,128)}, f32[8,128]{1,0:T(8,128)}) custom-call(f32[150,32,128]{2,1,0:T(8,128)} %state.3, f32[150,32,128]{2,1,0:T(8,128)} %diff.3, s32[75,32,128]{2,1,0:T(8,128)} %mask.3), custom_call_target="tpu_custom_call" | custom-call | flops 1048576 | bytes 3300000 | tf_op jit(solution)/shard_map/pallas_call | solution.py:257
  3.3 0.1 collective-permute-start
  3.4 5.1 %collective-permute-start.1 = (f32[456,128]{1,0:T(8,128)}, f32[456,128]{1,0:T(8,128)S(1)}, u32[]{:S(2)}, u32[]{:S(2)}) collective-permute-start(f32[456,128]{1,0:T(8,128)} %get-tuple-element.34), channel_id=1, source_target_pairs={{1,2},{2,1},{5,6},{6,5},{9,10},{10,9},{13,14},{14,13},{17,18},{18,... | collective-permute-start | bytes 700424 | tf_op jit(solution)/shard_map/ppermute | solution.py:592
  8.5 2.2 %shard_map.87 = (bf16[768,2048]{1,0:T(8,128)(2,1)S(1)}, bf16[768,2048]{1,0:T(8,128)(2,1)S(1)}) custom-call(s32[4,2048]{1,0:T(4,128)S(1)} %copy-done.7, f32[4,2048]{1,0:T(4,128)S(1)} %copy-done.8), custom_call_target="tpu_custom_call" | custom-call | flops 4000000000 | bytes 80000000 | tf_op jit(solution)/shard_map/pallas_call | solution.py:629
  10.7 7.4 %shard_map.88 = (f32[32,160,128]{2,1,0:T(8,128)S(1)}, bf16[320,4096]{1,0:T(8,128)(2,1)S(1)}, f32[32,160,128]{2,1,0:T(8,128)S(1)}, f32[32,160,128]{2,1,0:T(8,128)...) custom-call(f32[150,32,128]{2,1,0:T(8,128)S(1)} %copy-done, f32[150,32,128]{2,1,0:T(8,128)S(1)} %copy-done.1, ...), custom_call_target="tpu_custom_call" | custom-call | flops 1048576 | bytes 26400000 | tf_op jit(solution)/shard_map/pallas_call | solution.py:257
  18.2 0.3 shard_map.89
  18.5 0.1 collective-permute-start.2
  18.6 3.7 %collective-permute-start.3 = (f32[152,128]{1,0:T(8,128)S(1)}, f32[152,128]{1,0:T(8,128)S(1)}, u32[]{:S(2)}, u32[]{:S(2)}) collective-permute-start(f32[152,128]{1,0:T(8,128)S(1)} %get-tuple-element.38), channel_id=1, source_target_pairs={{0,28},{4,8},{8,4},{12,16},{16,12},{20,24},{24,20},{28,0},{1,29},{... | collective-permute-start | bytes 233480 | tf_op jit(solution)/shard_map/ppermute | solution.py:592
  22.3 2.2 %shard_map.90.inner = f32[160,768]{1,0:T(8,128)S(1)} custom-call(bf16[320,4096]{1,0:T(8,128)(2,1)S(1)} %get-tuple-element.41.smooth, s32[1,768]{1,0:T(1,128)S(1)} %copy-done.6), custom_call_target="tpu_custom_call" | custom-call | flops 1048576 | bytes 9900000 | tf_op jit(solution)/shard_map/pallas_call | solution.py:257
  24.5 1.8 %shard_map.91 = f32[960,128]{1,0:T(8,128)S(1)} custom-call(f32[456,128]{1,0:T(8,128)S(1)} %collective-permute-done.g_1, f32[456,128]{1,0:T(8,128)S(1)} %collective-permute-done.1.g_2, f32[152,128]{1,0:T(8,128)S(1)} %collective-permute-done.2.h_1, f32[152,128]{1,0:T(8,128)S(1)} %collective-permute-done.3.h_2, f32[640,128]{1,0:T(8,128)S(1)} %copy-done.5, ...), custom_call_target="tpu_custom_call" | custom-call | flops 1048576 | bytes 3300000 | tf_op jit(solution)/shard_map/pallas_call | solution.py:257
  26.3 18.7 %all_to_all.10 = f32[32,1,3840]{2,1,0:T(1,128)S(1)} all-to-all(f32[32,1,3840]{2,1,0:T(1,128)S(1)} %bitcast.5), channel_id=1, replica_groups=mesh['lon'=8,'lat'=4] {'lon','lat'}, dimensions={0} | all-to-all | bytes 983040 | tf_op jit(solution)/shard_map/all_to_all | solution.py:603
  45.1 5.5 %shard_map.92 = (f32[150,2048]{1,0:T(8,128)}, f32[960,128]{1,0:T(8,128)S(1)}) custom-call(f32[960,128]{1,0:T(8,128)S(1)} %bitcast.6, bf16[768,2048]{1,0:T(8,128)(2,1)S(1)} %get-tuple-element.44.after.w_hi, bf16[768,2048]{1,0:T(8,128)(2,1)S(1)} %get-tuple-element.45.w_lo, f32[150,2048]{1,0:T(8,128)S(1)} %copy-done.4), custom_call_target="tpu_custom_call" | custom-call | flops 1048576 | bytes 3300000 | tf_op jit(solution)/shard_map/pallas_call | solution.py:257
  50.6 17.7 %all_to_all.11 = f32[32,1,3840]{2,1,0:T(1,128)S(1)} all-to-all(f32[32,1,3840]{2,1,0:T(1,128)S(1)} %bitcast.7), channel_id=1, replica_groups=mesh['lon'=8,'lat'=4] {'lon','lat'}, dimensions={0} | all-to-all | bytes 983040 | tf_op jit(solution)/shard_map/all_to_all | solution.py:603
  68.3 1.0 %shard_map.93 = (f32[152,128]{1,0:T(8,128)S(1)}, f32[152,128]{1,0:T(8,128)S(1)}, bf16[320,768]{1,0:T(8,128)(2,1)S(1)}, f32[640,128]{1,0:T(8,128)S(1)}, f32[320,128]{1,0:T(8,128)S(1)}) custom-call(f32[960,128]{1,0:T(8,128)S(1)} %bitcast.4, s32[1,768]{1,0:T(1,128)S(1)} %copy-done.6, f32[640,128]{1,0:T(8,128)S(1)} %copy-done.3, f32[480,128]{1,0:T(8,128)S(1)} %get-tuple-element.36.pk), custom_call_target="tpu_custom_call" | custom-call | flops 1048576 | bytes 3300000 | tf_op jit(solution)/shard_map/pallas_call | solution.py:257
  69.3 0.1 collective-permute-start.4
  69.3 1.6 %collective-permute-start.5 = (f32[152,128]{1,0:T(8,128)S(1)}, f32[152,128]{1,0:T(8,128)S(1)}, u32[]{:S(2)}, u32[]{:S(2)}) collective-permute-start(f32[152,128]{1,0:T(8,128)S(1)} %get-tuple-element.48), channel_id=1, source_target_pairs={{0,28},{4,8},{8,4},{12,16},{16,12},{20,24},{24,20},{28,0},{1,29},{... | collective-permute-start | bytes 233480 | tf_op jit(solution)/shard_map/ppermute | solution.py:592
  70.9 2.7 %shard_map.94.mid = f32[32,160,128]{2,1,0:T(8,128)S(1)} custom-call(bf16[320,768]{1,0:T(8,128)(2,1)S(1)} %get-tuple-element.49.inc, s32[1,768]{1,0:T(1,128)S(1)} %copy-done.6, f32[32,160,128]{2,1,0:T(8,128)S(1)} %get-tuple-element.50.east, f32[32,160,128]{2,1,0:T(8,128)S(1)} %get-tuple-element.51.west, f32[32,160,128]{2,1,0:T(8,128)S(1)} %get-tuple-element.52.south), custom_call_target="tpu_custom_call" | custom-call | flops 1048576 | bytes 13200000 | tf_op jit(solution)/shard_map/pallas_call | solution.py:257
  73.6 1.5 %collective-permute-done.5.b_2 = f32[152,128]{1,0:T(8,128)S(1)} collective-permute-done((f32[152,128]{1,0:T(8,128)S(1)}, f32[152,128]{1,0:T(8,128)S(1)}, u32[]{:S(2)}, u32[]{:S(2)}) %collective-permute-start.5) | collective-permute-done | bytes 77856 | tf_op jit(solution)/shard_map/ppermute | solution.py:592
  75.1 0.3 shard_map.96
  75.4 1.9 %collective-permute-start.6 = (f32[304,128]{1,0:T(8,128)S(1)}, f32[304,128]{1,0:T(8,128)S(1)}, u32[]{:S(2)}, u32[]{:S(2)}) collective-permute-start(f32[304,128]{1,0:T(8,128)S(1)} %get-tuple-element.60), channel_id=1, source_target_pairs={{0,1},{1,0},{2,3},{3,2},{4,5},{5,4},{6,7},{7,6},{8,9},{9,8},{10,11... | collective-permute-start | bytes 466952 | tf_op jit(solution)/shard_map/ppermute | solution.py:592
  77.3 3.2 %collective-permute-start.7 = (f32[304,128]{1,0:T(8,128)S(1)}, f32[304,128]{1,0:T(8,128)S(1)}, u32[]{:S(2)}, u32[]{:S(2)}) collective-permute-start(f32[304,128]{1,0:T(8,128)S(1)} %get-tuple-element.61), channel_id=1, source_target_pairs={{1,2},{2,1},{5,6},{6,5},{9,10},{10,9},{13,14},{14,13},{17,18},{18,... | collective-permute-start | bytes 466952 | tf_op jit(solution)/shard_map/ppermute | solution.py:592
  80.5 3.3 %shard_map.95 = (f32[150,32,128]{2,1,0:T(8,128)}, f32[4,160,128]{2,1,0:T(8,128)S(1)}) custom-call(f32[32,160,128]{2,1,0:T(8,128)S(1)} %shard_map.94.mid, f32[32,160,128]{2,1,0:T(8,128)S(1)} %get-tuple-element.50.east, f32[32,160,128]{2,1,0:T(8,128)S(1)} %get-tuple-element.51.west, f32[32,160,128]{2,1,0:T(8,128)S(1)} %get-tuple-element.52.south, ...), custom_call_target="tpu_custom_call" | custom-call | flops 1048576 | bytes 13200000 | tf_op jit(solution)/shard_map/pallas_call | solution.py:257
  83.8 1.5 %collective-permute-done.7.a_2 = f32[304,128]{1,0:T(8,128)S(1)} collective-permute-done((f32[304,128]{1,0:T(8,128)S(1)}, f32[304,128]{1,0:T(8,128)S(1)}, u32[]{:S(2)}, u32[]{:S(2)}) %collective-permute-start.7) | collective-permute-done | bytes 155680 | tf_op jit(solution)/shard_map/ppermute | solution.py:592
  85.3 1.7 %shard_map.97 = f32[150,32,128]{2,1,0:T(8,128)} custom-call(f32[150,32,128]{2,1,0:T(8,128)} %get-tuple-element.58.most, f32[456,128]{1,0:T(8,128)S(1)} %collective-permute-done.g_1, f32[456,128]{1,0:T(8,128)S(1)} %collective-permute-done.1.g_2, f32[152,128]{1,0:T(8,128)S(1)} %collective-permute-done.2.h_1, ...), custom_call_target="tpu_custom_call", output_to_operand_aliasing={{}: (0, {})} | custom-call | flops 1048576 | bytes 3300000 | tf_op jit(solution)/shard_map/pallas_call | solution.py:257
  (24 shorter events, 0.1 us)
Async XLA Ops:
  0.6 7.9 %copy-start.8 = (f32[4,2048]{1,0:T(4,128)S(1)}, f32[4,2048]{1,0:T(4,128)}, u32[]{:S(2)}) copy-start(f32[4,2048]{1,0:T(4,128)} %weights) | copy-start | bytes 98308
  0.6 7.9 %copy-start.7 = (s32[4,2048]{1,0:T(4,128)S(1)}, s32[4,2048]{1,0:T(4,128)}, u32[]{:S(2)}) copy-start(s32[4,2048]{1,0:T(4,128)} %slots.1) | copy-start | bytes 98308
  3.3 14.9 %collective-permute-start = (f32[456,128]{1,0:T(8,128)}, f32[456,128]{1,0:T(8,128)S(1)}, u32[]{:S(2)}, u32[]{:S(2)}) collective-permute-start(f32[456,128]{1,0:T(8,128)} %get-tuple-element.33), channel_id=1, source_target_pairs={{0,1},{1,0},{2,3},{3,2},{4,5},{5,4},{6,7},{7,6},{8,9},{9,8},{10,11... | collective-permute-start | bytes 700424 | tf_op jit(solution)/shard_map/ppermute | solution.py:592
  3.3 7.3 %copy-start = (f32[150,32,128]{2,1,0:T(8,128)S(1)}, f32[150,32,128]{2,1,0:T(8,128)}, u32[]{:S(2)}) copy-start(f32[150,32,128]{2,1,0:T(8,128)} %state.3) | copy-start | bytes 7372804
  3.3 7.3 %copy-start.1 = (f32[150,32,128]{2,1,0:T(8,128)S(1)}, f32[150,32,128]{2,1,0:T(8,128)}, u32[]{:S(2)}) copy-start(f32[150,32,128]{2,1,0:T(8,128)} %diff.3) | copy-start | bytes 7372804
  3.4 7.3 %copy-start.2 = (s32[75,32,128]{2,1,0:T(8,128)S(1)}, s32[75,32,128]{2,1,0:T(8,128)}, u32[]{:S(2)}) copy-start(s32[75,32,128]{2,1,0:T(8,128)} %mask.3) | copy-start | bytes 3686404
  3.4 14.8 %collective-permute-start.1 = (f32[456,128]{1,0:T(8,128)}, f32[456,128]{1,0:T(8,128)S(1)}, u32[]{:S(2)}, u32[]{:S(2)}) collective-permute-start(f32[456,128]{1,0:T(8,128)} %get-tuple-element.34), channel_id=1, source_target_pairs={{1,2},{2,1},{5,6},{6,5},{9,10},{10,9},{13,14},{14,13},{17,18},{18,... | collective-permute-start | bytes 700424 | tf_op jit(solution)/shard_map/ppermute | solution.py:592
  10.7 11.6 %copy-start.6 = (s32[1,768]{1,0:T(1,128)S(1)}, s32[1,768]{1,0:T(1,128)}, u32[]{:S(2)}) copy-start(s32[1,768]{1,0:T(1,128)} %cells.7) | copy-start | bytes 9220
  18.1 6.4 %copy-start.3 = (f32[640,128]{1,0:T(8,128)S(1)}, f32[640,128]{1,0:T(8,128)}, u32[]{:S(2)}) copy-start(f32[640,128]{1,0:T(8,128)} %get-tuple-element.40.rc) | copy-start | bytes 983044
  18.1 6.4 %copy-start.5 = (f32[640,128]{1,0:T(8,128)S(1)}, f32[640,128]{1,0:T(8,128)}, u32[]{:S(2)}) copy-start(f32[640,128]{1,0:T(8,128)} %get-tuple-element.39.rv) | copy-start | bytes 983044
  18.5 6.0 %collective-permute-start.2 = (f32[152,128]{1,0:T(8,128)S(1)}, f32[152,128]{1,0:T(8,128)S(1)}, u32[]{:S(2)}, u32[]{:S(2)}) collective-permute-start(f32[152,128]{1,0:T(8,128)S(1)} %get-tuple-element.37), channel_id=1, source_target_pairs={{0,4},{4,0},{8,12},{12,8},{16,20},{20,16},{24,28},{28,24},{1,5},{5... | collective-permute-start | bytes 233480 | tf_op jit(solution)/shard_map/ppermute | solution.py:592
  18.6 5.9 %collective-permute-start.3 = (f32[152,128]{1,0:T(8,128)S(1)}, f32[152,128]{1,0:T(8,128)S(1)}, u32[]{:S(2)}, u32[]{:S(2)}) collective-permute-start(f32[152,128]{1,0:T(8,128)S(1)} %get-tuple-element.38), channel_id=1, source_target_pairs={{0,28},{4,8},{8,4},{12,16},{16,12},{20,24},{24,20},{28,0},{1,29},{... | collective-permute-start | bytes 233480 | tf_op jit(solution)/shard_map/ppermute | solution.py:592
  22.3 22.8 %copy-start.4 = (f32[150,2048]{1,0:T(8,128)S(1)}, f32[150,2048]{1,0:T(8,128)}, u32[]{:S(2)}) copy-start(f32[150,2048]{1,0:T(8,128)} %prec.1) | copy-start | bytes 3686404
  69.3 4.3 %collective-permute-start.4 = (f32[152,128]{1,0:T(8,128)S(1)}, f32[152,128]{1,0:T(8,128)S(1)}, u32[]{:S(2)}, u32[]{:S(2)}) collective-permute-start(f32[152,128]{1,0:T(8,128)S(1)} %get-tuple-element.47), channel_id=1, source_target_pairs={{0,4},{4,0},{8,12},{12,8},{16,20},{20,16},{24,28},{28,24},{1,5},{5... | collective-permute-start | bytes 233480 | tf_op jit(solution)/shard_map/ppermute | solution.py:592
  69.3 5.7 %collective-permute-start.5 = (f32[152,128]{1,0:T(8,128)S(1)}, f32[152,128]{1,0:T(8,128)S(1)}, u32[]{:S(2)}, u32[]{:S(2)}) collective-permute-start(f32[152,128]{1,0:T(8,128)S(1)} %get-tuple-element.48), channel_id=1, source_target_pairs={{0,28},{4,8},{8,4},{12,16},{16,12},{20,24},{24,20},{28,0},{1,29},{... | collective-permute-start | bytes 233480 | tf_op jit(solution)/shard_map/ppermute | solution.py:592
  75.4 8.4 %collective-permute-start.6 = (f32[304,128]{1,0:T(8,128)S(1)}, f32[304,128]{1,0:T(8,128)S(1)}, u32[]{:S(2)}, u32[]{:S(2)}) collective-permute-start(f32[304,128]{1,0:T(8,128)S(1)} %get-tuple-element.60), channel_id=1, source_target_pairs={{0,1},{1,0},{2,3},{3,2},{4,5},{5,4},{6,7},{7,6},{8,9},{9,8},{10,11... | collective-permute-start | bytes 466952 | tf_op jit(solution)/shard_map/ppermute | solution.py:592
  77.3 8.0 %collective-permute-start.7 = (f32[304,128]{1,0:T(8,128)S(1)}, f32[304,128]{1,0:T(8,128)S(1)}, u32[]{:S(2)}, u32[]{:S(2)}) collective-permute-start(f32[304,128]{1,0:T(8,128)S(1)} %get-tuple-element.61), channel_id=1, source_target_pairs={{1,2},{2,1},{5,6},{6,5},{9,10},{10,9},{13,14},{14,13},{17,18},{18,... | collective-permute-start | bytes 466952 | tf_op jit(solution)/shard_map/ppermute | solution.py:592

commit v6 on v5

--- a/solution.py
+++ b/solution.py
@@ -355,7 +355,7 @@
     return folded(total)
 
 
-def sweeps_kernel(vals, vp, state, diff, mask, after, field, out, east, west, south, pk, coef, mid):
+def sweeps_kernel(vals, vp, state, diff, mask, after, field, mid, east, west, south, pk, coef):
     half = vals // 2
     for v in range(0, vp, 8):
         if v >= vals:
@@ -389,12 +389,6 @@
         c = cn
     pv, pc = outer_columns(field), outer_columns(coef)
     write_parts(pk, (pv, pc, rim_pack(pv, pc)), vp)
-    edges = (east, west, south)
-
-    def split(i, y):
-        out[:, LANES * i : LANES * (i + 1)] = stacked(y)
-
-    sweep(mid, edges, split)
 
 
 def lon_kernel(vp, mp, g_1, g_2, pk, m_1, m_2):
@@ -403,7 +397,11 @@
     write_pair("lon", m_1, m_2, (west,), (east,), mp)
 
 
-def select_kernel(smooth, cells, out, hot):
+def select_kernel(mid, east, west, south, cells, out, smooth, hot):
+    def split(i, y):
+        smooth[:, LANES * i : LANES * (i + 1)] = stacked(y)
+
+    sweep(mid, (east, west, south), split)
     chunk = hot.shape[1]
     wide = 4 * LANES
     for base in range(0, cells.shape[1], chunk):
@@ -635,12 +633,12 @@
         compiler_params=pltpu.CompilerParams(vmem_limit_bytes=20 * MIB),
         cost_estimate=pl.CostEstimate(flops=int(4e9), bytes_accessed=int(80e6), transcendentals=0),
     )(obs_slots, obs_weights)
-    whole, split, east, west, south, pk = call(
+    whole, once, east, west, south, pk = call(
         functools.partial(sweeps_kernel, vals, vp),
-        [field, ((2 * vp, cell_count), BF16), field, field, field, lines(3, vp)],
+        [field, field, field, field, field, lines(3, vp)],
         state, diffusivity, sea_mask, w_hi,
         in_specs=[VMEM] * 3 + [HBM],
-        scratch=[pltpu.VMEM((ROWS, vp, LANES), F32)] * 2,
+        scratch=[pltpu.VMEM((ROWS, vp, LANES), F32)],
         vmem=24,
         us=8,
     )
@@ -653,8 +651,8 @@
     (inner,) = call(
         select_kernel,
         [((vp, slots), F32)],
-        split, cells,
-        scratch=[pltpu.VMEM((cell_count, CHUNK), BF16)],
+        once, east, west, south, cells,
+        scratch=[pltpu.VMEM((2 * vp, cell_count), BF16), pltpu.VMEM((cell_count, CHUNK), BF16)],
         vmem=24,
         us=3,
     )

time: 87.4 us -> 86.2 us (0.986)
  blocking collectives: 36.4 us -> 35.4 us
    all_to_all x2, blocking collectives: 36.4 us -> 35.4 us  [across(): lax.all_to_all(flat, ('lon', 'lat'), split_axis=0, concat_axis=0, tiled=T...]
  transfers between devices with their start and end apart: 8 -> 8, of which waited for: 2 -> 3; matrix products, arithmetic and copies ran while one was open for 0% -> 0% of each run, Pallas kernels for 20% -> 20%
where the time goes in v6:
time: 86.2 us; the launch traced here: 86 us
  blocking collectives  35.4 us (41%)
  Pallas kernels  30.3 us (35%)
  starting transfers between devices  15.4 us (18%)
  waiting for transfers between devices  3.66 us (4%)
  between operations  1.05 us (1%)
    all_to_all x2, blocking collectives, across(): lax.all_to_all(flat, ('lon', 'lat'), split_axis=0, concat_axis=0, tiled=T...  35.4 us
    pallas_call x11, Pallas kernels, call(): pl.pallas_call(kernel, out_shape=[jax.ShapeDtypeStruct(s, d) for s, d in...  28.2 us
    ppermute x8, starting transfers between devices, swap(): return lax.ppermute(x, axis, pairs)  15.4 us
    ppermute x8, waiting for transfers between devices, swap(): return lax.ppermute(x, axis, pairs)  3.66 us
    pallas_call x1, Pallas kernels, on_device(): pl.pallas_call(weights_kernel, grid=(obs // wide,), out_shape=[jax.ShapeD...  2.15 us
  transfers between devices with their start and end apart: 8, of which 3 were waited for; matrix products, arithmetic and copies ran while one was open for 0% of the time, Pallas kernels for 20%

profile of v6, /device:TPU:2, one launch (start us, length us, event | category | flops | bytes accessed | tf_op | source)
XLA Modules:
  0.0 86.0 jit_solution(12840205016542125765)
XLA Ops:
  0.6 2.6 %shard_map.86 = (f32[456,128]{1,0:T(8,128)}, f32[456,128]{1,0:T(8,128)}, f32[640,128]{1,0:T(8,128)}, f32[640,128]{1,0:T(8,128)}, f32[8,128]{1,0:T(8,128)}) custom-call(f32[150,32,128]{2,1,0:T(8,128)} %state.3, f32[150,32,128]{2,1,0:T(8,128)} %diff.3, s32[75,32,128]{2,1,0:T(8,128)} %mask.3), custom_call_target="tpu_custom_call" | custom-call | flops 1048576 | bytes 3300000 | tf_op jit(solution)/shard_map/pallas_call | solution.py:257
  3.4 5.1 %collective-permute-start.1 = (f32[456,128]{1,0:T(8,128)}, f32[456,128]{1,0:T(8,128)S(1)}, u32[]{:S(2)}, u32[]{:S(2)}) collective-permute-start(f32[456,128]{1,0:T(8,128)} %get-tuple-element.34), channel_id=1, source_target_pairs={{1,2},{2,1},{5,6},{6,5},{9,10},{10,9},{13,14},{14,13},{17,18},{18,... | collective-permute-start | bytes 700424 | tf_op jit(solution)/shard_map/ppermute | solution.py:590
  8.5 2.2 %shard_map.87 = (bf16[768,2048]{1,0:T(8,128)(2,1)S(1)}, bf16[768,2048]{1,0:T(8,128)(2,1)S(1)}) custom-call(s32[4,2048]{1,0:T(4,128)S(1)} %copy-done.7, f32[4,2048]{1,0:T(4,128)S(1)} %copy-done.8), custom_call_target="tpu_custom_call" | custom-call | flops 4000000000 | bytes 80000000 | tf_op jit(solution)/shard_map/pallas_call | solution.py:627
  10.7 5.7 %shard_map.88 = (f32[32,160,128]{2,1,0:T(8,128)S(1)}, f32[32,160,128]{2,1,0:T(8,128)S(1)}, f32[32,160,128]{2,1,0:T(8,128)S(1)}, f32[32,160,128]{2,1,0:T(8,128)S(...) custom-call(f32[150,32,128]{2,1,0:T(8,128)S(1)} %copy-done, f32[150,32,128]{2,1,0:T(8,128)S(1)} %copy-done.1, ...), custom_call_target="tpu_custom_call" | custom-call | flops 1048576 | bytes 26400000 | tf_op jit(solution)/shard_map/pallas_call | solution.py:257
  16.5 0.5 collective-permute-done.1.g_2
  16.9 0.3 shard_map.89
  17.2 0.1 collective-permute-start.2
  17.3 3.7 %collective-permute-start.3 = (f32[152,128]{1,0:T(8,128)S(1)}, f32[152,128]{1,0:T(8,128)S(1)}, u32[]{:S(2)}, u32[]{:S(2)}) collective-permute-start(f32[152,128]{1,0:T(8,128)S(1)} %get-tuple-element.38), channel_id=1, source_target_pairs={{0,28},{4,8},{8,4},{12,16},{16,12},{20,24},{24,20},{28,0},{1,29},{... | collective-permute-start | bytes 233480 | tf_op jit(solution)/shard_map/ppermute | solution.py:590
  21.0 3.2 %shard_map.90.inner = f32[160,768]{1,0:T(8,128)S(1)} custom-call(f32[32,160,128]{2,1,0:T(8,128)S(1)} %get-tuple-element.41.mid, f32[32,160,128]{2,1,0:T(8,128)S(1)} %get-tuple-element.42.east, f32[32,160,128]{2,1,0:T(8,128)S(1)} %get-tuple-element.43.west, f32[32,160,128]{2,1,0:T(8,128)S(1)} %get-tuple-element.44.south, s32[1,768]{1,0:T(1,128)S(1)} %copy-done.6), custom_call_target="tpu_custom_call" | custom-call | flops 1048576 | bytes 9900000 | tf_op jit(solution)/shard_map/pallas_call | solution.py:257
  24.3 1.8 %shard_map.91 = f32[960,128]{1,0:T(8,128)S(1)} custom-call(f32[456,128]{1,0:T(8,128)S(1)} %collective-permute-done.g_1, f32[456,128]{1,0:T(8,128)S(1)} %collective-permute-done.1.g_2, f32[152,128]{1,0:T(8,128)S(1)} %collective-permute-done.2.h_1, f32[152,128]{1,0:T(8,128)S(1)} %collective-permute-done.3.h_2, f32[640,128]{1,0:T(8,128)S(1)} %copy-done.5, ...), custom_call_target="tpu_custom_call" | custom-call | flops 1048576 | bytes 3300000 | tf_op jit(solution)/shard_map/pallas_call | solution.py:257
  26.1 17.7 %all_to_all.10 = f32[32,1,3840]{2,1,0:T(1,128)S(1)} all-to-all(f32[32,1,3840]{2,1,0:T(1,128)S(1)} %bitcast.5), channel_id=1, replica_groups=mesh['lon'=8,'lat'=4] {'lon','lat'}, dimensions={0} | all-to-all | bytes 983040 | tf_op jit(solution)/shard_map/all_to_all | solution.py:601
  43.8 5.5 %shard_map.92 = (f32[150,2048]{1,0:T(8,128)}, f32[960,128]{1,0:T(8,128)S(1)}) custom-call(f32[960,128]{1,0:T(8,128)S(1)} %bitcast.6, bf16[768,2048]{1,0:T(8,128)(2,1)S(1)} %get-tuple-element.47.after.w_hi, bf16[768,2048]{1,0:T(8,128)(2,1)S(1)} %get-tuple-element.48.w_lo, f32[150,2048]{1,0:T(8,128)S(1)} %copy-done.4), custom_call_target="tpu_custom_call" | custom-call | flops 1048576 | bytes 3300000 | tf_op jit(solution)/shard_map/pallas_call | solution.py:257
  49.3 17.7 %all_to_all.11 = f32[32,1,3840]{2,1,0:T(1,128)S(1)} all-to-all(f32[32,1,3840]{2,1,0:T(1,128)S(1)} %bitcast.7), channel_id=1, replica_groups=mesh['lon'=8,'lat'=4] {'lon','lat'}, dimensions={0} | all-to-all | bytes 983040 | tf_op jit(solution)/shard_map/all_to_all | solution.py:601
  67.1 1.0 %shard_map.93 = (f32[152,128]{1,0:T(8,128)S(1)}, f32[152,128]{1,0:T(8,128)S(1)}, bf16[320,768]{1,0:T(8,128)(2,1)S(1)}, f32[640,128]{1,0:T(8,128)S(1)}, f32[320,128]{1,0:T(8,128)S(1)}) custom-call(f32[960,128]{1,0:T(8,128)S(1)} %bitcast.4, s32[1,768]{1,0:T(1,128)S(1)} %copy-done.6, f32[640,128]{1,0:T(8,128)S(1)} %copy-done.3, f32[480,128]{1,0:T(8,128)S(1)} %get-tuple-element.36.pk), custom_call_target="tpu_custom_call" | custom-call | flops 1048576 | bytes 3300000 | tf_op jit(solution)/shard_map/pallas_call | solution.py:257
  68.1 0.1 collective-permute-start.4
  68.1 1.6 %collective-permute-start.5 = (f32[152,128]{1,0:T(8,128)S(1)}, f32[152,128]{1,0:T(8,128)S(1)}, u32[]{:S(2)}, u32[]{:S(2)}) collective-permute-start(f32[152,128]{1,0:T(8,128)S(1)} %get-tuple-element.51), channel_id=1, source_target_pairs={{0,28},{4,8},{8,4},{12,16},{16,12},{20,24},{24,20},{28,0},{1,29},{... | collective-permute-start | bytes 233480 | tf_op jit(solution)/shard_map/ppermute | solution.py:590
  69.7 2.7 %shard_map.94.mid = f32[32,160,128]{2,1,0:T(8,128)S(1)} custom-call(bf16[320,768]{1,0:T(8,128)(2,1)S(1)} %get-tuple-element.52.inc, s32[1,768]{1,0:T(1,128)S(1)} %copy-done.6, f32[32,160,128]{2,1,0:T(8,128)S(1)} %get-tuple-element.42.east, f32[32,160,128]{2,1,0:T(8,128)S(1)} %get-tuple-element.43.west, f32[32,160,128]{2,1,0:T(8,128)S(1)} %get-tuple-element.44.south), custom_call_target="tpu_custom_call" | custom-call | flops 1048576 | bytes 13200000 | tf_op jit(solution)/shard_map/pallas_call | solution.py:257
  72.4 1.5 %collective-permute-done.5.b_2 = f32[152,128]{1,0:T(8,128)S(1)} collective-permute-done((f32[152,128]{1,0:T(8,128)S(1)}, f32[152,128]{1,0:T(8,128)S(1)}, u32[]{:S(2)}, u32[]{:S(2)}) %collective-permute-start.5) | collective-permute-done | bytes 77856 | tf_op jit(solution)/shard_map/ppermute | solution.py:590
  73.9 0.3 shard_map.96
  74.2 1.9 %collective-permute-start.6 = (f32[304,128]{1,0:T(8,128)S(1)}, f32[304,128]{1,0:T(8,128)S(1)}, u32[]{:S(2)}, u32[]{:S(2)}) collective-permute-start(f32[304,128]{1,0:T(8,128)S(1)} %get-tuple-element.60), channel_id=1, source_target_pairs={{0,1},{1,0},{2,3},{3,2},{4,5},{5,4},{6,7},{7,6},{8,9},{9,8},{10,11... | collective-permute-start | bytes 466952 | tf_op jit(solution)/shard_map/ppermute | solution.py:590
  76.1 3.0 %collective-permute-start.7 = (f32[304,128]{1,0:T(8,128)S(1)}, f32[304,128]{1,0:T(8,128)S(1)}, u32[]{:S(2)}, u32[]{:S(2)}) collective-permute-start(f32[304,128]{1,0:T(8,128)S(1)} %get-tuple-element.61), channel_id=1, source_target_pairs={{1,2},{2,1},{5,6},{6,5},{9,10},{10,9},{13,14},{14,13},{17,18},{18,... | collective-permute-start | bytes 466952 | tf_op jit(solution)/shard_map/ppermute | solution.py:590
  79.0 3.3 %shard_map.95 = (f32[150,32,128]{2,1,0:T(8,128)}, f32[4,160,128]{2,1,0:T(8,128)S(1)}) custom-call(f32[32,160,128]{2,1,0:T(8,128)S(1)} %shard_map.94.mid, f32[32,160,128]{2,1,0:T(8,128)S(1)} %get-tuple-element.42.east, f32[32,160,128]{2,1,0:T(8,128)S(1)} %get-tuple-element.43.west, f32[32,160,128]{2,1,0:T(8,128)S(1)} %get-tuple-element.44.south, ...), custom_call_target="tpu_custom_call" | custom-call | flops 1048576 | bytes 13200000 | tf_op jit(solution)/shard_map/pallas_call | solution.py:257
  82.3 1.7 %collective-permute-done.7.a_2 = f32[304,128]{1,0:T(8,128)S(1)} collective-permute-done((f32[304,128]{1,0:T(8,128)S(1)}, f32[304,128]{1,0:T(8,128)S(1)}, u32[]{:S(2)}, u32[]{:S(2)}) %collective-permute-start.7) | collective-permute-done | bytes 155680 | tf_op jit(solution)/shard_map/ppermute | solution.py:590
  84.1 1.7 %shard_map.97 = f32[150,32,128]{2,1,0:T(8,128)} custom-call(f32[150,32,128]{2,1,0:T(8,128)} %get-tuple-element.58.most, f32[456,128]{1,0:T(8,128)S(1)} %collective-permute-done.g_1, f32[456,128]{1,0:T(8,128)S(1)} %collective-permute-done.1.g_2, f32[152,128]{1,0:T(8,128)S(1)} %collective-permute-done.2.h_1, ...), custom_call_target="tpu_custom_call", output_to_operand_aliasing={{}: (0, {})} | custom-call | flops 1048576 | bytes 3300000 | tf_op jit(solution)/shard_map/pallas_call | solution.py:257
  (24 shorter events, 0.1 us)
Async XLA Ops:
  0.6 7.9 %copy-start.8 = (f32[4,2048]{1,0:T(4,128)S(1)}, f32[4,2048]{1,0:T(4,128)}, u32[]{:S(2)}) copy-start(f32[4,2048]{1,0:T(4,128)} %weights) | copy-start | bytes 98308
  0.6 7.9 %copy-start.7 = (s32[4,2048]{1,0:T(4,128)S(1)}, s32[4,2048]{1,0:T(4,128)}, u32[]{:S(2)}) copy-start(s32[4,2048]{1,0:T(4,128)} %slots.1) | copy-start | bytes 98308
  3.3 13.2 %collective-permute-start = (f32[456,128]{1,0:T(8,128)}, f32[456,128]{1,0:T(8,128)S(1)}, u32[]{:S(2)}, u32[]{:S(2)}) collective-permute-start(f32[456,128]{1,0:T(8,128)} %get-tuple-element.33), channel_id=1, source_target_pairs={{0,1},{1,0},{2,3},{3,2},{4,5},{5,4},{6,7},{7,6},{8,9},{9,8},{10,11... | collective-permute-start | bytes 700424 | tf_op jit(solution)/shard_map/ppermute | solution.py:590
  3.3 7.3 %copy-start = (f32[150,32,128]{2,1,0:T(8,128)S(1)}, f32[150,32,128]{2,1,0:T(8,128)}, u32[]{:S(2)}) copy-start(f32[150,32,128]{2,1,0:T(8,128)} %state.3) | copy-start | bytes 7372804
  3.3 7.3 %copy-start.1 = (f32[150,32,128]{2,1,0:T(8,128)S(1)}, f32[150,32,128]{2,1,0:T(8,128)}, u32[]{:S(2)}) copy-start(f32[150,32,128]{2,1,0:T(8,128)} %diff.3) | copy-start | bytes 7372804
  3.4 7.3 %copy-start.2 = (s32[75,32,128]{2,1,0:T(8,128)S(1)}, s32[75,32,128]{2,1,0:T(8,128)}, u32[]{:S(2)}) copy-start(s32[75,32,128]{2,1,0:T(8,128)} %mask.3) | copy-start | bytes 3686404
  3.4 13.6 %collective-permute-start.1 = (f32[456,128]{1,0:T(8,128)}, f32[456,128]{1,0:T(8,128)S(1)}, u32[]{:S(2)}, u32[]{:S(2)}) collective-permute-start(f32[456,128]{1,0:T(8,128)} %get-tuple-element.34), channel_id=1, source_target_pairs={{1,2},{2,1},{5,6},{6,5},{9,10},{10,9},{13,14},{14,13},{17,18},{18,... | collective-permute-start | bytes 700424 | tf_op jit(solution)/shard_map/ppermute | solution.py:590
  10.7 10.3 %copy-start.6 = (s32[1,768]{1,0:T(1,128)S(1)}, s32[1,768]{1,0:T(1,128)}, u32[]{:S(2)}) copy-start(s32[1,768]{1,0:T(1,128)} %cells.7) | copy-start | bytes 9220
  17.2 7.0 %collective-permute-start.2 = (f32[152,128]{1,0:T(8,128)S(1)}, f32[152,128]{1,0:T(8,128)S(1)}, u32[]{:S(2)}, u32[]{:S(2)}) collective-permute-start(f32[152,128]{1,0:T(8,128)S(1)} %get-tuple-element.37), channel_id=1, source_target_pairs={{0,4},{4,0},{8,12},{12,8},{16,20},{20,16},{24,28},{28,24},{1,5},{5... | collective-permute-start | bytes 233480 | tf_op jit(solution)/shard_map/ppermute | solution.py:590
  17.3 7.0 %collective-permute-start.3 = (f32[152,128]{1,0:T(8,128)S(1)}, f32[152,128]{1,0:T(8,128)S(1)}, u32[]{:S(2)}, u32[]{:S(2)}) collective-permute-start(f32[152,128]{1,0:T(8,128)S(1)} %get-tuple-element.38), channel_id=1, source_target_pairs={{0,28},{4,8},{8,4},{12,16},{16,12},{20,24},{24,20},{28,0},{1,29},{... | collective-permute-start | bytes 233480 | tf_op jit(solution)/shard_map/ppermute | solution.py:590
  21.0 3.3 %copy-start.3 = (f32[640,128]{1,0:T(8,128)S(1)}, f32[640,128]{1,0:T(8,128)}, u32[]{:S(2)}) copy-start(f32[640,128]{1,0:T(8,128)} %get-tuple-element.40.rc) | copy-start | bytes 983044
  21.0 3.3 %copy-start.5 = (f32[640,128]{1,0:T(8,128)S(1)}, f32[640,128]{1,0:T(8,128)}, u32[]{:S(2)}) copy-start(f32[640,128]{1,0:T(8,128)} %get-tuple-element.39.rv) | copy-start | bytes 983044
  24.2 19.6 %copy-start.4 = (f32[150,2048]{1,0:T(8,128)S(1)}, f32[150,2048]{1,0:T(8,128)}, u32[]{:S(2)}) copy-start(f32[150,2048]{1,0:T(8,128)} %prec.1) | copy-start | bytes 3686404
  68.1 4.3 %collective-permute-start.4 = (f32[152,128]{1,0:T(8,128)S(1)}, f32[152,128]{1,0:T(8,128)S(1)}, u32[]{:S(2)}, u32[]{:S(2)}) collective-permute-start(f32[152,128]{1,0:T(8,128)S(1)} %get-tuple-element.50), channel_id=1, source_target_pairs={{0,4},{4,0},{8,12},{12,8},{16,20},{20,16},{24,28},{28,24},{1,5},{5... | collective-permute-start | bytes 233480 | tf_op jit(solution)/shard_map/ppermute | solution.py:590
  68.1 5.7 %collective-permute-start.5 = (f32[152,128]{1,0:T(8,128)S(1)}, f32[152,128]{1,0:T(8,128)S(1)}, u32[]{:S(2)}, u32[]{:S(2)}) collective-permute-start(f32[152,128]{1,0:T(8,128)S(1)} %get-tuple-element.51), channel_id=1, source_target_pairs={{0,28},{4,8},{8,4},{12,16},{16,12},{20,24},{24,20},{28,0},{1,29},{... | collective-permute-start | bytes 233480 | tf_op jit(solution)/shard_map/ppermute | solution.py:590
  74.2 8.2 %collective-permute-start.6 = (f32[304,128]{1,0:T(8,128)S(1)}, f32[304,128]{1,0:T(8,128)S(1)}, u32[]{:S(2)}, u32[]{:S(2)}) collective-permute-start(f32[304,128]{1,0:T(8,128)S(1)} %get-tuple-element.60), channel_id=1, source_target_pairs={{0,1},{1,0},{2,3},{3,2},{4,5},{5,4},{6,7},{7,6},{8,9},{9,8},{10,11... | collective-permute-start | bytes 466952 | tf_op jit(solution)/shard_map/ppermute | solution.py:590
  76.1 8.0 %collective-permute-start.7 = (f32[304,128]{1,0:T(8,128)S(1)}, f32[304,128]{1,0:T(8,128)S(1)}, u32[]{:S(2)}, u32[]{:S(2)}) collective-permute-start(f32[304,128]{1,0:T(8,128)S(1)} %get-tuple-element.61), channel_id=1, source_target_pairs={{1,2},{2,1},{5,6},{6,5},{9,10},{10,9},{13,14},{14,13},{17,18},{18,... | collective-permute-start | bytes 466952 | tf_op jit(solution)/shard_map/ppermute | solution.py:590
